TPU v7x, 128 devices: a whole 4x4x4 slice. The times are simulated.
128 devices in a mesh: dp: 8 (over z_lo, y), seq: 16 (over z_hi, x, core).
Axes of the slice: x: 4, y: 4, z: 4 (z_hi: 2, z_lo: 2; z = z_hi * 2 + z_lo), core: 2. Of those that a mesh axis runs over, the one named last changes fastest.
Arguments:
- activations: bfloat16 [8, 8192, 16384], P('dp', 'seq'), may hold values from -16 to 16
- query_weight: bfloat16 [16384, 1024], P('dp'), may hold values from -1 to 1
- kv_weight: bfloat16 [16384, 256], P('dp'), may hold values from -1 to 1
- picks: int32 [8, 128, 16], P('dp', 'seq'), may hold values from 0 to 127, as said below
Outputs:
- attended: bfloat16 [8, 8192, 1024], P('dp', 'seq')
Inputs may be any that keep to these rules, and one draw needn't show every extreme that they name: `picks`: entry 0 of row b of a sequence is b; the 16 entries of row b are distinct and none exceeds max(b, 15).
All inputs are finite; a program needn't handle non-finite values.
Results may differ from a plain program's by a relative error of at most 0.0095.
Values may be sent and summed in bfloat16 or wider, within the bound.
No kernel may reach another device: no remote copies, remote signals or barrier semaphores. Data moves between devices by JAX's collectives and lax.ppermute only.
A program may use at most 192 MiB of HBM per device.

v0:
```python
import jax
import jax.numpy as jnp
from jax import lax
from jax.sharding import PartitionSpec as P

QH = 8
HD = 128
BLK = 64
PICKS = 16


def rotate(vals, positions):
    half = vals.shape[-1] // 2
    freq = 500000.0 ** (-(jnp.arange(half).astype(jnp.float32) * 2.0 / vals.shape[-1]))
    angle = positions.astype(jnp.float32)[:, None] * freq[None, :]
    cosine = jnp.cos(angle)[:, None, :]
    sine = jnp.sin(angle)[:, None, :]
    first = vals[..., :half]
    second = vals[..., half:]
    return jnp.concatenate(
        [first * cosine - second * sine, second * cosine + first * sine], axis=-1
    )


def local(activations, query_weight, kv_weight, picks):
    tokens = activations[0]
    tok_rows = tokens.shape[0]
    width = QH * HD
    positions = lax.axis_index("seq") * tok_rows + jnp.arange(tok_rows)

    def add_rows(piece):
        return jnp.dot(tokens, piece, preferred_element_type=jnp.float32)

    query_raw = add_rows(lax.all_gather(query_weight, "dp", axis=0, tiled=True))
    kv_raw = add_rows(lax.all_gather(kv_weight, "dp", axis=0, tiled=True))
    keys = rotate(kv_raw[:, None, :HD], positions)[:, 0].astype(jnp.bfloat16)
    values = kv_raw[:, HD:].astype(jnp.bfloat16)
    all_keys, all_values = (
        lax.all_gather(keys, "seq", axis=0, tiled=True),
        lax.all_gather(values, "seq", axis=0, tiled=True),
    )
    blocks_here = tok_rows // BLK
    query_vectors = (rotate(query_raw.reshape(tok_rows, QH, HD), positions) * HD ** (-0.5)).astype(
        jnp.bfloat16
    )
    query_vectors = query_vectors.reshape(blocks_here, BLK, QH, HD)
    chosen = picks[0]
    blocks_all = all_keys.shape[0] // BLK
    selected_key_rows = all_keys.reshape(blocks_all, BLK, HD)[chosen].reshape(
        blocks_here, PICKS * BLK, HD
    )
    selected_value_rows = all_values.reshape(blocks_all, BLK, HD)[chosen].reshape(
        blocks_here, PICKS * BLK, HD
    )
    logit_scores = jnp.einsum(
        "pilz,psz->plis", query_vectors, selected_key_rows, preferred_element_type=jnp.float32
    )
    key_pos = (chosen[:, :, None] * BLK + jnp.arange(BLK)[None, None, :]).reshape(
        blocks_here, PICKS * BLK
    )
    query_pos = positions.reshape(blocks_here, BLK)
    valid = key_pos[:, None, None, :] <= query_pos[:, None, :, None]
    logit_scores = jnp.where(valid, logit_scores, -1e30)
    top = jnp.max(logit_scores, axis=-1, keepdims=True)
    weights = jnp.exp(logit_scores - top)
    probability_weights = (weights / jnp.sum(weights, axis=-1, keepdims=True)).astype(jnp.bfloat16)
    attended_output = jnp.einsum(
        "nxvm,nmg->nvxg",
        probability_weights,
        selected_value_rows,
        preferred_element_type=jnp.float32,
    )
    return attended_output.astype(jnp.bfloat16).reshape(1, tok_rows, width)


def solution(mesh):
    in_specs = (P("dp", "seq", None), P("dp", None), P("dp", None), P("dp", "seq", None))
    out_specs = P("dp", "seq", None)
    return jax.shard_map(local, mesh=mesh, in_specs=in_specs, out_specs=out_specs, check_vma=False)
```

profile of v0, /device:TPU:1, one launch (start us, length us, event | category | flops | bytes accessed | tf_op | source)
XLA Modules:
  0.0 666.2 jit_solution(8252316388969084596)
XLA Ops:
  6.5 0.0 all-gather.6.cloned.1.call-start
  6.5 0.7 all-gather.6.cloned.1.call-update
  7.3 0.0 all-gather.12.cloned.1.call-start
  7.3 96.9 %all-gather.6.cloned.1.call-done = bf16[16384,256]{1,0:T(8,128)(2,1)} async-done(((bf16[2048,256]{1,0:T(8,128)(2,1)}), bf16[16384,256]{1,0:T(8,128)(2,1)}) %all-gather.6.cloned.1.call-update) | async-done | bytes 8388624 | tf_op jit(solution)/shard_map/all_gather | solution.py:35
  104.2 12.2 %fusion.3 = f32[512,256]{0,1:T(8,128)S(1)} fusion(bf16[16384,256]{1,0:T(8,128)(2,1)} %all-gather.6.cloned.1.call-done, bf16[1,512,16384]{2,1,0:T(8,128)(2,1)} %param.4), kind=kOutput, calls=%fused_computation.6 | convolution fusion | flops 4294967296 | bytes 25690112 | tf_op jit(solution)/shard_map/dot_general | solution.py:32
  116.5 0.6 fusion.20
  117.1 0.7 pad_maximum_fusion
  117.7 0.0 all-gather.12.cloned.1.call-update
  117.8 0.0 all-gather.8.cloned.1.call-start
  117.8 0.7 slice.45
  118.5 0.0 all-gather.8.cloned.1.call-update
  118.5 0.0 copy-start.2
  118.5 0.0 all-gather.10.cloned.1.call-start
  118.6 0.5 all-gather.10.cloned.1.call-update
  119.1 0.1 copy-done.2
  119.2 0.1 reshape.200
  119.3 0.1 add.67
  119.4 0.1 add.64
  119.4 0.1 add.65
  119.6 0.5 multiply_cosine_fusion
  120.1 1.2 broadcast_compare_fusion
  121.3 45.4 %all-gather.12.cloned.1.call-done = bf16[8192,1,128]{0,2,1:T(8,128)(2,1)} async-done(((bf16[512,1,128]{0,2,1:T(8,128)(2,1)}), bf16[8192,1,128]{0,2,1:T(8,128)(2,1)}) %all-gather.12.cloned.1.call-update) | async-done | bytes 2097168 | tf_op jit(solution)/shard_map/all_gather | solution.py:39
  166.7 3.2 copy.11
  169.9 2.2 gather_fusion.1
  172.1 45.1 %all-gather.8.cloned.1.call-done = bf16[8192,128]{0,1:T(8,128)(2,1)} async-done(((bf16[512,128]{0,1:T(8,128)(2,1)}), bf16[8192,128]{0,1:T(8,128)(2,1)}) %all-gather.8.cloned.1.call-update) | async-done | bytes 2097168 | tf_op jit(solution)/shard_map/all_gather | solution.py:40
  217.2 3.2 copy.10
  220.5 2.1 gather_fusion
  222.6 322.2 %all-gather.10.cloned.1.call-done = bf16[16384,1024]{1,0:T(8,128)(2,1)} async-done(((bf16[2048,1024]{1,0:T(8,128)(2,1)}), bf16[16384,1024]{1,0:T(8,128)(2,1)}) %all-gather.10.cloned.1.call-update) | async-done | bytes 33554448 | tf_op jit(solution)/shard_map/all_gather | solution.py:34
  544.8 44.0 %copy.12 = bf16[1024,16384]{1,0:T(8,128)(2,1)} copy(bf16[1024,16384]{0,1:T(8,128)(2,1)} %bitcast.51) | data formatting | bytes 67108864 | tf_op jit(solution)/shard_map/dot_general | solution.py:32
  588.8 24.4 %fusion.1 = f32[512,8,128]{0,2,1:T(8,128)S(1)} fusion(bf16[8,128,16384]{2,1,0:T(8,128)(2,1)} %bitcast.52, bf16[1,512,16384]{2,1,0:T(8,128)(2,1)} %param.4), kind=kOutput, calls=%fused_computation.4 | convolution fusion | flops 17179869184 | bytes 52428800 | tf_op jit(solution)/shard_map/dot_general | solution.py:32
  613.3 1.4 multiply_subtract_fusion
  614.6 1.6 concatenate.13
  616.2 1.9 copy.13
  618.1 0.4 concatenate.14
  618.5 1.9 copy.14
  620.4 0.0 copy-start
  620.4 11.0 %fusion.12 = f32[8,1024,64,8]{1,2,3,0:T(8,128)} fusion(bf16[8,1024,128,1]{2,1,3,0:T(8,128)(2,1)} %bitcast.55, f32[8,64,8,64]{3,1,2,0:T(8,128)} %copy.14, f32[8,64,8,64]{3,1,2,0:T(8,128)} %copy.13), kind=kOutput, calls=%fused_computation.18 | convolution fusion | flops 1075314688 | bytes 20971520 | tf_op jit(solution)/shard_map/pilz,psz->plis/dot_general | solution.py:55
  631.4 0.0 copy-done
  631.4 0.0 copy-start.1
  631.4 19.1 %fusion.26 = (f32[8,8,64]{2,1,0:T(8,128)S(1)}, f32[8,8,64,1024]{3,2,1,0:T(8,128)}) fusion(f32[8,1024,64,8]{1,2,3,0:T(8,128)} %fusion.12, pred[8,64,1024]{2,1,0:T(8,128)(4,1)S(1)} %copy-done), kind=kOutput, calls=%fused_computation.48 | output fusion | flops 16778240 | bytes 34095104 | tf_op jit(solution)/shard_map/sub | solution.py:65
  650.5 0.0 copy-done.1
  650.6 7.1 %fusion.11 = bf16[8,64,8,128]{3,1,2,0:T(8,128)(2,1)S(1)} fusion(bf16[8,1024,128,1]{2,1,3,0:T(8,128)(2,1)S(1)} %bitcast.56, f32[8,8,64,1024]{3,2,1,0:T(8,128)} %get-tuple-element.12, f32[8,8,64]{2,1,0:T(8,128)S(1)} %get-tuple-element.11), kind=kOutput, calls=%fused_computation.17 | convolution fusion | flops 1082654720 | bytes 19939328 | tf_op jit(solution)/shard_map/nxvm,nmg->nvxg/dot_general | solution.py:67
  657.6 0.7 copy.15
  658.3 1.3 reshape.197
  (9 shorter events, 0.1 us)
Async XLA Ops:
  6.5 97.7 %all-gather.6.cloned.1.call-start = ((), (), s32[]{:S(2)}) async-start(), calls=%async_computation | async-start | bytes 9437184 | tf_op jit(solution)/shard_map/all_gather | solution.py:35
  7.3 159.4 %all-gather.12.cloned.1.call-start = ((), (), s32[]{:S(2)}) async-start(), calls=%async_computation.3 | async-start | bytes 2228224 | tf_op jit(solution)/shard_map/all_gather | solution.py:39
  117.8 99.5 %all-gather.8.cloned.1.call-start = ((), (), s32[]{:S(2)}) async-start(), calls=%async_computation.1 | async-start | bytes 2228224 | tf_op jit(solution)/shard_map/all_gather | solution.py:40
  118.5 0.7 copy-start.2
  118.5 426.3 %all-gather.10.cloned.1.call-start = ((), (), s32[]{:S(2)}) async-start(), calls=%async_computation.2 | async-start | bytes 37748736 | tf_op jit(solution)/shard_map/all_gather | solution.py:34
  620.4 11.0 %copy-start = (pred[8,64,1024]{2,1,0:T(8,128)(4,1)S(1)}, pred[8,64,1024]{2,1,0:T(8,128)(4,1)}, u32[]{:S(2)}) copy-start(pred[8,64,1024]{2,1,0:T(8,128)(4,1)} %broadcast_compare_fusion) | copy-start | bytes 1572868
  631.4 19.1 %copy-start.1 = (bf16[128,64,128]{2,1,0:T(8,128)(2,1)S(1)}, bf16[128,64,128]{2,1,0:T(8,128)(2,1)}, u32[]{:S(2)}) copy-start(bf16[128,64,128]{2,1,0:T(8,128)(2,1)} %gather_fusion) | copy-start | bytes 6291460
Sparse Core Ops, SparseCore 0:
  9.0 95.1 all-gather.5
  117.9 48.7 all-gather.11
  169.0 48.2 all-gather.7
  218.7 326.0 all-gather.9
where the time goes:
time: 668 us; the launch traced here: 666 us
  waiting for transfers between devices  511 us (76%)
  local copies, waits for them, and re-layouts  63.5 us (10%)
  matrix products  54.8 us (8%)
  other arithmetic  23.4 us (4%)
  between operations  13.3 us (2%)
    all_gather x1, waiting for transfers between devices, local(): query_raw = add_rows(lax.all_gather(query_weight, 'dp', axis=0, tiled=True))  322 us
    all_gather x1, waiting for transfers between devices, local(): kv_raw = add_rows(lax.all_gather(kv_weight, 'dp', axis=0, tiled=True))  96.9 us
    all_gather x1, waiting for transfers between devices, local(): lax.all_gather(keys, 'seq', axis=0, tiled=True)  45.4 us
    all_gather x1, waiting for transfers between devices, local(): lax.all_gather(values, 'seq', axis=0, tiled=True)  45.1 us
    dot_general x1, local copies, waits for them, and re-layouts, add_rows(): return jnp.dot(tokens, piece, preferred_element_type=jnp.float32)  44 us
    dot_general x2, matrix products, add_rows(): return jnp.dot(tokens, piece, preferred_element_type=jnp.float32)  36.7 us
    sub x1, other arithmetic, local(): weights = jnp.exp(logit_scores - top)  19.1 us
  transfers between devices with their start and end apart: 4, of which 4 were waited for; matrix products, arithmetic and copies ran while one was open for 2% of the time, Pallas kernels for 0%

commit v1 on v0

v1 whole, which is shorter than its diff:
```python
import functools

import jax
import jax.numpy as jnp
from jax import lax
from jax.experimental import pallas as pl
from jax.experimental.pallas import tpu as pltpu
from jax.sharding import PartitionSpec as P

QH = 8
HD = 128
BLK = 64
PICKS = 16
SIDE = 4
AXES = ("dp", "seq")
F32 = jnp.float32
BF16 = jnp.bfloat16


def place(x, y, z, c):
    x, y, z = x % SIDE, y % SIDE, z % SIDE
    return ((z % 2) * SIDE + y) * 16 + (z // 2) * 8 + x * 2 + c


def receive_from(source):
    r = range(SIDE)
    return [
        (place(*source(x, y, z, c)), place(x, y, z, c))
        for x in r for y in r for z in r for c in range(2)
    ]


def sign(c):
    return 1 - 2 * c


FROM_Y = receive_from(lambda x, y, z, c: (x, y + sign(c), z, c))
FROM_Z = receive_from(lambda x, y, z, c: (x, y, z + sign(c), c))
FROM_X = receive_from(lambda x, y, z, c: (x + sign(c), y, z, c))
FROM_Z2 = receive_from(lambda x, y, z, c: (x, y, z + 2, c))
FROM_PAIR = receive_from(lambda x, y, z, c: (x + sign(x % 2) * sign(c), y, z, c))
FROM_CORE = receive_from(lambda x, y, z, c: (x, y, z, 1 - c))


def get(value, perm):
    return lax.ppermute(value, AXES, perm)


def rotated(raw, cosine, sine):
    return raw * cosine + pltpu.roll(raw, HD // 2, 1) * sine


def project_kernel(n, first, last, *refs):
    refs = list(refs)
    refs.pop(0)
    own, sib = refs.pop(0), refs.pop(0)
    pieces = [refs.pop(0) for _ in range(n)]
    g = pl.program_id(0)
    if not first:
        acc_own, acc_sib = refs.pop(0), refs.pop(0)
    if last:
        tables = [refs.pop(0) for _ in range(4)]
        fin_own, fin_sib = refs.pop(0), refs.pop(0)
    out_own, out_sib = refs.pop(0), refs.pop(0)
    for p in range(n):

        @pl.when(g == p)
        def _(p=p):
            for x, out, base in (
                (own, out_own, None if first else acc_own),
                (sib, out_sib, None if first else acc_sib),
            ):
                part = jnp.dot(x[...], pieces[p][...], preferred_element_type=F32)
                if p:
                    out[...] += part
                elif first:
                    out[...] = part
                else:
                    out[...] = base[...] + part

    if last:

        @pl.when(g == n - 1)
        def _():
            fin_own[...] = rotated(out_own[...], tables[0][...], tables[1][...]).astype(BF16)
            fin_sib[...] = rotated(out_sib[...], tables[2][...], tables[3][...]).astype(BF16)


def project(blocks, own, sib, pieces, acc=None, tables=None):
    n = len(pieces)
    rows = own.shape[0]
    depth, width = pieces[0].shape
    first, last = acc is None, tables is not None

    def whole(shape):
        return pl.BlockSpec(shape, lambda g, b: (0,) * len(shape))

    tile = pl.BlockSpec((rows, depth), lambda g, b: (0, b[g]))
    in_specs = [tile, tile] + [whole((depth, width))] * n
    args = [own, sib, *pieces]
    if not first:
        in_specs += [whole((rows, width))] * 2
        args += list(acc)
    scratch = []
    if last:
        in_specs += [whole((rows, width))] * 4
        args += list(tables)
        scratch = [pltpu.VMEM((rows, width), F32)] * 2
    return pl.pallas_call(
        functools.partial(project_kernel, n, first, last),
        grid_spec=pltpu.PrefetchScalarGridSpec(
            num_scalar_prefetch=1,
            grid=(n,),
            in_specs=in_specs,
            out_specs=[whole((rows, width))] * 2,
            scratch_shapes=scratch,
        ),
        out_shape=[jax.ShapeDtypeStruct((rows, width), BF16 if last else F32)] * 2,
        compiler_params=pltpu.CompilerParams(vmem_limit_bytes=40 << 20),
        cost_estimate=pl.CostEstimate(
            flops=4 * rows * depth * width * n,
            bytes_accessed=n * depth * (4 * rows + 2 * width) + 16 * rows * width,
            transcendentals=0,
        ),
    )(blocks, *args)


def attend_kernel(nblk, heads, picks, where, raw, cosine, sine, kv, out, ksel, vsel, qsel):
    def body(i, carry):
        block = where[0] + i
        core = where[3]
        for t in range(PICKS):
            pick = picks[i, t]
            chunk = pick // 16
            inside = (pick % 16) * BLK
            away_x = chunk % SIDE - where[1] + SIDE
            away_z = lax.rem(chunk // SIDE + where[2], 2)
            k_slot = lax.rem(away_x, SIDE) * 2 + away_z + core * 8
            v_slot = lax.rem(2 * SIDE - away_x, SIDE) * 2 + away_z + (1 - core) * 8
            k_row = pl.multiple_of(k_slot * 1024 + inside, BLK)
            v_row = pl.multiple_of(v_slot * 1024 + inside, BLK)
            ksel[t * BLK : (t + 1) * BLK, :] = kv[pl.ds(k_row, BLK), :]
            vsel[t * BLK : (t + 1) * BLK, :] = kv[pl.ds(v_row, BLK), :]
        rows = pl.ds(pl.multiple_of(i * BLK, BLK), BLK)
        cos, sin = cosine[rows, :], sine[rows, :]
        for h in range(heads):
            q = rotated(raw[rows, h * HD : (h + 1) * HD], cos, sin) * HD**-0.5
            qsel[h * BLK : (h + 1) * BLK, :] = q.astype(BF16)
        scores = lax.dot_general(
            ksel[...], qsel[...], (((1,), (1,)), ((), ())), preferred_element_type=F32
        )
        parts = []
        for t in range(PICKS):
            part = scores[t * BLK : (t + 1) * BLK, :]
            if t == 0:
                key = lax.broadcasted_iota(jnp.int32, part.shape, 0)
                query = lax.rem(lax.broadcasted_iota(jnp.int32, part.shape, 1), BLK)
                part = jnp.where(key <= query, part, -1e30)
            else:
                part = part + jnp.where(picks[i, t] > block, -1e30, 0.0).astype(F32)
            parts.append(part)
        scores = jnp.concatenate(parts, axis=0)
        top = jnp.max(scores, axis=0, keepdims=True)
        weights = jnp.exp(scores - top)
        total = jnp.sum(weights, axis=0, keepdims=True)
        mixed = lax.dot_general(
            vsel[...], weights.astype(BF16), (((0,), (0,)), ((), ())), preferred_element_type=F32
        )
        mixed = (mixed / total).T.astype(BF16)
        for h in range(heads):
            out[rows, h * HD : (h + 1) * HD] = mixed[h * BLK : (h + 1) * BLK, :]
        return carry

    lax.fori_loop(0, nblk, body, 0)


def attend(picks, where, raw, cosine, sine, kv):
    rows, width = raw.shape
    heads = width // HD
    nblk = rows // BLK
    smem = pl.BlockSpec(memory_space=pltpu.SMEM)
    vmem = pl.BlockSpec(memory_space=pltpu.VMEM)
    pairs = rows * heads * PICKS * BLK
    return pl.pallas_call(
        functools.partial(attend_kernel, nblk, heads),
        in_specs=[smem, smem, vmem, vmem, vmem, vmem],
        out_specs=vmem,
        out_shape=jax.ShapeDtypeStruct((rows, width), BF16),
        scratch_shapes=[
            pltpu.VMEM((PICKS * BLK, HD), BF16),
            pltpu.VMEM((PICKS * BLK, HD), BF16),
            pltpu.VMEM((heads * BLK, HD), BF16),
        ],
        compiler_params=pltpu.CompilerParams(vmem_limit_bytes=40 << 20),
        cost_estimate=pl.CostEstimate(
            flops=4 * pairs * HD, bytes_accessed=kv.size * 2 + raw.size * 8, transcendentals=pairs
        ),
    )(picks, where, raw, cosine, sine, kv)


def tables_of(first, rows):
    positions = first + jnp.arange(rows)
    half = HD // 2
    freq = 500000.0 ** (-(jnp.arange(half).astype(F32) * 2.0 / HD))
    angle = positions.astype(F32)[:, None] * freq[None, :]
    cosine, sine = jnp.cos(angle), jnp.sin(angle)
    return jnp.concatenate([cosine, cosine], 1), jnp.concatenate([-sine, sine], 1)


def local(activations, query_weight, kv_weight, picks):
    own = activations[0]
    rows = own.shape[0]
    shard = query_weight.shape[0]
    half = shard // 2
    width = query_weight.shape[1] // 2
    dp, seq = lax.axis_index("dp"), lax.axis_index("seq")
    y, z_lo = dp % SIDE, dp // SIDE
    z_hi, x, c = seq // 8, (seq // 2) % SIDE, seq % 2
    mine = x % 2
    step = 1 - 2 * c

    def block(k, flip, h):
        shard_at = (z_lo ^ flip) * SIDE + (y + step * k + 2 * SIDE) % SIDE
        return shard_at if h is None else shard_at * 2 + (mine if h == 0 else 1 - mine)

    def blocks(*names):
        return jnp.stack([block(*name) for name in names]).astype(jnp.int32)

    kv_a0 = lax.dynamic_slice(kv_weight, (0, c * HD), (shard, HD))
    sib = get(own, FROM_CORE)
    sib_picks = get(picks[0], FROM_CORE)
    kv_a1 = get(kv_a0, FROM_Y)
    kv_b0 = get(kv_a0, FROM_Z)
    kv_a2 = get(kv_a1, FROM_Y)
    kv_b1 = get(kv_a1, FROM_Z)
    kv_a3 = get(kv_a2, FROM_Y)
    kv_b2 = get(kv_a2, FROM_Z)
    kv_b3 = get(kv_a3, FROM_Z)

    a0n = lax.dynamic_slice(query_weight, (mine * half, c * width), (half, width))
    a0f = lax.dynamic_slice(query_weight, ((1 - mine) * half, c * width), (half, width))
    a1n = get(a0n, FROM_Y)
    b0n = get(a0n, FROM_Z)
    a1f = get(a1n, FROM_PAIR)
    a2n = get(a1n, FROM_Y)
    b1n = get(a1n, FROM_Z)
    a2f = get(a2n, FROM_PAIR)
    a3n = get(a2n, FROM_Y)
    b0f = get(a0f, FROM_Z)
    a3f = get(a3n, FROM_PAIR)
    b1f = get(b0f, FROM_Y)
    b2n = get(a2n, FROM_Z)
    b2f = get(b2n, FROM_PAIR)
    b3n = get(b2n, FROM_Y)
    b3f = get(a3f, FROM_Z)

    cos_own, sin_own = tables_of(seq * rows, rows)
    cos_sib, sin_sib = tables_of((seq + step) * rows, rows)
    plain = c == 1
    kv_tables = [
        jnp.where(plain, 1.0, cos_own), jnp.where(plain, 0.0, sin_own),
        jnp.where(plain, 1.0, cos_sib), jnp.where(plain, 0.0, sin_sib),
    ]
    kv_own, kv_sib = project(
        blocks(*[(k, flip, None) for flip in (0, 1) for k in range(SIDE)]),
        own, sib, [kv_a0, kv_a1, kv_a2, kv_a3, kv_b0, kv_b1, kv_b2, kv_b3],
        tables=kv_tables,
    )
    here = jnp.where(
        plain,
        jnp.concatenate([kv_sib, kv_own], 0),
        jnp.concatenate([kv_own, kv_sib], 0),
    )
    chunks = [jnp.concatenate([here, get(here, FROM_Z2)], 0)]
    for _ in range(SIDE - 1):
        chunks.append(get(chunks[-1], FROM_X))
    kv = jnp.concatenate(chunks + [get(chunk, FROM_CORE) for chunk in chunks], 0)

    acc = project(blocks((0, 0, 0), (0, 0, 1)), own, sib, [a0n, a0f])
    acc = project(blocks((1, 0, 0), (0, 1, 0)), own, sib, [a1n, b0n], acc)
    acc = project(blocks((1, 0, 1), (2, 0, 0), (1, 1, 0)), own, sib, [a1f, a2n, b1n], acc)
    acc = project(blocks((2, 0, 1), (3, 0, 0), (0, 1, 1)), own, sib, [a2f, a3n, b0f], acc)
    acc = project(blocks((3, 0, 1), (1, 1, 1), (2, 1, 0)), own, sib, [a3f, b1f, b2n], acc)
    acc = project(blocks((2, 1, 1), (3, 1, 0), (3, 1, 1)), own, sib, [b2f, b3n, b3f], acc)

    blocks_here = rows // BLK

    def where(s):
        return jnp.stack([s * blocks_here, x, z_hi, c]).astype(jnp.int32)

    out_sib = attend(sib_picks, where(seq + step), acc[1], cos_sib, sin_sib, kv)
    received = get(out_sib, FROM_CORE)
    out_own = attend(picks[0], where(seq), acc[0], cos_own, sin_own, kv)
    out = jnp.where(
        plain,
        jnp.concatenate([received, out_own], 1),
        jnp.concatenate([out_own, received], 1),
    )
    return out[None]


def solution(mesh):
    in_specs = (P("dp", "seq", None), P("dp", None), P("dp", None), P("dp", "seq", None))
    out_specs = P("dp", "seq", None)
    return jax.shard_map(local, mesh=mesh, in_specs=in_specs, out_specs=out_specs, check_vma=False)
```

time: 668 us -> 182 us (0.27)
  waiting for transfers between devices: 511 us -> 46.7 us
  Pallas kernels: 0 us -> 71.6 us
  matrix products: 54.8 us -> 0 us
  local copies, waits for them, and re-layouts: 63.5 us -> 11.2 us
  starting transfers between devices: 0.13 us -> 41 us
  between operations: 13.3 us -> 0.36 us
  other arithmetic: 23.4 us -> 10.6 us
    all_gather x4 -> x0, waiting for transfers between devices: 510 us -> none  [the longest x1 322 us: local(): query_raw = add_rows(lax.all_gather(query_weight, 'dp', axis=0, tiled=True))]
    pallas_call x0 -> x9, Pallas kernels: none -> 71.6 us  [the longest x7 54.5 us: project(): pl.pallas_call(functools.partial(project_kernel, n, first, last), grid_sp...]
    dot_general x4 -> x0, matrix products: 54.8 us -> none  [the longest x2 36.7 us: add_rows(): return jnp.dot(tokens, piece, preferred_element_type=jnp.float32)]
    ppermute x0 -> x32, waiting for transfers between devices: none -> 46.7 us  [get(): return lax.ppermute(value, AXES, perm)]
    dot_general x1 -> x0, local copies, waits for them, and re-layouts: 44 us -> none  [add_rows(): return jnp.dot(tokens, piece, preferred_element_type=jnp.float32)]
    ppermute x0 -> x32, starting transfers between devices: none -> 41 us  [get(): return lax.ppermute(value, AXES, perm)]
    sub x2 -> x0, other arithmetic: 20.5 us -> none  [the longest x1 19.1 us: local(): weights = jnp.exp(logit_scores - top)]
    unnamed x6 -> x39, local copies, waits for them, and re-layouts: 0.11 us -> 9.38 us
  transfers between devices with their start and end apart: 4 -> 32, of which waited for: 4 -> 9; matrix products, arithmetic and copies ran while one was open for 2% -> 6% of each run, Pallas kernels for 0% -> 35%
where the time goes in v1:
time: 182 us; the launch traced here: 181 us
  Pallas kernels  71.6 us (39%)
  waiting for transfers between devices  46.7 us (26%)
  starting transfers between devices  41 us (23%)
  local copies, waits for them, and re-layouts  11.2 us (6%)
  other arithmetic  10.6 us (6%)
    pallas_call x7, Pallas kernels, project(): pl.pallas_call(functools.partial(project_kernel, n, first, last), grid_sp...  54.5 us
    ppermute x32, waiting for transfers between devices, get(): return lax.ppermute(value, AXES, perm)  46.7 us
    ppermute x32, starting transfers between devices, get(): return lax.ppermute(value, AXES, perm)  41 us
    pallas_call x2, Pallas kernels, attend(): pl.pallas_call(functools.partial(attend_kernel, nblk, heads), in_specs=[s...  17.1 us
    unnamed x39, local copies, waits for them, and re-layouts  9.38 us
  transfers between devices with their start and end apart: 32, of which 9 were waited for; matrix products, arithmetic and copies ran while one was open for 6% of the time, Pallas kernels for 35%

profile of v1, /device:TPU:1, one launch (start us, length us, event | category | flops | bytes accessed | tf_op | source)
XLA Modules:
  0.0 181.4 jit_solution(12758501539778824211)
XLA Ops:
  0.0 1.4 collective-permute-start.1
  1.4 1.7 fusion.2
  3.1 1.4 collective-permute-start.2
  4.6 1.4 collective-permute-start.16
  6.0 1.6 collective-permute-start.19
  7.6 0.8 copy-done.4
  8.4 9.9 %collective-permute-done.2.refs_3_ = bf16[1024,512]{1,0:T(8,128)(2,1)} collective-permute-done((bf16[1024,512]{1,0:T(8,128)(2,1)S(1)}, bf16[1024,512]{1,0:T(8,128)(2,1)}, u32[]{:S(2)}, u32[]{:S(2)}) %collective-permute-start.2) | collective-permute-done | bytes 1048608 | tf_op jit(solution)/shard_map/ppermute | solution.py:46
  18.3 0.3 collective-permute-start.3
  18.6 1.6 collective-permute-start.15
  20.2 3.6 %collective-permute-done.16.refs_4_ = bf16[2048,128]{1,0:T(8,128)(2,1)S(1)} collective-permute-done((bf16[2048,128]{1,0:T(8,128)(2,1)S(1)}, bf16[2048,128]{1,0:T(8,128)(2,1)S(1)}, u32[]{:S(2)}, u32[]{:S(2)}) %collective-permute-start.16) | collective-permute-done | bytes 524320 | tf_op jit(solution)/shard_map/ppermute | solution.py:46
  23.8 0.4 collective-permute-start.17
  24.2 0.8 copy-done.13
  25.0 1.6 collective-permute-start.20
  26.7 14.1 %collective-permute-done.17.refs_5_ = bf16[2048,128]{1,0:T(8,128)(2,1)} collective-permute-done((bf16[2048,128]{1,0:T(8,128)(2,1)S(1)}, bf16[2048,128]{1,0:T(8,128)(2,1)}, u32[]{:S(2)}, u32[]{:S(2)}) %collective-permute-start.17) | collective-permute-done | bytes 524320 | tf_op jit(solution)/shard_map/ppermute | solution.py:46
  40.8 1.6 collective-permute-start.10
  42.4 0.4 collective-permute-start.18
  42.8 1.4 collective-permute-start.7
  44.2 1.6 collective-permute-start.21
  46.0 3.0 %fusion = (f32[512,64]{1,0:T(8,128)}, f32[512,64]{1,0:T(8,128)}, f32[512,64]{1,0:T(8,128)}, f32[512,64]{1,0:T(8,128)S(1)}, f32[512,64]{1,0:T(8,128)}, /*index=5*/f32[512,64]{1,0:T(8,128)}) fusion(f32[64]{0:T(128)S(1)} %negate_power_fusion, f32[512]{0:T(512)S(1)} %add_convert_fusion.1, f32[512]{0:T(512)S(1)} %add_convert_fusion), kind=kLoop, calls=%fused_computation.15 | loop fusion | flops 131072 | bytes 790784 | tf_op jit(solution)/shard_map/neg | solution.py:207
  48.9 3.1 %collective-permute-done.18.refs_6_ = bf16[2048,128]{1,0:T(8,128)(2,1)} collective-permute-done((bf16[2048,128]{1,0:T(8,128)(2,1)}, bf16[2048,128]{1,0:T(8,128)(2,1)}, u32[]{:S(2)}, u32[]{:S(2)}) %collective-permute-start.18) | collective-permute-done | bytes 524320 | tf_op jit(solution)/shard_map/ppermute | solution.py:46
  52.0 1.6 collective-permute-start.22
  53.7 0.1 pad_add_fusion.3.refs_0_
  53.8 0.1 pad_add_fusion.2.refs_0_
  53.8 3.3 %collective-permute-done.10.refs_5_ = bf16[1024,512]{1,0:T(8,128)(2,1)} collective-permute-done((bf16[1024,512]{1,0:T(8,128)(2,1)S(1)}, bf16[1024,512]{1,0:T(8,128)(2,1)}, u32[]{:S(2)}, u32[]{:S(2)}) %collective-permute-start.10) | collective-permute-done | bytes 1048608 | tf_op jit(solution)/shard_map/ppermute | solution.py:46
  57.1 2.5 %collective-permute-start.13 = (bf16[1024,512]{1,0:T(8,128)(2,1)}, bf16[1024,512]{1,0:T(8,128)(2,1)}, u32[]{:S(2)}, u32[]{:S(2)}) collective-permute-start(bf16[1024,512]{1,0:T(8,128)(2,1)} %collective-permute-done.2.refs_3_), channel_id=1, source_target_pairs={{2,0},{7,1},{66,64},{71,65},{10,8},{15,9},{74,72},{79,73},{18,16},... | collective-permute-start | bytes 3145736 | tf_op jit(solution)/shard_map/ppermute | solution.py:46
  59.6 3.1 %collective-permute-done.21.refs_9_ = bf16[2048,128]{1,0:T(8,128)(2,1)} collective-permute-done((bf16[2048,128]{1,0:T(8,128)(2,1)}, bf16[2048,128]{1,0:T(8,128)(2,1)}, u32[]{:S(2)}, u32[]{:S(2)}) %collective-permute-start.21) | collective-permute-done | bytes 524320 | tf_op jit(solution)/shard_map/ppermute | solution.py:46
  62.7 0.1 pad_add_fusion.1.refs_0_
  62.8 2.1 %broadcast_select_fusion.1 = (f32[512,128]{1,0:T(8,128)S(1)}, f32[512,128]{1,0:T(8,128)}, f32[512,128]{1,0:T(8,128)}, f32[512,128]{1,0:T(8,128)S(1)}) fusion(pred[]{:T(512)S(6)} %eq.32, f32[512,64]{1,0:T(8,128)S(1)} %get-tuple-element.51, f32[512,64]{1,0:T(8,128)} %get-tuple-element.53, f32[512,64]{1,0:T(8,128)} %get-tuple-element.52), kind=kLoop, calls=%fused_computation.12 | loop fusion | flops 262144 | bytes 1441793 | tf_op jit(solution)/shard_map/jit(_where)/select_n | solution.py:261
  64.9 2.3 %pad_maximum_fusion.1 = (f32[512,128]{1,0:T(8,128)}, f32[512,128]{1,0:T(8,128)S(1)}, f32[512,128]{1,0:T(8,128)}, f32[512,128]{1,0:T(8,128)}) fusion(f32[512,64]{1,0:T(8,128)} %get-tuple-element.47, pred[]{:T(512)S(6)} %eq.32, f32[512,64]{1,0:T(8,128)} %get-tuple-element.46, f32[512,64]{1,0:T(8,128)} %get-tuple-element.45), kind=kLoop, calls=%fused_computation.6 | loop fusion | flops 262144 | bytes 1441793 | tf_op jit(solution)/shard_map/concatenate | solution.py:207
  67.2 1.2 collective-permute-done.22.refs_10_
  68.3 2.5 %collective-permute-start.8 = (bf16[1024,512]{1,0:T(8,128)(2,1)}, bf16[1024,512]{1,0:T(8,128)(2,1)}, u32[]{:S(2)}, u32[]{:S(2)}) collective-permute-start(bf16[1024,512]{1,0:T(8,128)(2,1)} %collective-permute-done.7.refs_4_), channel_id=1, source_target_pairs={{2,0},{7,1},{66,64},{71,65},{10,8},{15,9},{74,72},{79,73},{18,16},... | collective-permute-start | bytes 3145736 | tf_op jit(solution)/shard_map/ppermute | solution.py:46
  70.8 0.1 pad_add_fusion.refs_0_
  70.9 0.1 stack.152.refs_0_
  71.0 0.1 add_add_fusion.where
  71.1 0.4 collective-permute-start.12
  71.5 0.9 copy-done.6
  72.4 1.0 copy-done.12
  73.5 1.0 copy-done.14
  74.5 17.2 %shard_map.52 = (bf16[512,128]{1,0:T(8,128)(2,1)S(1)}, bf16[512,128]{1,0:T(8,128)(2,1)S(1)}) custom-call(s32[8]{0:T(128)S(1)} %stack.152.refs_0_, bf16[512,16384]{1,0:T(8,128)(2,1)} %bitcast.37, bf16[512,16384]{1,0:T(8,128)(2,1)} %collective-permute-done.1.refs_2_, bf16[2048,128]{1,0:T(8,128)(2,1)S(1)} %copy-done.5, bf16[2048,128]{1,0:T(8,128)(2,1)S(1)} %copy-done.12, ...), custom_call_target="tpu_custom_call" | custom-call | flops 4294967296 | bytes 38797312 | tf_op jit(solution)/shard_map/pallas_call | solution.py:109
  91.9 0.2 collective-permute-start.11
  92.1 3.1 %collective-permute-start.23 = (bf16[1024,128]{1,0:T(8,128)(2,1)S(1)}, bf16[1024,128]{1,0:T(8,128)(2,1)S(1)}, u32[]{:S(2)}, u32[]{:S(2)}) collective-permute-start(bf16[1024,128]{1,0:T(8,128)(2,1)S(1)} %get-tuple-element.34), channel_id=1, source_target_pairs={{8,0},{9,1},{72,64},{73,65},{0,8},{1,9},{64,72},{65,73},{24,16},{2... | collective-permute-start | bytes 786440 | tf_op jit(solution)/shard_map/ppermute | solution.py:46
  95.2 4.7 %shard_map.46 = (f32[512,512]{1,0:T(8,128)S(1)}, f32[512,512]{1,0:T(8,128)S(1)}) custom-call(s32[2]{0:T(128)S(1)} %pad_add_fusion.5.refs_0_, bf16[512,16384]{1,0:T(8,128)(2,1)} %bitcast.38, bf16[512,16384]{1,0:T(8,128)(2,1)} %collective-permute-done.1.refs_2_, bf16[1024,512]{1,0:T(8,128)(2,1)S(1)} %get-tuple-element.40.refs_3_, ...), custom_call_target="tpu_custom_call" | custom-call | flops 2147483648 | bytes 10485760 | tf_op jit(solution)/shard_map/pallas_call | solution.py:109
  99.9 5.4 %shard_map.47 = (f32[512,512]{1,0:T(8,128)S(1)}, f32[512,512]{1,0:T(8,128)S(1)}) custom-call(s32[2]{0:T(128)S(1)} %pad_add_fusion.4.refs_0_, bf16[512,16384]{1,0:T(8,128)(2,1)} %bitcast.39, bf16[512,16384]{1,0:T(8,128)(2,1)} %collective-permute-done.1.refs_2_, bf16[1024,512]{1,0:T(8,128)(2,1)} %collective-permute-done.2.refs_3_, ...), custom_call_target="tpu_custom_call" | custom-call | flops 2147483648 | bytes 10485760 | tf_op jit(solution)/shard_map/pallas_call | solution.py:109
  105.2 2.6 %collective-permute-start.5 = (bf16[1024,512]{1,0:T(8,128)(2,1)}, bf16[1024,512]{1,0:T(8,128)(2,1)S(1)}, u32[]{:S(2)}, u32[]{:S(2)}) collective-permute-start(bf16[1024,512]{1,0:T(8,128)(2,1)} %collective-permute-done.4.refs_5_), channel_id=1, source_target_pairs={{2,0},{7,1},{66,64},{71,65},{10,8},{15,9},{74,72},{79,73},{18,16},... | collective-permute-start | bytes 3145736 | tf_op jit(solution)/shard_map/ppermute | solution.py:46
  107.8 1.0 collective-permute-start.6
  108.8 0.3 collective-permute-start.9
  109.2 7.2 %shard_map.48 = (f32[512,512]{1,0:T(8,128)S(1)}, f32[512,512]{1,0:T(8,128)S(1)}) custom-call(s32[3]{0:T(128)S(1)} %pad_add_fusion.3.refs_0_, bf16[512,16384]{1,0:T(8,128)(2,1)} %bitcast.40, bf16[512,16384]{1,0:T(8,128)(2,1)} %collective-permute-done.1.refs_2_, bf16[1024,512]{1,0:T(8,128)(2,1)} %collective-permute-done.13.refs_3_, ...), custom_call_target="tpu_custom_call" | custom-call | flops 3221225472 | bytes 13631488 | tf_op jit(solution)/shard_map/pallas_call | solution.py:109
  116.5 6.9 %shard_map.49 = (f32[512,512]{1,0:T(8,128)S(1)}, f32[512,512]{1,0:T(8,128)S(1)}) custom-call(s32[3]{0:T(128)S(1)} %pad_add_fusion.2.refs_0_, bf16[512,16384]{1,0:T(8,128)(2,1)} %bitcast.41, bf16[512,16384]{1,0:T(8,128)(2,1)} %collective-permute-done.1.refs_2_, bf16[1024,512]{1,0:T(8,128)(2,1)S(1)} %collective-permute-done.12.refs_3_, ...), custom_call_target="tpu_custom_call" | custom-call | flops 3221225472 | bytes 13631488 | tf_op jit(solution)/shard_map/pallas_call | solution.py:109
  123.4 7.9 %collective-permute-start = (s32[8,16]{1,0:T(8,128)S(1)}, s32[8,16]{1,0:T(8,128)S(1)}, u32[]{:S(2)}, u32[]{:S(2)}) collective-permute-start(s32[8,16]{1,0:T(8,128)S(1)} %bitcast.34), channel_id=1, source_target_pairs={{1,0},{0,1},{65,64},{64,65},{9,8},{8,9},{73,72},{72,73},{17,16},{1... | collective-permute-start | bytes 1544 | tf_op jit(solution)/shard_map/ppermute | solution.py:46
  131.3 6.9 %shard_map.50 = (f32[512,512]{1,0:T(8,128)S(1)}, f32[512,512]{1,0:T(8,128)S(1)}) custom-call(s32[3]{0:T(128)S(1)} %pad_add_fusion.1.refs_0_, bf16[512,16384]{1,0:T(8,128)(2,1)} %bitcast.42, bf16[512,16384]{1,0:T(8,128)(2,1)} %collective-permute-done.1.refs_2_, bf16[1024,512]{1,0:T(8,128)(2,1)} %collective-permute-done.8.refs_3_, ...), custom_call_target="tpu_custom_call" | custom-call | flops 3221225472 | bytes 13631488 | tf_op jit(solution)/shard_map/pallas_call | solution.py:109
  138.2 6.3 %shard_map.51 = (f32[512,512]{1,0:T(8,128)S(1)}, f32[512,512]{1,0:T(8,128)S(1)}) custom-call(s32[3]{0:T(128)S(1)} %pad_add_fusion.refs_0_, bf16[512,16384]{1,0:T(8,128)(2,1)} %bitcast.43, bf16[512,16384]{1,0:T(8,128)(2,1)} %collective-permute-done.1.refs_2_, bf16[1024,512]{1,0:T(8,128)(2,1)S(1)} %collective-permute-done.5.refs_3_, ...), custom_call_target="tpu_custom_call" | custom-call | flops 3221225472 | bytes 13631488 | tf_op jit(solution)/shard_map/pallas_call | solution.py:109
  144.5 1.6 collective-permute-start.27
  146.1 0.6 collective-permute-start.26
  146.7 1.5 collective-permute-start.28
  148.2 0.1 collective-permute-start.29
  148.4 7.0 %collective-permute-done.26 = bf16[2048,128]{1,0:T(8,128)(2,1)S(1)} collective-permute-done((bf16[2048,128]{1,0:T(8,128)(2,1)S(1)}, bf16[2048,128]{1,0:T(8,128)(2,1)S(1)}, u32[]{:S(2)}, u32[]{:S(2)}) %collective-permute-start.26) | collective-permute-done | bytes 524320 | tf_op jit(solution)/shard_map/ppermute | solution.py:46
  155.7 1.5 collective-permute-done.30
  157.3 8.6 %shard_map.53 = bf16[512,512]{1,0:T(8,128)(2,1)S(1)} custom-call(s32[8,16]{1,0:T(8,128)S(1)} %collective-permute-done.picks, s32[4]{0:T(128)S(1)} %add_add_fusion.where, f32[512,512]{1,0:T(8,128)S(1)} %get-tuple-element.29.raw, f32[512,128]{1,0:T(8,128)S(1)} %copy-done.9, f32[512,128]{1,0:T(8,128)S(1)} %copy-done.10, ...), custom_call_target="tpu_custom_call" | custom-call | flops 1073741824 | bytes 6291456 | tf_op jit(solution)/shard_map/pallas_call | solution.py:184
  165.9 2.0 %copy-done.2 = bf16[16384,128]{1,0:T(8,128)(2,1)} copy-done((bf16[16384,128]{1,0:T(8,128)(2,1)}, bf16[16384,128]{1,0:T(8,128)(2,1)S(1)}, u32[]{:S(2)}) %copy-start.2) | copy-done | bytes 4194328
  167.9 0.1 collective-permute-start.31
  168.0 0.1 add_add_fusion.1.where
  168.1 2.3 %copy-done.3 = bf16[16384,128]{1,0:T(8,128)(2,1)S(1)} copy-done((bf16[16384,128]{1,0:T(8,128)(2,1)S(1)}, bf16[16384,128]{1,0:T(8,128)(2,1)}, u32[]{:S(2)}) %copy-start.3) | copy-done | bytes 4194328
  170.4 8.5 %shard_map.54 = bf16[512,512]{1,0:T(8,128)(2,1)S(1)} custom-call(s32[8,16]{1,0:T(8,128)S(1)} %bitcast.35, s32[4]{0:T(128)S(1)} %add_add_fusion.1.where, f32[512,512]{1,0:T(8,128)S(1)} %get-tuple-element.32.raw, f32[512,128]{1,0:T(8,128)S(1)} %copy-done.8, f32[512,128]{1,0:T(8,128)S(1)} %copy-done.7, bf16[16384,128]{1,0:T(8,128)(2,1)S(1)} %copy-done.3), custom_call_target="tpu_custom_call" | custom-call | flops 1073741824 | bytes 6291456 | tf_op jit(solution)/shard_map/pallas_call | solution.py:184
  178.9 2.5 %maximum_select_fusion = bf16[1,512,1024]{2,1,0:T(8,128)(2,1)} fusion(bf16[1,512,512]{2,1,0:T(8,128)(2,1)S(1)} %bitcast.33, bf16[1,512,512]{2,1,0:T(8,128)(2,1)} %bitcast.30, pred[]{:T(512)S(6)} %eq.32), kind=kLoop, calls=%fused_computation | loop fusion | flops 4718592 | bytes 2097153 | tf_op jit(solution)/shard_map/jit(_where)/select_n | solution.py:294
  (69 shorter events, 1.1 us)
Async XLA Ops:
  0.0 4.6 %copy-start = (bf16[2048,256]{1,0:T(8,128)(2,1)S(1)}, bf16[2048,256]{1,0:T(8,128)(2,1)}, u32[]{:S(2)}) copy-start(bf16[2048,256]{1,0:T(8,128)(2,1)} %param.6) | copy-start | bytes 3145732
  0.0 71.1 %collective-permute-start.1 = (bf16[512,16384]{1,0:T(8,128)(2,1)}, bf16[512,16384]{1,0:T(8,128)(2,1)}, u32[]{:S(2)}, u32[]{:S(2)}) collective-permute-start(bf16[512,16384]{1,0:T(8,128)(2,1)} %bitcast.36), channel_id=1, source_target_pairs={{1,0},{0,1},{65,64},{64,65},{9,8},{8,9},{73,72},{72,73},{17,16},{1... | collective-permute-start | bytes 50331656 | tf_op jit(solution)/shard_map/ppermute | solution.py:46
  3.1 15.2 %collective-permute-start.2 = (bf16[1024,512]{1,0:T(8,128)(2,1)S(1)}, bf16[1024,512]{1,0:T(8,128)(2,1)}, u32[]{:S(2)}, u32[]{:S(2)}) collective-permute-start(bf16[1024,512]{1,0:T(8,128)(2,1)S(1)} %get-tuple-element.40.refs_3_), channel_id=1, source_target_pairs={{16,0},{49,1},{80,64},{113,65},{24,8},{57,9},{88,72},{121,73},{32,... | collective-permute-start | bytes 3145736 | tf_op jit(solution)/shard_map/ppermute | solution.py:46
  4.6 19.2 %collective-permute-start.16 = (bf16[2048,128]{1,0:T(8,128)(2,1)S(1)}, bf16[2048,128]{1,0:T(8,128)(2,1)S(1)}, u32[]{:S(2)}, u32[]{:S(2)}) collective-permute-start(bf16[2048,128]{1,0:T(8,128)(2,1)S(1)} %constant_dynamic-slice_fusion.refs_3_), channel_id=1, source_target_pairs={{16,0},{49,1},{80,64},{113,65},{24,8},{57,9},{88,72},{121,73},{32,... | collective-permute-start | bytes 1572872 | tf_op jit(solution)/shard_map/ppermute | solution.py:46
  6.0 18.3 %collective-permute-start.19 = (bf16[2048,128]{1,0:T(8,128)(2,1)S(1)}, bf16[2048,128]{1,0:T(8,128)(2,1)S(1)}, u32[]{:S(2)}, u32[]{:S(2)}) collective-permute-start(bf16[2048,128]{1,0:T(8,128)(2,1)S(1)} %constant_dynamic-slice_fusion.refs_3_), channel_id=1, source_target_pairs={{64,0},{73,1},{8,64},{1,65},{72,8},{65,9},{0,72},{9,73},{80,16},{8... | collective-permute-start | bytes 1572872 | tf_op jit(solution)/shard_map/ppermute | solution.py:46
  7.6 0.8 copy-start.4
  18.3 53.2 %copy-start.5 = (bf16[2048,128]{1,0:T(8,128)(2,1)S(1)}, bf16[2048,128]{1,0:T(8,128)(2,1)}, u32[]{:S(2)}) copy-start(bf16[2048,128]{1,0:T(8,128)(2,1)} %copy-done.4) | copy-start | bytes 1572868
  18.3 24.5 %collective-permute-start.3 = (bf16[1024,512]{1,0:T(8,128)(2,1)}, bf16[1024,512]{1,0:T(8,128)(2,1)}, u32[]{:S(2)}, u32[]{:S(2)}) collective-permute-start(bf16[1024,512]{1,0:T(8,128)(2,1)} %collective-permute-done.2.refs_3_), channel_id=1, source_target_pairs={{16,0},{49,1},{80,64},{113,65},{24,8},{57,9},{88,72},{121,73},{32,... | collective-permute-start | bytes 3145736 | tf_op jit(solution)/shard_map/ppermute | solution.py:46
  18.6 25.6 %collective-permute-start.15 = (bf16[1024,512]{1,0:T(8,128)(2,1)S(1)}, bf16[1024,512]{1,0:T(8,128)(2,1)}, u32[]{:S(2)}, u32[]{:S(2)}) collective-permute-start(bf16[1024,512]{1,0:T(8,128)(2,1)S(1)} %get-tuple-element.40.refs_3_), channel_id=1, source_target_pairs={{64,0},{73,1},{8,64},{1,65},{72,8},{65,9},{0,72},{9,73},{80,16},{8... | collective-permute-start | bytes 3145736 | tf_op jit(solution)/shard_map/ppermute | solution.py:46
  23.8 39.0 %copy-start.11 = (bf16[2048,128]{1,0:T(8,128)(2,1)}, bf16[2048,128]{1,0:T(8,128)(2,1)S(1)}, u32[]{:S(2)}) copy-start(bf16[2048,128]{1,0:T(8,128)(2,1)S(1)} %collective-permute-done.16.refs_4_) | copy-start | bytes 1572868
  23.8 17.0 %collective-permute-start.17 = (bf16[2048,128]{1,0:T(8,128)(2,1)S(1)}, bf16[2048,128]{1,0:T(8,128)(2,1)}, u32[]{:S(2)}, u32[]{:S(2)}) collective-permute-start(bf16[2048,128]{1,0:T(8,128)(2,1)S(1)} %collective-permute-done.16.refs_4_), channel_id=1, source_target_pairs={{16,0},{49,1},{80,64},{113,65},{24,8},{57,9},{88,72},{121,73},{32,... | collective-permute-start | bytes 1572872 | tf_op jit(solution)/shard_map/ppermute | solution.py:46
  24.2 0.8 copy-start.13
  25.0 17.4 %collective-permute-start.20 = (bf16[2048,128]{1,0:T(8,128)(2,1)S(1)}, bf16[2048,128]{1,0:T(8,128)(2,1)}, u32[]{:S(2)}, u32[]{:S(2)}) collective-permute-start(bf16[2048,128]{1,0:T(8,128)(2,1)S(1)} %collective-permute-done.16.refs_4_), channel_id=1, source_target_pairs={{64,0},{73,1},{8,64},{1,65},{72,8},{65,9},{0,72},{9,73},{80,16},{8... | collective-permute-start | bytes 1572872 | tf_op jit(solution)/shard_map/ppermute | solution.py:46
  40.8 16.3 %collective-permute-start.10 = (bf16[1024,512]{1,0:T(8,128)(2,1)S(1)}, bf16[1024,512]{1,0:T(8,128)(2,1)}, u32[]{:S(2)}, u32[]{:S(2)}) collective-permute-start(bf16[1024,512]{1,0:T(8,128)(2,1)S(1)} %get-tuple-element.39.refs_4_), channel_id=1, source_target_pairs={{64,0},{73,1},{8,64},{1,65},{72,8},{65,9},{0,72},{9,73},{80,16},{8... | collective-permute-start | bytes 3145736 | tf_op jit(solution)/shard_map/ppermute | solution.py:46
  42.4 9.6 %collective-permute-start.18 = (bf16[2048,128]{1,0:T(8,128)(2,1)}, bf16[2048,128]{1,0:T(8,128)(2,1)}, u32[]{:S(2)}, u32[]{:S(2)}) collective-permute-start(bf16[2048,128]{1,0:T(8,128)(2,1)} %collective-permute-done.17.refs_5_), channel_id=1, source_target_pairs={{16,0},{49,1},{80,64},{113,65},{24,8},{57,9},{88,72},{121,73},{32,... | collective-permute-start | bytes 1572872 | tf_op jit(solution)/shard_map/ppermute | solution.py:46
  42.8 25.5 %collective-permute-start.7 = (bf16[1024,512]{1,0:T(8,128)(2,1)}, bf16[1024,512]{1,0:T(8,128)(2,1)}, u32[]{:S(2)}, u32[]{:S(2)}) collective-permute-start(bf16[1024,512]{1,0:T(8,128)(2,1)} %collective-permute-done.3.refs_4_), channel_id=1, source_target_pairs={{16,0},{49,1},{80,64},{113,65},{24,8},{57,9},{88,72},{121,73},{32,... | collective-permute-start | bytes 3145736 | tf_op jit(solution)/shard_map/ppermute | solution.py:46
  44.2 18.5 %collective-permute-start.21 = (bf16[2048,128]{1,0:T(8,128)(2,1)}, bf16[2048,128]{1,0:T(8,128)(2,1)}, u32[]{:S(2)}, u32[]{:S(2)}) collective-permute-start(bf16[2048,128]{1,0:T(8,128)(2,1)} %collective-permute-done.17.refs_5_), channel_id=1, source_target_pairs={{64,0},{73,1},{8,64},{1,65},{72,8},{65,9},{0,72},{9,73},{80,16},{8... | collective-permute-start | bytes 1572872 | tf_op jit(solution)/shard_map/ppermute | solution.py:46
  52.0 16.3 %collective-permute-start.22 = (bf16[2048,128]{1,0:T(8,128)(2,1)}, bf16[2048,128]{1,0:T(8,128)(2,1)}, u32[]{:S(2)}, u32[]{:S(2)}) collective-permute-start(bf16[2048,128]{1,0:T(8,128)(2,1)} %collective-permute-done.18.refs_6_), channel_id=1, source_target_pairs={{64,0},{73,1},{8,64},{1,65},{72,8},{65,9},{0,72},{9,73},{80,16},{8... | collective-permute-start | bytes 1572872 | tf_op jit(solution)/shard_map/ppermute | solution.py:46
  57.1 34.7 %collective-permute-start.13 = (bf16[1024,512]{1,0:T(8,128)(2,1)}, bf16[1024,512]{1,0:T(8,128)(2,1)}, u32[]{:S(2)}, u32[]{:S(2)}) collective-permute-start(bf16[1024,512]{1,0:T(8,128)(2,1)} %collective-permute-done.2.refs_3_), channel_id=1, source_target_pairs={{2,0},{7,1},{66,64},{71,65},{10,8},{15,9},{74,72},{79,73},{18,16},... | collective-permute-start | bytes 3145736 | tf_op jit(solution)/shard_map/ppermute | solution.py:46
  62.7 29.4 %collective-permute-start.14 = (bf16[1024,512]{1,0:T(8,128)(2,1)}, bf16[1024,512]{1,0:T(8,128)(2,1)}, u32[]{:S(2)}, u32[]{:S(2)}) collective-permute-start(bf16[1024,512]{1,0:T(8,128)(2,1)} %collective-permute-done.2.refs_3_), channel_id=1, source_target_pairs={{64,0},{73,1},{8,64},{1,65},{72,8},{65,9},{0,72},{9,73},{80,16},{8... | collective-permute-start | bytes 3145736 | tf_op jit(solution)/shard_map/ppermute | solution.py:46
  68.3 36.9 %collective-permute-start.4 = (bf16[1024,512]{1,0:T(8,128)(2,1)}, bf16[1024,512]{1,0:T(8,128)(2,1)}, u32[]{:S(2)}, u32[]{:S(2)}) collective-permute-start(bf16[1024,512]{1,0:T(8,128)(2,1)} %collective-permute-done.3.refs_4_), channel_id=1, source_target_pairs={{64,0},{73,1},{8,64},{1,65},{72,8},{65,9},{0,72},{9,73},{80,16},{8... | collective-permute-start | bytes 3145736 | tf_op jit(solution)/shard_map/ppermute | solution.py:46
  68.3 39.5 %collective-permute-start.8 = (bf16[1024,512]{1,0:T(8,128)(2,1)}, bf16[1024,512]{1,0:T(8,128)(2,1)}, u32[]{:S(2)}, u32[]{:S(2)}) collective-permute-start(bf16[1024,512]{1,0:T(8,128)(2,1)} %collective-permute-done.7.refs_4_), channel_id=1, source_target_pairs={{2,0},{7,1},{66,64},{71,65},{10,8},{15,9},{74,72},{79,73},{18,16},... | collective-permute-start | bytes 3145736 | tf_op jit(solution)/shard_map/ppermute | solution.py:46
  71.1 38.1 %collective-permute-start.12 = (bf16[1024,512]{1,0:T(8,128)(2,1)}, bf16[1024,512]{1,0:T(8,128)(2,1)S(1)}, u32[]{:S(2)}, u32[]{:S(2)}) collective-permute-start(bf16[1024,512]{1,0:T(8,128)(2,1)} %collective-permute-done.3.refs_4_), channel_id=1, source_target_pairs={{2,0},{7,1},{66,64},{71,65},{10,8},{15,9},{74,72},{79,73},{18,16},... | collective-permute-start | bytes 3145736 | tf_op jit(solution)/shard_map/ppermute | solution.py:46
  71.5 1.0 copy-start.6
  72.4 1.0 copy-start.12
  73.5 1.0 copy-start.14
  91.9 31.5 %collective-permute-start.11 = (bf16[1024,512]{1,0:T(8,128)(2,1)}, bf16[1024,512]{1,0:T(8,128)(2,1)S(1)}, u32[]{:S(2)}, u32[]{:S(2)}) collective-permute-start(bf16[1024,512]{1,0:T(8,128)(2,1)} %collective-permute-done.10.refs_5_), channel_id=1, source_target_pairs={{16,0},{49,1},{80,64},{113,65},{24,8},{57,9},{88,72},{121,73},{32,... | collective-permute-start | bytes 3145736 | tf_op jit(solution)/shard_map/ppermute | solution.py:46
  92.1 16.7 %collective-permute-start.23 = (bf16[1024,128]{1,0:T(8,128)(2,1)S(1)}, bf16[1024,128]{1,0:T(8,128)(2,1)S(1)}, u32[]{:S(2)}, u32[]{:S(2)}) collective-permute-start(bf16[1024,128]{1,0:T(8,128)(2,1)S(1)} %get-tuple-element.34), channel_id=1, source_target_pairs={{8,0},{9,1},{72,64},{73,65},{0,8},{1,9},{64,72},{65,73},{24,16},{2... | collective-permute-start | bytes 786440 | tf_op jit(solution)/shard_map/ppermute | solution.py:46
  105.2 32.9 %collective-permute-start.5 = (bf16[1024,512]{1,0:T(8,128)(2,1)}, bf16[1024,512]{1,0:T(8,128)(2,1)S(1)}, u32[]{:S(2)}, u32[]{:S(2)}) collective-permute-start(bf16[1024,512]{1,0:T(8,128)(2,1)} %collective-permute-done.4.refs_5_), channel_id=1, source_target_pairs={{2,0},{7,1},{66,64},{71,65},{10,8},{15,9},{74,72},{79,73},{18,16},... | collective-permute-start | bytes 3145736 | tf_op jit(solution)/shard_map/ppermute | solution.py:46
  107.8 30.4 %collective-permute-start.6 = (bf16[1024,512]{1,0:T(8,128)(2,1)}, bf16[1024,512]{1,0:T(8,128)(2,1)S(1)}, u32[]{:S(2)}, u32[]{:S(2)}) collective-permute-start(bf16[1024,512]{1,0:T(8,128)(2,1)} %collective-permute-done.4.refs_5_), channel_id=1, source_target_pairs={{16,0},{49,1},{80,64},{113,65},{24,8},{57,9},{88,72},{121,73},{32,... | collective-permute-start | bytes 3145736 | tf_op jit(solution)/shard_map/ppermute | solution.py:46
  108.8 29.4 %collective-permute-start.9 = (bf16[1024,512]{1,0:T(8,128)(2,1)}, bf16[1024,512]{1,0:T(8,128)(2,1)S(1)}, u32[]{:S(2)}, u32[]{:S(2)}) collective-permute-start(bf16[1024,512]{1,0:T(8,128)(2,1)} %collective-permute-done.8.refs_3_), channel_id=1, source_target_pairs={{64,0},{73,1},{8,64},{1,65},{72,8},{65,9},{0,72},{9,73},{80,16},{8... | collective-permute-start | bytes 3145736 | tf_op jit(solution)/shard_map/ppermute | solution.py:46
  109.2 22.1 %collective-permute-start.24 = (bf16[2048,128]{1,0:T(8,128)(2,1)S(1)}, bf16[2048,128]{1,0:T(8,128)(2,1)S(1)}, u32[]{:S(2)}, u32[]{:S(2)}) collective-permute-start(bf16[2048,128]{1,0:T(8,128)(2,1)S(1)} %pad_maximum_fusion), channel_id=1, source_target_pairs={{2,0},{7,1},{66,64},{71,65},{10,8},{15,9},{74,72},{79,73},{18,16},... | collective-permute-start | bytes 1572872 | tf_op jit(solution)/shard_map/ppermute | solution.py:46
  116.4 6.9 %copy-start.15 = (s32[1,8,16]{2,1,0:T(8,128)S(1)}, s32[1,8,16]{2,1,0:T(8,128)}, u32[]{:S(2)}) copy-start(s32[1,8,16]{2,1,0:T(8,128)} %param.7) | copy-start | bytes 1540
  123.4 33.9 %collective-permute-start = (s32[8,16]{1,0:T(8,128)S(1)}, s32[8,16]{1,0:T(8,128)S(1)}, u32[]{:S(2)}, u32[]{:S(2)}) collective-permute-start(s32[8,16]{1,0:T(8,128)S(1)} %bitcast.34), channel_id=1, source_target_pairs={{1,0},{0,1},{65,64},{64,65},{9,8},{8,9},{73,72},{72,73},{17,16},{1... | collective-permute-start | bytes 1544 | tf_op jit(solution)/shard_map/ppermute | solution.py:46
  131.3 14.8 %collective-permute-start.25 = (bf16[2048,128]{1,0:T(8,128)(2,1)S(1)}, bf16[2048,128]{1,0:T(8,128)(2,1)S(1)}, u32[]{:S(2)}, u32[]{:S(2)}) collective-permute-start(bf16[2048,128]{1,0:T(8,128)(2,1)S(1)} %collective-permute-done.24), channel_id=1, source_target_pairs={{2,0},{7,1},{66,64},{71,65},{10,8},{15,9},{74,72},{79,73},{18,16},... | collective-permute-start | bytes 1572872 | tf_op jit(solution)/shard_map/ppermute | solution.py:46
  144.4 12.9 %copy-start.9 = (f32[512,128]{1,0:T(8,128)S(1)}, f32[512,128]{1,0:T(8,128)}, u32[]{:S(2)}) copy-start(f32[512,128]{1,0:T(8,128)} %get-tuple-element.41.cosine) | copy-start | bytes 786436
  144.4 12.9 %copy-start.10 = (f32[512,128]{1,0:T(8,128)S(1)}, f32[512,128]{1,0:T(8,128)}, u32[]{:S(2)}) copy-start(f32[512,128]{1,0:T(8,128)} %get-tuple-element.55.sine) | copy-start | bytes 786436
  144.5 11.0 %collective-permute-start.27 = (bf16[2048,128]{1,0:T(8,128)(2,1)S(1)}, bf16[2048,128]{1,0:T(8,128)(2,1)S(1)}, u32[]{:S(2)}, u32[]{:S(2)}) collective-permute-start(bf16[2048,128]{1,0:T(8,128)(2,1)S(1)} %pad_maximum_fusion), channel_id=1, source_target_pairs={{1,0},{0,1},{65,64},{64,65},{9,8},{8,9},{73,72},{72,73},{17,16},{1... | collective-permute-start | bytes 1572872 | tf_op jit(solution)/shard_map/ppermute | solution.py:46
  146.1 9.2 %collective-permute-start.26 = (bf16[2048,128]{1,0:T(8,128)(2,1)S(1)}, bf16[2048,128]{1,0:T(8,128)(2,1)S(1)}, u32[]{:S(2)}, u32[]{:S(2)}) collective-permute-start(bf16[2048,128]{1,0:T(8,128)(2,1)S(1)} %collective-permute-done.25), channel_id=1, source_target_pairs={{2,0},{7,1},{66,64},{71,65},{10,8},{15,9},{74,72},{79,73},{18,16},... | collective-permute-start | bytes 1572872 | tf_op jit(solution)/shard_map/ppermute | solution.py:46
  146.7 8.8 %collective-permute-start.28 = (bf16[2048,128]{1,0:T(8,128)(2,1)S(1)}, bf16[2048,128]{1,0:T(8,128)(2,1)S(1)}, u32[]{:S(2)}, u32[]{:S(2)}) collective-permute-start(bf16[2048,128]{1,0:T(8,128)(2,1)S(1)} %collective-permute-done.24), channel_id=1, source_target_pairs={{1,0},{0,1},{65,64},{64,65},{9,8},{8,9},{73,72},{72,73},{17,16},{1... | collective-permute-start | bytes 1572872 | tf_op jit(solution)/shard_map/ppermute | solution.py:46
  148.2 7.4 %collective-permute-start.29 = (bf16[2048,128]{1,0:T(8,128)(2,1)S(1)}, bf16[2048,128]{1,0:T(8,128)(2,1)S(1)}, u32[]{:S(2)}, u32[]{:S(2)}) collective-permute-start(bf16[2048,128]{1,0:T(8,128)(2,1)S(1)} %collective-permute-done.25), channel_id=1, source_target_pairs={{1,0},{0,1},{65,64},{64,65},{9,8},{8,9},{73,72},{72,73},{17,16},{1... | collective-permute-start | bytes 1572872 | tf_op jit(solution)/shard_map/ppermute | solution.py:46
  155.3 1.9 %collective-permute-start.30 = (bf16[2048,128]{1,0:T(8,128)(2,1)S(1)}, bf16[2048,128]{1,0:T(8,128)(2,1)S(1)}, u32[]{:S(2)}, u32[]{:S(2)}) collective-permute-start(bf16[2048,128]{1,0:T(8,128)(2,1)S(1)} %collective-permute-done.26), channel_id=1, source_target_pairs={{1,0},{0,1},{65,64},{64,65},{9,8},{8,9},{73,72},{72,73},{17,16},{1... | collective-permute-start | bytes 1572872 | tf_op jit(solution)/shard_map/ppermute | solution.py:46
  155.6 12.5 %copy-start.7 = (f32[512,128]{1,0:T(8,128)S(1)}, f32[512,128]{1,0:T(8,128)}, u32[]{:S(2)}) copy-start(f32[512,128]{1,0:T(8,128)} %get-tuple-element.38.sine) | copy-start | bytes 786436
  155.6 12.5 %copy-start.8 = (f32[512,128]{1,0:T(8,128)S(1)}, f32[512,128]{1,0:T(8,128)}, u32[]{:S(2)}) copy-start(f32[512,128]{1,0:T(8,128)} %get-tuple-element.56.cosine) | copy-start | bytes 786436
  165.9 2.0 %copy-start.2 = (bf16[16384,128]{1,0:T(8,128)(2,1)}, bf16[16384,128]{1,0:T(8,128)(2,1)S(1)}, u32[]{:S(2)}) copy-start(bf16[16384,128]{1,0:T(8,128)(2,1)S(1)} %constant_dynamic-update-slice_fusion.kv) | copy-start | bytes 12582916
  167.9 11.0 %collective-permute-start.31 = (bf16[512,512]{1,0:T(8,128)(2,1)S(1)}, bf16[512,512]{1,0:T(8,128)(2,1)}, u32[]{:S(2)}, u32[]{:S(2)}) collective-permute-start(bf16[512,512]{1,0:T(8,128)(2,1)S(1)} %shard_map.53), channel_id=1, source_target_pairs={{1,0},{0,1},{65,64},{64,65},{9,8},{8,9},{73,72},{72,73},{17,16},{1... | collective-permute-start | bytes 1572872 | tf_op jit(solution)/shard_map/ppermute | solution.py:46
  168.1 13.3 %copy-start.1 = (bf16[2048,256]{1,0:T(8,128)(2,1)S(1)}, bf16[2048,256]{1,0:T(8,128)(2,1)}, u32[]{:S(2)}) copy-start(bf16[2048,256]{1,0:T(8,128)(2,1)} %param.6) | copy-start | bytes 3145732
  168.1 2.3 %copy-start.3 = (bf16[16384,128]{1,0:T(8,128)(2,1)S(1)}, bf16[16384,128]{1,0:T(8,128)(2,1)}, u32[]{:S(2)}) copy-start(bf16[16384,128]{1,0:T(8,128)(2,1)} %copy-done.2) | copy-start | bytes 12582916

commit v2 on v1

--- a/solution.py
+++ b/solution.py
@@ -34,9 +34,10 @@
     return 1 - 2 * c
 
 
-FROM_Y = receive_from(lambda x, y, z, c: (x, y + sign(c), z, c))
+FROM_Y = receive_from(lambda x, y, z, c: (x, y + sign(c) * sign(x % 2), z, c))
 FROM_Z = receive_from(lambda x, y, z, c: (x, y, z + sign(c), c))
 FROM_X = receive_from(lambda x, y, z, c: (x + sign(c), y, z, c))
+FROM_X_BACK = receive_from(lambda x, y, z, c: (x - sign(c), y, z, c))
 FROM_Z2 = receive_from(lambda x, y, z, c: (x, y, z + 2, c))
 FROM_PAIR = receive_from(lambda x, y, z, c: (x + sign(x % 2) * sign(c), y, z, c))
 FROM_CORE = receive_from(lambda x, y, z, c: (x, y, z, 1 - c))
@@ -44,6 +45,9 @@
 
 def get(value, perm):
     return lax.ppermute(value, AXES, perm)
+
+
+fence = lax.optimization_barrier
 
 
 def rotated(raw, cosine, sine):
@@ -116,13 +120,67 @@
             scratch_shapes=scratch,
         ),
         out_shape=[jax.ShapeDtypeStruct((rows, width), BF16 if last else F32)] * 2,
+        compiler_params=pltpu.CompilerParams(vmem_limit_bytes=56 << 20),
+        cost_estimate=pl.CostEstimate(
+            flops=4 * rows * depth * width * n,
+            bytes_accessed=n * depth * (4 * rows + 2 * width) + 16 * rows * width,
+            transcendentals=0,
+        ),
+    )(blocks, *args)
+
+
+def query_kernel(n, first, blocks, own, sib, *refs):
+    pieces, refs = refs[:n], refs[n:]
+    bases, (out_own, out_sib, held, sems) = refs[:-4], refs[-4:]
+    g = pl.program_id(0)
+
+    def fetch(p):
+        return pltpu.make_async_copy(pieces[p], held.at[p % 2], sems.at[p % 2])
+
+    for p in range(n):
+
+        @pl.when(g == p)
+        def _(p=p):
+            if p == 0:
+                fetch(0).start()
+            if p + 1 < n:
+                fetch(p + 1).start()
+            fetch(p).wait()
+            for i, (x, out) in enumerate(((own, out_own), (sib, out_sib))):
+                part = jnp.dot(x[...], held[p % 2], preferred_element_type=F32)
+                if p:
+                    out[...] += part
+                elif first:
+                    out[...] = part
+                else:
+                    out[...] = bases[i][...] + part
+
+
+def project_query(blocks, own, sib, pieces, acc=()):
+    n = len(pieces)
+    rows = own.shape[0]
+    depth, width = pieces[0].shape
+    tile = pl.BlockSpec((rows, depth), lambda g, b: (0, b[g]))
+    result = pl.BlockSpec((rows, width), lambda g, b: (0, 0))
+    return pl.pallas_call(
+        functools.partial(query_kernel, n, not acc),
+        grid_spec=pltpu.PrefetchScalarGridSpec(
+            num_scalar_prefetch=1,
+            grid=(n,),
+            in_specs=[tile, tile]
+            + [pl.BlockSpec(memory_space=pl.ANY)] * n
+            + [result] * len(acc),
+            out_specs=[result] * 2,
+            scratch_shapes=[pltpu.VMEM((2, depth, width), BF16), pltpu.SemaphoreType.DMA((2,))],
+        ),
+        out_shape=[jax.ShapeDtypeStruct((rows, width), F32)] * 2,
         compiler_params=pltpu.CompilerParams(vmem_limit_bytes=40 << 20),
         cost_estimate=pl.CostEstimate(
             flops=4 * rows * depth * width * n,
             bytes_accessed=n * depth * (4 * rows + 2 * width) + 16 * rows * width,
             transcendentals=0,
         ),
-    )(blocks, *args)
+    )(blocks, own, sib, *pieces, *acc)
 
 
 def attend_kernel(nblk, heads, picks, where, raw, cosine, sine, kv, out, ksel, vsel, qsel):
@@ -211,20 +269,17 @@
     own = activations[0]
     rows = own.shape[0]
     shard = query_weight.shape[0]
-    half = shard // 2
     width = query_weight.shape[1] // 2
     dp, seq = lax.axis_index("dp"), lax.axis_index("seq")
     y, z_lo = dp % SIDE, dp // SIDE
     z_hi, x, c = seq // 8, (seq // 2) % SIDE, seq % 2
-    mine = x % 2
     step = 1 - 2 * c
-
-    def block(k, flip, h):
-        shard_at = (z_lo ^ flip) * SIDE + (y + step * k + 2 * SIDE) % SIDE
-        return shard_at if h is None else shard_at * 2 + (mine if h == 0 else 1 - mine)
+    along = step * (1 - 2 * (x % 2))
 
     def blocks(*names):
-        return jnp.stack([block(*name) for name in names]).astype(jnp.int32)
+        return jnp.stack(
+            [(z_lo ^ flip) * SIDE + (y + along * k + SIDE) % SIDE for k, flip in names]
+        ).astype(jnp.int32)
 
     kv_a0 = lax.dynamic_slice(kv_weight, (0, c * HD), (shard, HD))
     sib = get(own, FROM_CORE)
@@ -237,22 +292,14 @@
     kv_b2 = get(kv_a2, FROM_Z)
     kv_b3 = get(kv_a3, FROM_Z)
 
-    a0n = lax.dynamic_slice(query_weight, (mine * half, c * width), (half, width))
-    a0f = lax.dynamic_slice(query_weight, ((1 - mine) * half, c * width), (half, width))
-    a1n = get(a0n, FROM_Y)
-    b0n = get(a0n, FROM_Z)
-    a1f = get(a1n, FROM_PAIR)
-    a2n = get(a1n, FROM_Y)
-    b1n = get(a1n, FROM_Z)
-    a2f = get(a2n, FROM_PAIR)
-    a3n = get(a2n, FROM_Y)
-    b0f = get(a0f, FROM_Z)
-    a3f = get(a3n, FROM_PAIR)
-    b1f = get(b0f, FROM_Y)
-    b2n = get(a2n, FROM_Z)
-    b2f = get(b2n, FROM_PAIR)
-    b3n = get(b2n, FROM_Y)
-    b3f = get(a3f, FROM_Z)
+    a0 = lax.dynamic_slice(query_weight, (0, c * width), (shard, width))
+    a1 = get(a0, FROM_Y)
+    b0 = get(a0, FROM_Z)
+    a2 = get(a1, FROM_Y)
+    b1 = get(a1, FROM_Z)
+    a3 = get(a1, FROM_PAIR)
+    b2 = get(b1, FROM_Y)
+    b3 = get(a3, FROM_Z)
 
     cos_own, sin_own = tables_of(seq * rows, rows)
     cos_sib, sin_sib = tables_of((seq + step) * rows, rows)
@@ -262,7 +309,7 @@
         jnp.where(plain, 1.0, cos_sib), jnp.where(plain, 0.0, sin_sib),
     ]
     kv_own, kv_sib = project(
-        blocks(*[(k, flip, None) for flip in (0, 1) for k in range(SIDE)]),
+        blocks(*[(k, flip) for flip in (0, 1) for k in range(SIDE)]),
         own, sib, [kv_a0, kv_a1, kv_a2, kv_a3, kv_b0, kv_b1, kv_b2, kv_b3],
         tables=kv_tables,
     )
@@ -271,17 +318,14 @@
         jnp.concatenate([kv_sib, kv_own], 0),
         jnp.concatenate([kv_own, kv_sib], 0),
     )
-    chunks = [jnp.concatenate([here, get(here, FROM_Z2)], 0)]
-    for _ in range(SIDE - 1):
-        chunks.append(get(chunks[-1], FROM_X))
+    near = jnp.concatenate([here, get(here, FROM_Z2)], 0)
+    ahead, back = fence((get(near, FROM_X), get(near, FROM_X_BACK)))
+    chunks = [near, ahead, get(ahead, FROM_X), back]
     kv = jnp.concatenate(chunks + [get(chunk, FROM_CORE) for chunk in chunks], 0)
 
-    acc = project(blocks((0, 0, 0), (0, 0, 1)), own, sib, [a0n, a0f])
-    acc = project(blocks((1, 0, 0), (0, 1, 0)), own, sib, [a1n, b0n], acc)
-    acc = project(blocks((1, 0, 1), (2, 0, 0), (1, 1, 0)), own, sib, [a1f, a2n, b1n], acc)
-    acc = project(blocks((2, 0, 1), (3, 0, 0), (0, 1, 1)), own, sib, [a2f, a3n, b0f], acc)
-    acc = project(blocks((3, 0, 1), (1, 1, 1), (2, 1, 0)), own, sib, [a3f, b1f, b2n], acc)
-    acc = project(blocks((2, 1, 1), (3, 1, 0), (3, 1, 1)), own, sib, [b2f, b3n, b3f], acc)
+    acc = project_query(blocks((0, 0), (1, 0), (0, 1)), own, sib, [a0, a1, b0])
+    acc = project_query(blocks((2, 0), (3, 0), (1, 1)), own, sib, [a2, a3, b1], acc)
+    acc = project_query(blocks((2, 1), (3, 1)), own, sib, [b2, b3], acc)
 
     blocks_here = rows // BLK
 

time: 182 us -> 203 us (1.12)
  waiting for transfers between devices: 46.7 us -> 86 us
  starting transfers between devices: 41 us -> 32.7 us
  local copies, waits for them, and re-layouts: 11.2 us -> 7.18 us
  Pallas kernels: 71.6 us -> 68.5 us
  other arithmetic: 10.6 us -> 8.09 us
    ppermute x32 -> x25, waiting for transfers between devices: 46.7 us -> 86 us  [get(): return lax.ppermute(value, AXES, perm)]
    pallas_call x7 -> x1, Pallas kernels: 54.5 us -> 18.8 us  [project(): pl.pallas_call(functools.partial(project_kernel, n, first, last), grid_sp...]
    pallas_call x0 -> x3, Pallas kernels: none -> 32.6 us  [project_query(): pl.pallas_call(functools.partial(query_kernel, n, not acc), grid_spec=plt...]
    ppermute x32 -> x25, starting transfers between devices: 41 us -> 32.7 us  [get(): return lax.ppermute(value, AXES, perm)]
    unnamed x39 -> x31, local copies, waits for them, and re-layouts: 9.38 us -> 4.73 us
  transfers between devices with their start and end apart: 32 -> 25, of which waited for: 9 -> 9; matrix products, arithmetic and copies ran while one was open for 6% -> 4% of each run, Pallas kernels for 35% -> 30%
where the time goes in v2:
time: 203 us
  waiting for transfers between devices  86 us (42%)
  Pallas kernels  68.5 us (34%)
  starting transfers between devices  32.7 us (16%)
  other arithmetic  8.09 us (4%)
  local copies, waits for them, and re-layouts  7.18 us (4%)
    ppermute x25, waiting for transfers between devices, get(): return lax.ppermute(value, AXES, perm)  86 us
    ppermute x25, starting transfers between devices, get(): return lax.ppermute(value, AXES, perm)  32.7 us
    pallas_call x3, Pallas kernels, project_query(): pl.pallas_call(functools.partial(query_kernel, n, not acc), grid_spec=plt...  32.6 us
    pallas_call x1, Pallas kernels, project(): pl.pallas_call(functools.partial(project_kernel, n, first, last), grid_sp...  18.8 us
    pallas_call x2, Pallas kernels, attend(): pl.pallas_call(functools.partial(attend_kernel, nblk, heads), in_specs=[s...  17.1 us
    unnamed x31, local copies, waits for them, and re-layouts  4.73 us
  transfers between devices with their start and end apart: 25, of which 9 were waited for; matrix products, arithmetic and copies ran while one was open for 4% of the time, Pallas kernels for 30%

profile of v2, /device:TPU:1, one launch (start us, length us, event | category | flops | bytes accessed | tf_op | source)
XLA Modules:
  0.0 202.7 jit_solution(10295040511834140239)
XLA Ops:
  0.0 1.4 collective-permute-start.1
  1.4 1.7 constant_dynamic-slice_fusion.1.refs_0_
  3.2 0.0 copy-start.5
  3.2 1.4 collective-permute-start.2
  4.7 0.0 copy-start.6
  4.7 1.4 collective-permute-start.9
  6.0 1.6 collective-permute-start.12
  7.7 27.4 %collective-permute-done.9.refs_4_ = bf16[2048,128]{1,0:T(8,128)(2,1)S(1)} collective-permute-done((bf16[2048,128]{1,0:T(8,128)(2,1)S(1)}, bf16[2048,128]{1,0:T(8,128)(2,1)S(1)}, u32[]{:S(2)}, u32[]{:S(2)}) %collective-permute-start.9) | collective-permute-done | bytes 524320 | tf_op jit(solution)/shard_map/ppermute | solution.py:47
  35.1 0.3 collective-permute-start.10
  35.4 1.6 collective-permute-start.13
  37.1 0.0 collective-permute-done.2.refs_1_
  37.1 1.6 collective-permute-start.3
  38.7 0.0 collective-permute-done.12.refs_7_
  38.7 4.8 %collective-permute-start.5 = (bf16[2048,512]{1,0:T(8,128)(2,1)}, bf16[2048,512]{1,0:T(8,128)(2,1)}, u32[]{:S(2)}, u32[]{:S(2)}) collective-permute-start(bf16[2048,512]{1,0:T(8,128)(2,1)} %collective-permute-done.2.refs_1_), channel_id=1, source_target_pairs={{2,0},{7,1},{66,64},{71,65},{10,8},{15,9},{74,72},{79,73},{18,16},... | collective-permute-start | bytes 6291464 | tf_op jit(solution)/shard_map/ppermute | solution.py:47
  43.5 0.8 collective-permute-done.10.refs_5_
  44.3 0.0 collective-permute-start.11
  44.3 1.4 collective-permute-done.13.refs_8_
  45.7 0.3 collective-permute-start.14
  46.1 7.6 %collective-permute-done.11.refs_6_ = bf16[2048,128]{1,0:T(8,128)(2,1)} collective-permute-done((bf16[2048,128]{1,0:T(8,128)(2,1)S(1)}, bf16[2048,128]{1,0:T(8,128)(2,1)}, u32[]{:S(2)}, u32[]{:S(2)}) %collective-permute-start.11) | collective-permute-done | bytes 524320 | tf_op jit(solution)/shard_map/ppermute | solution.py:47
  53.7 1.6 collective-permute-start.8
  55.3 18.6 %collective-permute-done.14.refs_9_ = bf16[2048,128]{1,0:T(8,128)(2,1)} collective-permute-done((bf16[2048,128]{1,0:T(8,128)(2,1)S(1)}, bf16[2048,128]{1,0:T(8,128)(2,1)}, u32[]{:S(2)}, u32[]{:S(2)}) %collective-permute-start.14) | collective-permute-done | bytes 524320 | tf_op jit(solution)/shard_map/ppermute | solution.py:47
  73.9 0.0 collective-permute-start.15
  74.0 0.1 pad_add_fusion.blocks
  74.0 0.1 pad_add_fusion.2.blocks
  74.1 27.8 %collective-permute-done.15.refs_10_ = bf16[2048,128]{1,0:T(8,128)(2,1)S(1)} collective-permute-done((bf16[2048,128]{1,0:T(8,128)(2,1)}, bf16[2048,128]{1,0:T(8,128)(2,1)S(1)}, u32[]{:S(2)}, u32[]{:S(2)}) %collective-permute-start.15) | collective-permute-done | bytes 524320 | tf_op jit(solution)/shard_map/ppermute | solution.py:47
  101.9 1.3 collective-permute-start.7
  103.2 1.9 fusion
  105.1 1.1 broadcast_select_fusion.1
  106.2 1.0 pad_maximum_fusion.1
  107.2 1.0 collective-permute-start.4
  108.2 0.1 pad_add_fusion.1.blocks
  108.3 0.6 stack.84.refs_0_
  108.9 0.1 add_add_fusion.where
  109.0 6.0 %collective-permute-start = (s32[8,16]{1,0:T(8,128)S(1)}, s32[8,16]{1,0:T(8,128)S(1)}, u32[]{:S(2)}, u32[]{:S(2)}) collective-permute-start(s32[8,16]{1,0:T(8,128)S(1)} %bitcast.18), channel_id=1, source_target_pairs={{1,0},{0,1},{65,64},{64,65},{9,8},{8,9},{73,72},{72,73},{17,16},{1... | collective-permute-start | bytes 1544 | tf_op jit(solution)/shard_map/ppermute | solution.py:47
  115.0 18.8 %shard_map.49 = (bf16[512,128]{1,0:T(8,128)(2,1)}, bf16[512,128]{1,0:T(8,128)(2,1)}) custom-call(s32[8]{0:T(128)} %stack.84.refs_0_, bf16[512,16384]{1,0:T(8,128)(2,1)} %bitcast.21, bf16[512,16384]{1,0:T(8,128)(2,1)} %collective-permute-done.1.sib.refs_2_, bf16[2048,128]{1,0:T(8,128)(2,1)} %copy-done.6, bf16[2048,128]{1,0:T(8,128)(2,1)} %copy-done.7, ...), custom_call_target="tpu_custom_call" | custom-call | flops 4294967296 | bytes 38797312 | tf_op jit(solution)/shard_map/pallas_call | solution.py:113
  133.9 1.2 constant_dynamic-update-slice_fusion.8
  135.1 0.3 collective-permute-start.16
  135.4 10.5 %shard_map.46 = (f32[512,512]{1,0:T(8,128)S(1)}, f32[512,512]{1,0:T(8,128)S(1)}) custom-call(s32[3]{0:T(128)S(1)} %pad_add_fusion.2.blocks, bf16[512,16384]{1,0:T(8,128)(2,1)} %bitcast.22, bf16[512,16384]{1,0:T(8,128)(2,1)} %collective-permute-done.1.sib.refs_2_, bf16[2048,512]{1,0:T(8,128)(2,1)S(1)} %constant_dynamic-slice_fusion.1.refs_0_, ...), custom_call_target="tpu_custom_call" | custom-call | flops 6442450944 | bytes 23068672 | tf_op jit(solution)/shard_map/pallas_call | solution.py:165
  146.0 1.4 collective-permute-start.17
  147.4 1.4 collective-permute-start.18
  148.7 12.5 %shard_map.47 = (f32[512,512]{1,0:T(8,128)S(1)}, f32[512,512]{1,0:T(8,128)S(1)}) custom-call(s32[3]{0:T(128)S(1)} %pad_add_fusion.1.blocks, bf16[512,16384]{1,0:T(8,128)(2,1)} %bitcast.23, bf16[512,16384]{1,0:T(8,128)(2,1)} %collective-permute-done.1.sib.refs_2_, bf16[2048,512]{1,0:T(8,128)(2,1)} %collective-permute-done.7.refs_0_, ...), custom_call_target="tpu_custom_call" | custom-call | flops 6442450944 | bytes 23068672 | tf_op jit(solution)/shard_map/pallas_call | solution.py:165
  161.2 0.3 collective-permute-start.19
  161.5 9.6 %shard_map.48 = (f32[512,512]{1,0:T(8,128)S(1)}, f32[512,512]{1,0:T(8,128)S(1)}) custom-call(s32[2]{0:T(128)S(1)} %pad_add_fusion.blocks, bf16[512,16384]{1,0:T(8,128)(2,1)} %bitcast.24, bf16[512,16384]{1,0:T(8,128)(2,1)} %collective-permute-done.1.sib.refs_2_, bf16[2048,512]{1,0:T(8,128)(2,1)} %collective-permute-done.4.refs_0_, ...), custom_call_target="tpu_custom_call" | custom-call | flops 4294967296 | bytes 16777216 | tf_op jit(solution)/shard_map/pallas_call | solution.py:165
  171.1 3.3 %collective-permute-start.20 = (bf16[2048,128]{1,0:T(8,128)(2,1)S(1)}, bf16[2048,128]{1,0:T(8,128)(2,1)S(1)}, u32[]{:S(2)}, u32[]{:S(2)}) collective-permute-start(bf16[2048,128]{1,0:T(8,128)(2,1)S(1)} %pad_maximum_fusion), channel_id=1, source_target_pairs={{1,0},{0,1},{65,64},{64,65},{9,8},{8,9},{73,72},{72,73},{17,16},{1... | collective-permute-start | bytes 1572872 | tf_op jit(solution)/shard_map/ppermute | solution.py:47
  174.5 0.1 collective-permute-start.21
  174.6 0.1 constant_dynamic-update-slice_fusion.6
  174.7 0.6 collective-permute-start.23
  175.3 0.4 collective-permute-start.22
  175.6 0.1 constant_dynamic-update-slice_fusion.5
  175.7 0.1 constant_dynamic-update-slice_fusion.4
  175.8 0.2 collective-permute-done.20
  176.0 0.1 constant_dynamic-update-slice_fusion.3
  176.1 0.7 collective-permute-done.21
  176.8 0.1 constant_dynamic-update-slice_fusion.2
  176.8 1.4 collective-permute-done.22
  178.3 0.1 constant_dynamic-update-slice_fusion.1
  178.3 0.1 constant_dynamic-update-slice_fusion.kv
  178.4 8.6 %shard_map.50 = bf16[512,512]{1,0:T(8,128)(2,1)S(1)} custom-call(s32[8,16]{1,0:T(8,128)S(1)} %collective-permute-done.picks, s32[4]{0:T(128)S(1)} %add_add_fusion.where, f32[512,512]{1,0:T(8,128)S(1)} %get-tuple-element.19.raw, f32[512,128]{1,0:T(8,128)S(1)} %get-tuple-element.31.cosine, f32[512,128]{1,0:T(8,128)S(1)} %get-tuple-element.45.sine, ...), custom_call_target="tpu_custom_call" | custom-call | flops 1073741824 | bytes 6291456 | tf_op jit(solution)/shard_map/pallas_call | solution.py:242
  187.0 2.0 copy-done.2
  189.0 0.4 collective-permute-start.24
  189.3 0.1 add_add_fusion.1.where
  189.4 2.3 %copy-done.3 = bf16[16384,128]{1,0:T(8,128)(2,1)S(1)} copy-done((bf16[16384,128]{1,0:T(8,128)(2,1)S(1)}, bf16[16384,128]{1,0:T(8,128)(2,1)}, u32[]{:S(2)}) %copy-start.3) | copy-done | bytes 4194328
  191.7 8.5 %shard_map.51 = bf16[512,512]{1,0:T(8,128)(2,1)S(1)} custom-call(s32[8,16]{1,0:T(8,128)S(1)} %bitcast.19, s32[4]{0:T(128)S(1)} %add_add_fusion.1.where, f32[512,512]{1,0:T(8,128)S(1)} %get-tuple-element.24.raw, f32[512,128]{1,0:T(8,128)S(1)} %copy-done.4, f32[512,128]{1,0:T(8,128)S(1)} %get-tuple-element.30.sine, bf16[16384,128]{1,0:T(8,128)(2,1)S(1)} %copy-done.3), custom_call_target="tpu_custom_call" | custom-call | flops 1073741824 | bytes 6291456 | tf_op jit(solution)/shard_map/pallas_call | solution.py:242
  200.2 2.5 %maximum_select_fusion = bf16[1,512,1024]{2,1,0:T(8,128)(2,1)} fusion(bf16[1,512,512]{2,1,0:T(8,128)(2,1)S(1)} %bitcast.17, bf16[1,512,512]{2,1,0:T(8,128)(2,1)} %bitcast.14, pred[]{:T(512)S(6)} %eq.24), kind=kLoop, calls=%fused_computation | loop fusion | flops 4718592 | bytes 2097153 | tf_op jit(solution)/shard_map/jit(_where)/select_n | solution.py:338
  (41 shorter events, 0.2 us)
Async XLA Ops:
  0.0 4.6 %copy-start = (bf16[2048,256]{1,0:T(8,128)(2,1)S(1)}, bf16[2048,256]{1,0:T(8,128)(2,1)}, u32[]{:S(2)}) copy-start(bf16[2048,256]{1,0:T(8,128)(2,1)} %param.6) | copy-start | bytes 3145732
  0.0 109.0 %collective-permute-start.1 = (bf16[512,16384]{1,0:T(8,128)(2,1)}, bf16[512,16384]{1,0:T(8,128)(2,1)}, u32[]{:S(2)}, u32[]{:S(2)}) collective-permute-start(bf16[512,16384]{1,0:T(8,128)(2,1)} %bitcast.20), channel_id=1, source_target_pairs={{1,0},{0,1},{65,64},{64,65},{9,8},{8,9},{73,72},{72,73},{17,16},{1... | collective-permute-start | bytes 50331656 | tf_op jit(solution)/shard_map/ppermute | solution.py:47
  3.2 105.9 %copy-start.5 = (s32[1,8,16]{2,1,0:T(8,128)S(1)}, s32[1,8,16]{2,1,0:T(8,128)}, u32[]{:S(2)}) copy-start(s32[1,8,16]{2,1,0:T(8,128)} %param.7) | copy-start | bytes 1540
  3.2 33.9 %collective-permute-start.2 = (bf16[2048,512]{1,0:T(8,128)(2,1)S(1)}, bf16[2048,512]{1,0:T(8,128)(2,1)}, u32[]{:S(2)}, u32[]{:S(2)}) collective-permute-start(bf16[2048,512]{1,0:T(8,128)(2,1)S(1)} %constant_dynamic-slice_fusion.1.refs_0_), channel_id=1, source_target_pairs={{16,0},{49,1},{80,64},{113,65},{24,8},{57,9},{88,72},{121,73},{32,... | collective-permute-start | bytes 6291464 | tf_op jit(solution)/shard_map/ppermute | solution.py:47
  4.7 41.4 %copy-start.6 = (bf16[2048,128]{1,0:T(8,128)(2,1)}, bf16[2048,128]{1,0:T(8,128)(2,1)S(1)}, u32[]{:S(2)}) copy-start(bf16[2048,128]{1,0:T(8,128)(2,1)S(1)} %constant_dynamic-slice_fusion.refs_3_) | copy-start | bytes 1572868
  4.7 30.4 %collective-permute-start.9 = (bf16[2048,128]{1,0:T(8,128)(2,1)S(1)}, bf16[2048,128]{1,0:T(8,128)(2,1)S(1)}, u32[]{:S(2)}, u32[]{:S(2)}) collective-permute-start(bf16[2048,128]{1,0:T(8,128)(2,1)S(1)} %constant_dynamic-slice_fusion.refs_3_), channel_id=1, source_target_pairs={{16,0},{49,1},{80,64},{113,65},{24,8},{57,9},{88,72},{121,73},{32,... | collective-permute-start | bytes 1572872 | tf_op jit(solution)/shard_map/ppermute | solution.py:47
  6.0 32.7 %collective-permute-start.12 = (bf16[2048,128]{1,0:T(8,128)(2,1)S(1)}, bf16[2048,128]{1,0:T(8,128)(2,1)S(1)}, u32[]{:S(2)}, u32[]{:S(2)}) collective-permute-start(bf16[2048,128]{1,0:T(8,128)(2,1)S(1)} %constant_dynamic-slice_fusion.refs_3_), channel_id=1, source_target_pairs={{64,0},{73,1},{8,64},{1,65},{72,8},{65,9},{0,72},{9,73},{80,16},{8... | collective-permute-start | bytes 1572872 | tf_op jit(solution)/shard_map/ppermute | solution.py:47
  35.1 18.6 %copy-start.7 = (bf16[2048,128]{1,0:T(8,128)(2,1)}, bf16[2048,128]{1,0:T(8,128)(2,1)S(1)}, u32[]{:S(2)}) copy-start(bf16[2048,128]{1,0:T(8,128)(2,1)S(1)} %collective-permute-done.9.refs_4_) | copy-start | bytes 1572868
  35.1 9.2 %collective-permute-start.10 = (bf16[2048,128]{1,0:T(8,128)(2,1)S(1)}, bf16[2048,128]{1,0:T(8,128)(2,1)S(1)}, u32[]{:S(2)}, u32[]{:S(2)}) collective-permute-start(bf16[2048,128]{1,0:T(8,128)(2,1)S(1)} %collective-permute-done.9.refs_4_), channel_id=1, source_target_pairs={{16,0},{49,1},{80,64},{113,65},{24,8},{57,9},{88,72},{121,73},{32,... | collective-permute-start | bytes 1572872 | tf_op jit(solution)/shard_map/ppermute | solution.py:47
  35.4 10.3 %collective-permute-start.13 = (bf16[2048,128]{1,0:T(8,128)(2,1)S(1)}, bf16[2048,128]{1,0:T(8,128)(2,1)S(1)}, u32[]{:S(2)}, u32[]{:S(2)}) collective-permute-start(bf16[2048,128]{1,0:T(8,128)(2,1)S(1)} %collective-permute-done.9.refs_4_), channel_id=1, source_target_pairs={{64,0},{73,1},{8,64},{1,65},{72,8},{65,9},{0,72},{9,73},{80,16},{8... | collective-permute-start | bytes 1572872 | tf_op jit(solution)/shard_map/ppermute | solution.py:47
  37.1 70.2 %collective-permute-start.3 = (bf16[2048,512]{1,0:T(8,128)(2,1)}, bf16[2048,512]{1,0:T(8,128)(2,1)}, u32[]{:S(2)}, u32[]{:S(2)}) collective-permute-start(bf16[2048,512]{1,0:T(8,128)(2,1)} %collective-permute-done.2.refs_1_), channel_id=1, source_target_pairs={{64,0},{73,1},{8,64},{1,65},{72,8},{65,9},{0,72},{9,73},{80,16},{8... | collective-permute-start | bytes 6291464 | tf_op jit(solution)/shard_map/ppermute | solution.py:47
  38.7 15.0 %copy-start.8 = (bf16[2048,128]{1,0:T(8,128)(2,1)}, bf16[2048,128]{1,0:T(8,128)(2,1)S(1)}, u32[]{:S(2)}) copy-start(bf16[2048,128]{1,0:T(8,128)(2,1)S(1)} %collective-permute-done.12.refs_7_) | copy-start | bytes 1572868
  38.7 69.5 %collective-permute-start.5 = (bf16[2048,512]{1,0:T(8,128)(2,1)}, bf16[2048,512]{1,0:T(8,128)(2,1)}, u32[]{:S(2)}, u32[]{:S(2)}) collective-permute-start(bf16[2048,512]{1,0:T(8,128)(2,1)} %collective-permute-done.2.refs_1_), channel_id=1, source_target_pairs={{2,0},{7,1},{66,64},{71,65},{10,8},{15,9},{74,72},{79,73},{18,16},... | collective-permute-start | bytes 6291464 | tf_op jit(solution)/shard_map/ppermute | solution.py:47
  44.3 61.9 %copy-start.9 = (bf16[2048,128]{1,0:T(8,128)(2,1)}, bf16[2048,128]{1,0:T(8,128)(2,1)S(1)}, u32[]{:S(2)}) copy-start(bf16[2048,128]{1,0:T(8,128)(2,1)S(1)} %collective-permute-done.10.refs_5_) | copy-start | bytes 1572868
  44.3 9.3 %collective-permute-start.11 = (bf16[2048,128]{1,0:T(8,128)(2,1)S(1)}, bf16[2048,128]{1,0:T(8,128)(2,1)}, u32[]{:S(2)}, u32[]{:S(2)}) collective-permute-start(bf16[2048,128]{1,0:T(8,128)(2,1)S(1)} %collective-permute-done.10.refs_5_), channel_id=1, source_target_pairs={{16,0},{49,1},{80,64},{113,65},{24,8},{57,9},{88,72},{121,73},{32,... | collective-permute-start | bytes 1572872 | tf_op jit(solution)/shard_map/ppermute | solution.py:47
  45.7 28.2 %copy-start.10 = (bf16[2048,128]{1,0:T(8,128)(2,1)}, bf16[2048,128]{1,0:T(8,128)(2,1)S(1)}, u32[]{:S(2)}) copy-start(bf16[2048,128]{1,0:T(8,128)(2,1)S(1)} %collective-permute-done.13.refs_8_) | copy-start | bytes 1572868
  45.7 28.2 %collective-permute-start.14 = (bf16[2048,128]{1,0:T(8,128)(2,1)S(1)}, bf16[2048,128]{1,0:T(8,128)(2,1)}, u32[]{:S(2)}, u32[]{:S(2)}) collective-permute-start(bf16[2048,128]{1,0:T(8,128)(2,1)S(1)} %collective-permute-done.10.refs_5_), channel_id=1, source_target_pairs={{64,0},{73,1},{8,64},{1,65},{72,8},{65,9},{0,72},{9,73},{80,16},{8... | collective-permute-start | bytes 1572872 | tf_op jit(solution)/shard_map/ppermute | solution.py:47
  53.7 81.4 %collective-permute-start.8 = (bf16[2048,512]{1,0:T(8,128)(2,1)S(1)}, bf16[2048,512]{1,0:T(8,128)(2,1)}, u32[]{:S(2)}, u32[]{:S(2)}) collective-permute-start(bf16[2048,512]{1,0:T(8,128)(2,1)S(1)} %constant_dynamic-slice_fusion.1.refs_0_), channel_id=1, source_target_pairs={{64,0},{73,1},{8,64},{1,65},{72,8},{65,9},{0,72},{9,73},{80,16},{8... | collective-permute-start | bytes 6291464 | tf_op jit(solution)/shard_map/ppermute | solution.py:47
  73.9 28.0 %collective-permute-start.15 = (bf16[2048,128]{1,0:T(8,128)(2,1)}, bf16[2048,128]{1,0:T(8,128)(2,1)S(1)}, u32[]{:S(2)}, u32[]{:S(2)}) collective-permute-start(bf16[2048,128]{1,0:T(8,128)(2,1)} %collective-permute-done.11.refs_6_), channel_id=1, source_target_pairs={{64,0},{73,1},{8,64},{1,65},{72,8},{65,9},{0,72},{9,73},{80,16},{8... | collective-permute-start | bytes 1572872 | tf_op jit(solution)/shard_map/ppermute | solution.py:47
  101.9 3.2 %copy-start.11 = (bf16[2048,128]{1,0:T(8,128)(2,1)}, bf16[2048,128]{1,0:T(8,128)(2,1)S(1)}, u32[]{:S(2)}) copy-start(bf16[2048,128]{1,0:T(8,128)(2,1)S(1)} %collective-permute-done.15.refs_10_) | copy-start | bytes 1572868
  101.9 45.5 %collective-permute-start.7 = (bf16[2048,512]{1,0:T(8,128)(2,1)}, bf16[2048,512]{1,0:T(8,128)(2,1)}, u32[]{:S(2)}, u32[]{:S(2)}) collective-permute-start(bf16[2048,512]{1,0:T(8,128)(2,1)} %collective-permute-done.2.refs_1_), channel_id=1, source_target_pairs={{16,0},{49,1},{80,64},{113,65},{24,8},{57,9},{88,72},{121,73},{32,... | collective-permute-start | bytes 6291464 | tf_op jit(solution)/shard_map/ppermute | solution.py:47
  107.2 54.3 %collective-permute-start.4 = (bf16[2048,512]{1,0:T(8,128)(2,1)}, bf16[2048,512]{1,0:T(8,128)(2,1)}, u32[]{:S(2)}, u32[]{:S(2)}) collective-permute-start(bf16[2048,512]{1,0:T(8,128)(2,1)} %collective-permute-done.3.refs_2_), channel_id=1, source_target_pairs={{16,0},{49,1},{80,64},{113,65},{24,8},{57,9},{88,72},{121,73},{32,... | collective-permute-start | bytes 6291464 | tf_op jit(solution)/shard_map/ppermute | solution.py:47
  108.2 53.3 %collective-permute-start.6 = (bf16[2048,512]{1,0:T(8,128)(2,1)}, bf16[2048,512]{1,0:T(8,128)(2,1)}, u32[]{:S(2)}, u32[]{:S(2)}) collective-permute-start(bf16[2048,512]{1,0:T(8,128)(2,1)} %collective-permute-done.5.refs_1_), channel_id=1, source_target_pairs={{64,0},{73,1},{8,64},{1,65},{72,8},{65,9},{0,72},{9,73},{80,16},{8... | collective-permute-start | bytes 6291464 | tf_op jit(solution)/shard_map/ppermute | solution.py:47
  109.0 69.4 %collective-permute-start = (s32[8,16]{1,0:T(8,128)S(1)}, s32[8,16]{1,0:T(8,128)S(1)}, u32[]{:S(2)}, u32[]{:S(2)}) collective-permute-start(s32[8,16]{1,0:T(8,128)S(1)} %bitcast.18), channel_id=1, source_target_pairs={{1,0},{0,1},{65,64},{64,65},{9,8},{8,9},{73,72},{72,73},{17,16},{1... | collective-permute-start | bytes 1544 | tf_op jit(solution)/shard_map/ppermute | solution.py:47
  135.1 10.9 %collective-permute-start.16 = (bf16[1024,128]{1,0:T(8,128)(2,1)S(1)}, bf16[1024,128]{1,0:T(8,128)(2,1)S(1)}, u32[]{:S(2)}, u32[]{:S(2)}) collective-permute-start(bf16[1024,128]{1,0:T(8,128)(2,1)S(1)} %get-tuple-element.26), channel_id=1, source_target_pairs={{8,0},{9,1},{72,64},{73,65},{0,8},{1,9},{64,72},{65,73},{24,16},{2... | collective-permute-start | bytes 786440 | tf_op jit(solution)/shard_map/ppermute | solution.py:47
  146.0 15.3 %collective-permute-start.17 = (bf16[2048,128]{1,0:T(8,128)(2,1)S(1)}, bf16[2048,128]{1,0:T(8,128)(2,1)S(1)}, u32[]{:S(2)}, u32[]{:S(2)}) collective-permute-start(bf16[2048,128]{1,0:T(8,128)(2,1)S(1)} %pad_maximum_fusion), channel_id=1, source_target_pairs={{2,0},{7,1},{66,64},{71,65},{10,8},{15,9},{74,72},{79,73},{18,16},... | collective-permute-start | bytes 1572872 | tf_op jit(solution)/shard_map/ppermute | solution.py:47
  147.4 13.9 %collective-permute-start.18 = (bf16[2048,128]{1,0:T(8,128)(2,1)S(1)}, bf16[2048,128]{1,0:T(8,128)(2,1)S(1)}, u32[]{:S(2)}, u32[]{:S(2)}) collective-permute-start(bf16[2048,128]{1,0:T(8,128)(2,1)S(1)} %pad_maximum_fusion), channel_id=1, source_target_pairs={{6,0},{3,1},{70,64},{67,65},{14,8},{11,9},{78,72},{75,73},{22,16},... | collective-permute-start | bytes 1572872 | tf_op jit(solution)/shard_map/ppermute | solution.py:47
  161.2 14.0 %collective-permute-start.19 = (bf16[2048,128]{1,0:T(8,128)(2,1)S(1)}, bf16[2048,128]{1,0:T(8,128)(2,1)S(1)}, u32[]{:S(2)}, u32[]{:S(2)}) collective-permute-start(bf16[2048,128]{1,0:T(8,128)(2,1)S(1)} %collective-permute-done.17), channel_id=1, source_target_pairs={{2,0},{7,1},{66,64},{71,65},{10,8},{15,9},{74,72},{79,73},{18,16},... | collective-permute-start | bytes 1572872 | tf_op jit(solution)/shard_map/ppermute | solution.py:47
  171.1 4.9 %collective-permute-start.20 = (bf16[2048,128]{1,0:T(8,128)(2,1)S(1)}, bf16[2048,128]{1,0:T(8,128)(2,1)S(1)}, u32[]{:S(2)}, u32[]{:S(2)}) collective-permute-start(bf16[2048,128]{1,0:T(8,128)(2,1)S(1)} %pad_maximum_fusion), channel_id=1, source_target_pairs={{1,0},{0,1},{65,64},{64,65},{9,8},{8,9},{73,72},{72,73},{17,16},{1... | collective-permute-start | bytes 1572872 | tf_op jit(solution)/shard_map/ppermute | solution.py:47
  174.5 2.2 %collective-permute-start.21 = (bf16[2048,128]{1,0:T(8,128)(2,1)S(1)}, bf16[2048,128]{1,0:T(8,128)(2,1)S(1)}, u32[]{:S(2)}, u32[]{:S(2)}) collective-permute-start(bf16[2048,128]{1,0:T(8,128)(2,1)S(1)} %collective-permute-done.17), channel_id=1, source_target_pairs={{1,0},{0,1},{65,64},{64,65},{9,8},{8,9},{73,72},{72,73},{17,16},{1... | collective-permute-start | bytes 1572872 | tf_op jit(solution)/shard_map/ppermute | solution.py:47
  174.7 3.7 %collective-permute-start.23 = (bf16[2048,128]{1,0:T(8,128)(2,1)S(1)}, bf16[2048,128]{1,0:T(8,128)(2,1)S(1)}, u32[]{:S(2)}, u32[]{:S(2)}) collective-permute-start(bf16[2048,128]{1,0:T(8,128)(2,1)S(1)} %collective-permute-done.18), channel_id=1, source_target_pairs={{1,0},{0,1},{65,64},{64,65},{9,8},{8,9},{73,72},{72,73},{17,16},{1... | collective-permute-start | bytes 1572872 | tf_op jit(solution)/shard_map/ppermute | solution.py:47
  175.3 3.0 %collective-permute-start.22 = (bf16[2048,128]{1,0:T(8,128)(2,1)S(1)}, bf16[2048,128]{1,0:T(8,128)(2,1)S(1)}, u32[]{:S(2)}, u32[]{:S(2)}) collective-permute-start(bf16[2048,128]{1,0:T(8,128)(2,1)S(1)} %collective-permute-done.19), channel_id=1, source_target_pairs={{1,0},{0,1},{65,64},{64,65},{9,8},{8,9},{73,72},{72,73},{17,16},{1... | collective-permute-start | bytes 1572872 | tf_op jit(solution)/shard_map/ppermute | solution.py:47
  176.8 12.6 %copy-start.4 = (f32[512,128]{1,0:T(8,128)S(1)}, f32[512,128]{1,0:T(8,128)}, u32[]{:S(2)}) copy-start(f32[512,128]{1,0:T(8,128)} %get-tuple-element.46.cosine) | copy-start | bytes 786436
  187.0 2.0 copy-start.2
  189.0 11.3 %collective-permute-start.24 = (bf16[512,512]{1,0:T(8,128)(2,1)S(1)}, bf16[512,512]{1,0:T(8,128)(2,1)}, u32[]{:S(2)}, u32[]{:S(2)}) collective-permute-start(bf16[512,512]{1,0:T(8,128)(2,1)S(1)} %shard_map.50), channel_id=1, source_target_pairs={{1,0},{0,1},{65,64},{64,65},{9,8},{8,9},{73,72},{72,73},{17,16},{1... | collective-permute-start | bytes 1572872 | tf_op jit(solution)/shard_map/ppermute | solution.py:47
  189.4 13.3 %copy-start.1 = (bf16[2048,256]{1,0:T(8,128)(2,1)S(1)}, bf16[2048,256]{1,0:T(8,128)(2,1)}, u32[]{:S(2)}) copy-start(bf16[2048,256]{1,0:T(8,128)(2,1)} %param.6) | copy-start | bytes 3145732
  189.4 2.3 %copy-start.3 = (bf16[16384,128]{1,0:T(8,128)(2,1)S(1)}, bf16[16384,128]{1,0:T(8,128)(2,1)}, u32[]{:S(2)}) copy-start(bf16[16384,128]{1,0:T(8,128)(2,1)} %copy-done.2) | copy-start | bytes 12582916

commit v3 on v2

--- a/solution.py
+++ b/solution.py
@@ -284,22 +284,15 @@
     kv_a0 = lax.dynamic_slice(kv_weight, (0, c * HD), (shard, HD))
     sib = get(own, FROM_CORE)
     sib_picks = get(picks[0], FROM_CORE)
-    kv_a1 = get(kv_a0, FROM_Y)
-    kv_b0 = get(kv_a0, FROM_Z)
-    kv_a2 = get(kv_a1, FROM_Y)
-    kv_b1 = get(kv_a1, FROM_Z)
-    kv_a3 = get(kv_a2, FROM_Y)
-    kv_b2 = get(kv_a2, FROM_Z)
-    kv_b3 = get(kv_a3, FROM_Z)
-
     a0 = lax.dynamic_slice(query_weight, (0, c * width), (shard, width))
+    kv_a1, kv_b0 = get(kv_a0, FROM_Y), get(kv_a0, FROM_Z)
+    kv_a1, kv_b0 = fence((kv_a1, kv_b0))
+    kv_a2, kv_b1, kv_a3 = get(kv_a1, FROM_Y), get(kv_a1, FROM_Z), get(kv_a1, FROM_PAIR)
+    kv_a2, kv_b1, kv_a3, a0 = fence((kv_a2, kv_b1, kv_a3, a0))
     a1 = get(a0, FROM_Y)
+    kv_b2, kv_b3 = get(kv_a2, FROM_Z), get(kv_b1, FROM_PAIR)
+    kv_b2, kv_b3, sib, a0 = fence((kv_b2, kv_b3, sib, a0))
     b0 = get(a0, FROM_Z)
-    a2 = get(a1, FROM_Y)
-    b1 = get(a1, FROM_Z)
-    a3 = get(a1, FROM_PAIR)
-    b2 = get(b1, FROM_Y)
-    b3 = get(a3, FROM_Z)
 
     cos_own, sin_own = tables_of(seq * rows, rows)
     cos_sib, sin_sib = tables_of((seq + step) * rows, rows)
@@ -318,13 +311,20 @@
         jnp.concatenate([kv_sib, kv_own], 0),
         jnp.concatenate([kv_own, kv_sib], 0),
     )
+    here, a1, b0 = fence((here, a1, b0))
+    a2 = get(a1, FROM_Y)
+    b1 = get(a1, FROM_Z)
+    a3 = get(a1, FROM_PAIR)
     near = jnp.concatenate([here, get(here, FROM_Z2)], 0)
-    ahead, back = fence((get(near, FROM_X), get(near, FROM_X_BACK)))
+    acc = project_query(blocks((0, 0), (1, 0), (0, 1)), own, sib, [a0, a1, b0])
+    near, a2, b1, a3, acc = fence((near, a2, b1, a3, acc))
+    ahead, back = get(near, FROM_X), get(near, FROM_X_BACK)
+    b2 = get(b1, FROM_Y)
+    b3 = get(a3, FROM_Z)
+    acc = project_query(blocks((2, 0), (3, 0), (1, 1)), own, sib, [a2, a3, b1], acc)
+    ahead, back, *acc = fence((ahead, back, *acc))
     chunks = [near, ahead, get(ahead, FROM_X), back]
     kv = jnp.concatenate(chunks + [get(chunk, FROM_CORE) for chunk in chunks], 0)
-
-    acc = project_query(blocks((0, 0), (1, 0), (0, 1)), own, sib, [a0, a1, b0])
-    acc = project_query(blocks((2, 0), (3, 0), (1, 1)), own, sib, [a2, a3, b1], acc)
     acc = project_query(blocks((2, 1), (3, 1)), own, sib, [b2, b3], acc)
 
     blocks_here = rows // BLK

time: 203 us -> 164 us (0.81)
  waiting for transfers between devices: 86 us -> 47.3 us
    ppermute x25, waiting for transfers between devices: 86 us -> 47.3 us  [get(): return lax.ppermute(value, AXES, perm)]
    unnamed x31 -> x29, local copies, waits for them, and re-layouts: 4.73 us -> 3.77 us
  transfers between devices with their start and end apart: 25 -> 25, of which waited for: 9 -> 12; matrix products, arithmetic and copies ran while one was open for 4% -> 6% of each run, Pallas kernels for 30% -> 36%
where the time goes in v3:
time: 164 us
  Pallas kernels  68.4 us (42%)
  waiting for transfers between devices  47.3 us (29%)
  starting transfers between devices  32.2 us (20%)
  other arithmetic  9.5 us (6%)
  local copies, waits for them, and re-layouts  6.26 us (4%)
    ppermute x25, waiting for transfers between devices, get(): return lax.ppermute(value, AXES, perm)  47.3 us
    ppermute x25, starting transfers between devices, get(): return lax.ppermute(value, AXES, perm)  32.2 us
    pallas_call x3, Pallas kernels, project_query(): pl.pallas_call(functools.partial(query_kernel, n, not acc), grid_spec=plt...  31.7 us
    pallas_call x1, Pallas kernels, project(): pl.pallas_call(functools.partial(project_kernel, n, first, last), grid_sp...  18.8 us
    pallas_call x2, Pallas kernels, attend(): pl.pallas_call(functools.partial(attend_kernel, nblk, heads), in_specs=[s...  17.9 us
    unnamed x29, local copies, waits for them, and re-layouts  3.77 us
  transfers between devices with their start and end apart: 25, of which 12 were waited for; matrix products, arithmetic and copies ran while one was open for 6% of the time, Pallas kernels for 36%

profile of v3, /device:TPU:1, one launch (start us, length us, event | category | flops | bytes accessed | tf_op | source)
XLA Modules:
  0.0 164.0 jit_solution(18361749932360395845)
XLA Ops:
  0.0 1.4 collective-permute-start.8
  1.5 0.0 copy-start.5
  1.5 2.3 %collective-permute-start.2 = (bf16[2048,128]{1,0:T(8,128)(2,1)S(1)}, bf16[2048,128]{1,0:T(8,128)(2,1)S(1)}, u32[]{:S(2)}, u32[]{:S(2)}) collective-permute-start(bf16[2048,128]{1,0:T(8,128)(2,1)S(1)} %constant_dynamic-slice_fusion.1.refs_3_), channel_id=1, source_target_pairs={{64,0},{73,1},{8,64},{1,65},{72,8},{65,9},{0,72},{9,73},{80,16},{8... | collective-permute-start | bytes 1572872 | tf_op jit(solution)/shard_map/ppermute | solution.py:47
  3.8 1.3 collective-permute-start.1
  5.1 7.4 %collective-permute-done.2.refs_7_ = bf16[2048,128]{1,0:T(8,128)(2,1)S(1)} collective-permute-done((bf16[2048,128]{1,0:T(8,128)(2,1)S(1)}, bf16[2048,128]{1,0:T(8,128)(2,1)S(1)}, u32[]{:S(2)}, u32[]{:S(2)}) %collective-permute-start.2) | collective-permute-done | bytes 524320 | tf_op jit(solution)/shard_map/ppermute | solution.py:47
  12.5 0.6 collective-permute-done.1.refs_4_
  13.1 0.2 copy-done.6
  13.3 2.8 %collective-permute-start.5 = (bf16[2048,128]{1,0:T(8,128)(2,1)S(1)}, bf16[2048,128]{1,0:T(8,128)(2,1)S(1)}, u32[]{:S(2)}, u32[]{:S(2)}) collective-permute-start(bf16[2048,128]{1,0:T(8,128)(2,1)S(1)} %collective-permute-done.1.refs_4_), channel_id=1, source_target_pairs={{2,0},{7,1},{66,64},{71,65},{10,8},{15,9},{74,72},{79,73},{18,16},... | collective-permute-start | bytes 1572872 | tf_op jit(solution)/shard_map/ppermute | solution.py:47
  16.1 0.7 collective-permute-start.4
  16.8 0.8 collective-permute-start.3
  17.6 1.7 %constant_dynamic-slice_fusion.refs_0_ = bf16[2048,512]{1,0:T(8,128)(2,1)S(1)} fusion(bf16[2048,1024]{1,0:T(8,128)(2,1)} %param.5, s32[]{:T(128)S(6)} %select_n.129), kind=kLoop, calls=%fused_computation.33 | loop fusion | bytes 4194308 | tf_op jit(solution)/shard_map/dynamic_slice | solution.py:287
  19.3 3.4 %collective-permute-done.5.refs_6_ = bf16[2048,128]{1,0:T(8,128)(2,1)S(1)} collective-permute-done((bf16[2048,128]{1,0:T(8,128)(2,1)S(1)}, bf16[2048,128]{1,0:T(8,128)(2,1)S(1)}, u32[]{:S(2)}, u32[]{:S(2)}) %collective-permute-start.5) | collective-permute-done | bytes 524320 | tf_op jit(solution)/shard_map/ppermute | solution.py:47
  22.6 2.8 %collective-permute-done.4.refs_8_ = bf16[2048,128]{1,0:T(8,128)(2,1)} collective-permute-done((bf16[2048,128]{1,0:T(8,128)(2,1)S(1)}, bf16[2048,128]{1,0:T(8,128)(2,1)}, u32[]{:S(2)}, u32[]{:S(2)}) %collective-permute-start.4) | collective-permute-done | bytes 524320 | tf_op jit(solution)/shard_map/ppermute | solution.py:47
  25.4 1.2 collective-permute-done.3.refs_5_
  26.6 1.3 collective-permute-start.6
  27.9 8.1 %collective-permute-done.6.refs_9_ = bf16[2048,128]{1,0:T(8,128)(2,1)S(1)} collective-permute-done((bf16[2048,128]{1,0:T(8,128)(2,1)}, bf16[2048,128]{1,0:T(8,128)(2,1)S(1)}, u32[]{:S(2)}, u32[]{:S(2)}) %collective-permute-start.6) | collective-permute-done | bytes 524320 | tf_op jit(solution)/shard_map/ppermute | solution.py:47
  36.0 1.3 collective-permute-done.7.refs_10_
  37.4 0.0 collective-permute-done.8.refs_2_.sib
  37.4 0.8 copy-done.10
  38.2 1.0 collective-permute-start.10
  39.2 0.7 stack.82.refs_0_
  39.9 1.9 %fusion.1 = (f32[512,64]{1,0:T(8,128)S(1)}, f32[512,64]{1,0:T(8,128)S(1)}, f32[512,64]{1,0:T(8,128)S(1)}, f32[512,64]{1,0:T(8,128)S(1)}, f32[512,64]{1,0:T(8,128)S(1)}, /*index=5*/f32[512,64]{1,0:T(8,128)S(1)}) fusion(f32[64]{0:T(128)S(1)} %negate_power_fusion, f32[512]{0:T(512)S(1)} %get-tuple-element.84, f32[512]{0:T(512)S(1)} %get-tuple-element.85), kind=kLoop, calls=%fused_computation.16 | loop fusion | flops 131072 | bytes 790784 | tf_op jit(solution)/shard_map/neg | solution.py:265
  41.8 0.9 pad_maximum_fusion.3
  42.7 0.9 pad_maximum_fusion.1
  43.6 0.9 broadcast_select_fusion
  44.4 0.9 broadcast_select_fusion.1
  45.3 18.8 %shard_map.46 = (bf16[512,128]{1,0:T(8,128)(2,1)}, bf16[512,128]{1,0:T(8,128)(2,1)}) custom-call(s32[8]{0:T(128)} %stack.82.refs_0_, bf16[512,16384]{1,0:T(8,128)(2,1)} %bitcast.21, bf16[512,16384]{1,0:T(8,128)(2,1)} %collective-permute-done.8.refs_2_.sib, bf16[2048,128]{1,0:T(8,128)(2,1)} %copy-done.5, bf16[2048,128]{1,0:T(8,128)(2,1)} %copy-done.7, ...), custom_call_target="tpu_custom_call" | custom-call | flops 4294967296 | bytes 38797312 | tf_op jit(solution)/shard_map/pallas_call | solution.py:113
  64.1 1.2 maximum_select_fusion.1
  65.3 0.1 collective-permute-start.14
  65.4 0.7 collective-permute-start.13
  66.1 0.1 pad_add_fusion.2.blocks
  66.2 0.1 pad_add_fusion.1.blocks
  66.2 0.1 pad_add_fusion.blocks
  66.3 2.5 %collective-permute-start.11 = (bf16[1024,128]{1,0:T(8,128)(2,1)S(1)}, bf16[1024,128]{1,0:T(8,128)(2,1)S(1)}, u32[]{:S(2)}, u32[]{:S(2)}) collective-permute-start(bf16[1024,128]{1,0:T(8,128)(2,1)S(1)} %maximum_select_fusion.1), channel_id=1, source_target_pairs={{8,0},{9,1},{72,64},{73,65},{0,8},{1,9},{64,72},{65,73},{24,16},{2... | collective-permute-start | bytes 786440 | tf_op jit(solution)/shard_map/ppermute | solution.py:47
  68.9 10.5 %shard_map.47 = (f32[512,512]{1,0:T(8,128)S(1)}, f32[512,512]{1,0:T(8,128)S(1)}) custom-call(s32[3]{0:T(128)S(1)} %pad_add_fusion.1.blocks, bf16[512,16384]{1,0:T(8,128)(2,1)} %bitcast.22, bf16[512,16384]{1,0:T(8,128)(2,1)} %collective-permute-done.8.refs_2_.sib, bf16[2048,512]{1,0:T(8,128)(2,1)S(1)} %constant_dynamic-slice_fusion.refs_0_, ...), custom_call_target="tpu_custom_call" | custom-call | flops 6442450944 | bytes 23068672 | tf_op jit(solution)/shard_map/pallas_call | solution.py:165
  79.4 18.5 %collective-permute-done.11 = bf16[1024,128]{1,0:T(8,128)(2,1)S(1)} collective-permute-done((bf16[1024,128]{1,0:T(8,128)(2,1)S(1)}, bf16[1024,128]{1,0:T(8,128)(2,1)S(1)}, u32[]{:S(2)}, u32[]{:S(2)}) %collective-permute-start.11) | collective-permute-done | bytes 262176 | tf_op jit(solution)/shard_map/ppermute | solution.py:47
  97.9 2.3 %collective-permute-start.18 = (bf16[2048,128]{1,0:T(8,128)(2,1)S(1)}, bf16[2048,128]{1,0:T(8,128)(2,1)S(1)}, u32[]{:S(2)}, u32[]{:S(2)}) collective-permute-start(bf16[2048,128]{1,0:T(8,128)(2,1)S(1)} %pad_maximum_fusion), channel_id=1, source_target_pairs={{6,0},{3,1},{70,64},{67,65},{14,8},{11,9},{78,72},{75,73},{22,16},... | collective-permute-start | bytes 1572872 | tf_op jit(solution)/shard_map/ppermute | solution.py:47
  100.3 12.5 %shard_map.48 = (f32[512,512]{1,0:T(8,128)S(1)}, f32[512,512]{1,0:T(8,128)S(1)}) custom-call(s32[3]{0:T(128)S(1)} %pad_add_fusion.2.blocks, bf16[512,16384]{1,0:T(8,128)(2,1)} %bitcast.23, bf16[512,16384]{1,0:T(8,128)(2,1)} %collective-permute-done.8.refs_2_.sib, bf16[2048,512]{1,0:T(8,128)(2,1)} %collective-permute-done.12.refs_0_, ...), custom_call_target="tpu_custom_call" | custom-call | flops 6442450944 | bytes 23068672 | tf_op jit(solution)/shard_map/pallas_call | solution.py:165
  112.8 0.0 copy-start.4
  112.8 0.1 collective-permute-done.17
  112.9 1.5 collective-permute-start.19
  114.4 0.1 add_add_fusion.where
  114.5 6.6 %collective-permute-start.20 = (bf16[2048,128]{1,0:T(8,128)(2,1)S(1)}, bf16[2048,128]{1,0:T(8,128)(2,1)S(1)}, u32[]{:S(2)}, u32[]{:S(2)}) collective-permute-start(bf16[2048,128]{1,0:T(8,128)(2,1)S(1)} %pad_maximum_fusion), channel_id=1, source_target_pairs={{1,0},{0,1},{65,64},{64,65},{9,8},{8,9},{73,72},{72,73},{17,16},{1... | collective-permute-start | bytes 1572872 | tf_op jit(solution)/shard_map/ppermute | solution.py:47
  121.1 0.1 collective-permute-start.21
  121.2 0.1 constant_dynamic-update-slice_fusion.6
  121.3 3.0 %collective-permute-done.19 = bf16[2048,128]{1,0:T(8,128)(2,1)S(1)} collective-permute-done((bf16[2048,128]{1,0:T(8,128)(2,1)S(1)}, bf16[2048,128]{1,0:T(8,128)(2,1)S(1)}, u32[]{:S(2)}, u32[]{:S(2)}) %collective-permute-start.19) | collective-permute-done | bytes 524320 | tf_op jit(solution)/shard_map/ppermute | solution.py:47
  124.3 5.4 %collective-permute-start.22 = (bf16[2048,128]{1,0:T(8,128)(2,1)S(1)}, bf16[2048,128]{1,0:T(8,128)(2,1)S(1)}, u32[]{:S(2)}, u32[]{:S(2)}) collective-permute-start(bf16[2048,128]{1,0:T(8,128)(2,1)S(1)} %collective-permute-done.19), channel_id=1, source_target_pairs={{1,0},{0,1},{65,64},{64,65},{9,8},{8,9},{73,72},{72,73},{17,16},{1... | collective-permute-start | bytes 1572872 | tf_op jit(solution)/shard_map/ppermute | solution.py:47
  129.7 0.1 constant_dynamic-update-slice_fusion.5
  129.7 0.1 constant_dynamic-update-slice_fusion.4
  129.8 0.1 collective-permute-start.23
  129.9 0.1 constant_dynamic-update-slice_fusion.3
  130.0 0.8 collective-permute-start
  130.8 0.1 constant_dynamic-update-slice_fusion.2
  130.9 0.3 collective-permute-done.22
  131.2 0.1 constant_dynamic-update-slice_fusion.1
  131.3 0.7 collective-permute-done.23
  131.9 0.1 constant_dynamic-update-slice_fusion.kv
  132.0 8.7 %shard_map.49 = (f32[512,512]{1,0:T(8,128)S(1)}, f32[512,512]{1,0:T(8,128)S(1)}) custom-call(s32[2]{0:T(128)S(1)} %pad_add_fusion.blocks, bf16[512,16384]{1,0:T(8,128)(2,1)} %bitcast.24, bf16[512,16384]{1,0:T(8,128)(2,1)} %collective-permute-done.8.refs_2_.sib, bf16[2048,512]{1,0:T(8,128)(2,1)S(1)} %collective-permute-done.15.refs_0_, ...), custom_call_target="tpu_custom_call" | custom-call | flops 4294967296 | bytes 16777216 | tf_op jit(solution)/shard_map/pallas_call | solution.py:165
  140.8 9.4 %shard_map.50 = bf16[512,512]{1,0:T(8,128)(2,1)} custom-call(s32[8,16]{1,0:T(8,128)S(1)} %collective-permute-done.picks, s32[4]{0:T(128)S(1)} %add_add_fusion.where, f32[512,512]{1,0:T(8,128)S(1)} %get-tuple-element.63.raw, f32[512,128]{1,0:T(8,128)S(1)} %get-tuple-element.71.cosine, f32[512,128]{1,0:T(8,128)S(1)} %get-tuple-element.68.sine, ...), custom_call_target="tpu_custom_call" | custom-call | flops 1073741824 | bytes 6291456 | tf_op jit(solution)/shard_map/pallas_call | solution.py:242
  150.1 0.4 collective-permute-start.24
  150.5 0.1 add_add_fusion.1.where
  150.6 2.3 %copy-done.3 = bf16[16384,128]{1,0:T(8,128)(2,1)S(1)} copy-done((bf16[16384,128]{1,0:T(8,128)(2,1)S(1)}, bf16[16384,128]{1,0:T(8,128)(2,1)}, u32[]{:S(2)}) %copy-start.3) | copy-done | bytes 4194328
  152.9 8.5 %shard_map.51 = bf16[512,512]{1,0:T(8,128)(2,1)S(1)} custom-call(s32[8,16]{1,0:T(8,128)S(1)} %bitcast.19, s32[4]{0:T(128)S(1)} %add_add_fusion.1.where, f32[512,512]{1,0:T(8,128)S(1)} %get-tuple-element.66.raw, f32[512,128]{1,0:T(8,128)S(1)} %get-tuple-element.73.cosine, f32[512,128]{1,0:T(8,128)S(1)} %get-tuple-element.70.sine, bf16[16384,128]{1,0:T(8,128)(2,1)S(1)} %copy-done.3), custom_call_target="tpu_custom_call" | custom-call | flops 1073741824 | bytes 6291456 | tf_op jit(solution)/shard_map/pallas_call | solution.py:242
  161.4 2.6 %maximum_select_fusion = bf16[1,512,1024]{2,1,0:T(8,128)(2,1)} fusion(bf16[1,512,512]{2,1,0:T(8,128)(2,1)S(1)} %bitcast.17, bf16[1,512,512]{2,1,0:T(8,128)(2,1)} %bitcast.14, pred[]{:T(512)S(6)} %eq.24), kind=kLoop, calls=%fused_computation | loop fusion | flops 4718592 | bytes 2097153 | tf_op jit(solution)/shard_map/jit(_where)/select_n | solution.py:338
  (40 shorter events, 0.2 us)
Async XLA Ops:
  0.0 1.4 copy-start
  0.0 37.4 %collective-permute-start.8 = (bf16[512,16384]{1,0:T(8,128)(2,1)}, bf16[512,16384]{1,0:T(8,128)(2,1)}, u32[]{:S(2)}, u32[]{:S(2)}) collective-permute-start(bf16[512,16384]{1,0:T(8,128)(2,1)} %bitcast.20), channel_id=1, source_target_pairs={{1,0},{0,1},{65,64},{64,65},{9,8},{8,9},{73,72},{72,73},{17,16},{1... | collective-permute-start | bytes 50331656 | tf_op jit(solution)/shard_map/ppermute | solution.py:47
  1.5 2.3 %copy-start.5 = (bf16[2048,128]{1,0:T(8,128)(2,1)}, bf16[2048,128]{1,0:T(8,128)(2,1)S(1)}, u32[]{:S(2)}) copy-start(bf16[2048,128]{1,0:T(8,128)(2,1)S(1)} %constant_dynamic-slice_fusion.1.refs_3_) | copy-start | bytes 1572868
  1.5 11.0 %collective-permute-start.2 = (bf16[2048,128]{1,0:T(8,128)(2,1)S(1)}, bf16[2048,128]{1,0:T(8,128)(2,1)S(1)}, u32[]{:S(2)}, u32[]{:S(2)}) collective-permute-start(bf16[2048,128]{1,0:T(8,128)(2,1)S(1)} %constant_dynamic-slice_fusion.1.refs_3_), channel_id=1, source_target_pairs={{64,0},{73,1},{8,64},{1,65},{72,8},{65,9},{0,72},{9,73},{80,16},{8... | collective-permute-start | bytes 1572872 | tf_op jit(solution)/shard_map/ppermute | solution.py:47
  3.8 9.3 %collective-permute-start.1 = (bf16[2048,128]{1,0:T(8,128)(2,1)S(1)}, bf16[2048,128]{1,0:T(8,128)(2,1)S(1)}, u32[]{:S(2)}, u32[]{:S(2)}) collective-permute-start(bf16[2048,128]{1,0:T(8,128)(2,1)S(1)} %constant_dynamic-slice_fusion.1.refs_3_), channel_id=1, source_target_pairs={{16,0},{49,1},{80,64},{113,65},{24,8},{57,9},{88,72},{121,73},{32,... | collective-permute-start | bytes 1572872 | tf_op jit(solution)/shard_map/ppermute | solution.py:47
  12.5 0.8 copy-start.6
  13.3 26.6 %copy-start.7 = (bf16[2048,128]{1,0:T(8,128)(2,1)}, bf16[2048,128]{1,0:T(8,128)(2,1)S(1)}, u32[]{:S(2)}) copy-start(bf16[2048,128]{1,0:T(8,128)(2,1)S(1)} %collective-permute-done.1.refs_4_) | copy-start | bytes 1572868
  13.3 9.3 %collective-permute-start.5 = (bf16[2048,128]{1,0:T(8,128)(2,1)S(1)}, bf16[2048,128]{1,0:T(8,128)(2,1)S(1)}, u32[]{:S(2)}, u32[]{:S(2)}) collective-permute-start(bf16[2048,128]{1,0:T(8,128)(2,1)S(1)} %collective-permute-done.1.refs_4_), channel_id=1, source_target_pairs={{2,0},{7,1},{66,64},{71,65},{10,8},{15,9},{74,72},{79,73},{18,16},... | collective-permute-start | bytes 1572872 | tf_op jit(solution)/shard_map/ppermute | solution.py:47
  16.1 9.3 %collective-permute-start.4 = (bf16[2048,128]{1,0:T(8,128)(2,1)S(1)}, bf16[2048,128]{1,0:T(8,128)(2,1)}, u32[]{:S(2)}, u32[]{:S(2)}) collective-permute-start(bf16[2048,128]{1,0:T(8,128)(2,1)S(1)} %collective-permute-done.1.refs_4_), channel_id=1, source_target_pairs={{64,0},{73,1},{8,64},{1,65},{72,8},{65,9},{0,72},{9,73},{80,16},{8... | collective-permute-start | bytes 1572872 | tf_op jit(solution)/shard_map/ppermute | solution.py:47
  16.8 9.8 %collective-permute-start.3 = (bf16[2048,128]{1,0:T(8,128)(2,1)S(1)}, bf16[2048,128]{1,0:T(8,128)(2,1)}, u32[]{:S(2)}, u32[]{:S(2)}) collective-permute-start(bf16[2048,128]{1,0:T(8,128)(2,1)S(1)} %collective-permute-done.1.refs_4_), channel_id=1, source_target_pairs={{16,0},{49,1},{80,64},{113,65},{24,8},{57,9},{88,72},{121,73},{32,... | collective-permute-start | bytes 1572872 | tf_op jit(solution)/shard_map/ppermute | solution.py:47
  22.6 19.2 %copy-start.8 = (bf16[2048,128]{1,0:T(8,128)(2,1)}, bf16[2048,128]{1,0:T(8,128)(2,1)S(1)}, u32[]{:S(2)}) copy-start(bf16[2048,128]{1,0:T(8,128)(2,1)S(1)} %collective-permute-done.5.refs_6_) | copy-start | bytes 1572868
  26.6 9.5 %collective-permute-start.6 = (bf16[2048,128]{1,0:T(8,128)(2,1)}, bf16[2048,128]{1,0:T(8,128)(2,1)S(1)}, u32[]{:S(2)}, u32[]{:S(2)}) collective-permute-start(bf16[2048,128]{1,0:T(8,128)(2,1)} %collective-permute-done.3.refs_5_), channel_id=1, source_target_pairs={{64,0},{73,1},{8,64},{1,65},{72,8},{65,9},{0,72},{9,73},{80,16},{8... | collective-permute-start | bytes 1572872 | tf_op jit(solution)/shard_map/ppermute | solution.py:47
  27.9 9.5 %collective-permute-start.7 = (bf16[2048,128]{1,0:T(8,128)(2,1)}, bf16[2048,128]{1,0:T(8,128)(2,1)S(1)}, u32[]{:S(2)}, u32[]{:S(2)}) collective-permute-start(bf16[2048,128]{1,0:T(8,128)(2,1)} %collective-permute-done.4.refs_8_), channel_id=1, source_target_pairs={{2,0},{7,1},{66,64},{71,65},{10,8},{15,9},{74,72},{79,73},{18,16},... | collective-permute-start | bytes 1572872 | tf_op jit(solution)/shard_map/ppermute | solution.py:47
  27.9 37.3 %collective-permute-start.9 = (bf16[2048,512]{1,0:T(8,128)(2,1)S(1)}, bf16[2048,512]{1,0:T(8,128)(2,1)}, u32[]{:S(2)}, u32[]{:S(2)}) collective-permute-start(bf16[2048,512]{1,0:T(8,128)(2,1)S(1)} %constant_dynamic-slice_fusion.refs_0_), channel_id=1, source_target_pairs={{16,0},{49,1},{80,64},{113,65},{24,8},{57,9},{88,72},{121,73},{32,... | collective-permute-start | bytes 6291464 | tf_op jit(solution)/shard_map/ppermute | solution.py:47
  36.0 1.3 copy-start.9
  37.4 0.8 copy-start.10
  38.2 27.1 %collective-permute-start.10 = (bf16[2048,512]{1,0:T(8,128)(2,1)S(1)}, bf16[2048,512]{1,0:T(8,128)(2,1)}, u32[]{:S(2)}, u32[]{:S(2)}) collective-permute-start(bf16[2048,512]{1,0:T(8,128)(2,1)S(1)} %constant_dynamic-slice_fusion.refs_0_), channel_id=1, source_target_pairs={{64,0},{73,1},{8,64},{1,65},{72,8},{65,9},{0,72},{9,73},{80,16},{8... | collective-permute-start | bytes 6291464 | tf_op jit(solution)/shard_map/ppermute | solution.py:47
  65.3 32.6 %collective-permute-start.14 = (bf16[2048,512]{1,0:T(8,128)(2,1)}, bf16[2048,512]{1,0:T(8,128)(2,1)}, u32[]{:S(2)}, u32[]{:S(2)}) collective-permute-start(bf16[2048,512]{1,0:T(8,128)(2,1)} %collective-permute-done.9.refs_1_), channel_id=1, source_target_pairs={{2,0},{7,1},{66,64},{71,65},{10,8},{15,9},{74,72},{79,73},{18,16},... | collective-permute-start | bytes 6291464 | tf_op jit(solution)/shard_map/ppermute | solution.py:47
  65.4 32.5 %collective-permute-start.13 = (bf16[2048,512]{1,0:T(8,128)(2,1)}, bf16[2048,512]{1,0:T(8,128)(2,1)}, u32[]{:S(2)}, u32[]{:S(2)}) collective-permute-start(bf16[2048,512]{1,0:T(8,128)(2,1)} %collective-permute-done.9.refs_1_), channel_id=1, source_target_pairs={{64,0},{73,1},{8,64},{1,65},{72,8},{65,9},{0,72},{9,73},{80,16},{8... | collective-permute-start | bytes 6291464 | tf_op jit(solution)/shard_map/ppermute | solution.py:47
  66.1 31.8 %collective-permute-start.12 = (bf16[2048,512]{1,0:T(8,128)(2,1)}, bf16[2048,512]{1,0:T(8,128)(2,1)}, u32[]{:S(2)}, u32[]{:S(2)}) collective-permute-start(bf16[2048,512]{1,0:T(8,128)(2,1)} %collective-permute-done.9.refs_1_), channel_id=1, source_target_pairs={{16,0},{49,1},{80,64},{113,65},{24,8},{57,9},{88,72},{121,73},{32,... | collective-permute-start | bytes 6291464 | tf_op jit(solution)/shard_map/ppermute | solution.py:47
  66.3 31.5 %collective-permute-start.11 = (bf16[1024,128]{1,0:T(8,128)(2,1)S(1)}, bf16[1024,128]{1,0:T(8,128)(2,1)S(1)}, u32[]{:S(2)}, u32[]{:S(2)}) collective-permute-start(bf16[1024,128]{1,0:T(8,128)(2,1)S(1)} %maximum_select_fusion.1), channel_id=1, source_target_pairs={{8,0},{9,1},{72,64},{73,65},{0,8},{1,9},{64,72},{65,73},{24,16},{2... | collective-permute-start | bytes 786440 | tf_op jit(solution)/shard_map/ppermute | solution.py:47
  97.9 14.9 %collective-permute-start.18 = (bf16[2048,128]{1,0:T(8,128)(2,1)S(1)}, bf16[2048,128]{1,0:T(8,128)(2,1)S(1)}, u32[]{:S(2)}, u32[]{:S(2)}) collective-permute-start(bf16[2048,128]{1,0:T(8,128)(2,1)S(1)} %pad_maximum_fusion), channel_id=1, source_target_pairs={{6,0},{3,1},{70,64},{67,65},{14,8},{11,9},{78,72},{75,73},{22,16},... | collective-permute-start | bytes 1572872 | tf_op jit(solution)/shard_map/ppermute | solution.py:47
  100.3 12.7 %collective-permute-start.17 = (bf16[2048,128]{1,0:T(8,128)(2,1)S(1)}, bf16[2048,128]{1,0:T(8,128)(2,1)S(1)}, u32[]{:S(2)}, u32[]{:S(2)}) collective-permute-start(bf16[2048,128]{1,0:T(8,128)(2,1)S(1)} %pad_maximum_fusion), channel_id=1, source_target_pairs={{2,0},{7,1},{66,64},{71,65},{10,8},{15,9},{74,72},{79,73},{18,16},... | collective-permute-start | bytes 1572872 | tf_op jit(solution)/shard_map/ppermute | solution.py:47
  100.3 31.7 %collective-permute-start.15 = (bf16[2048,512]{1,0:T(8,128)(2,1)}, bf16[2048,512]{1,0:T(8,128)(2,1)S(1)}, u32[]{:S(2)}, u32[]{:S(2)}) collective-permute-start(bf16[2048,512]{1,0:T(8,128)(2,1)} %collective-permute-done.13.refs_2_), channel_id=1, source_target_pairs={{16,0},{49,1},{80,64},{113,65},{24,8},{57,9},{88,72},{121,73},{32,... | collective-permute-start | bytes 6291464 | tf_op jit(solution)/shard_map/ppermute | solution.py:47
  100.3 31.8 %collective-permute-start.16 = (bf16[2048,512]{1,0:T(8,128)(2,1)}, bf16[2048,512]{1,0:T(8,128)(2,1)S(1)}, u32[]{:S(2)}, u32[]{:S(2)}) collective-permute-start(bf16[2048,512]{1,0:T(8,128)(2,1)} %collective-permute-done.14.refs_1_), channel_id=1, source_target_pairs={{64,0},{73,1},{8,64},{1,65},{72,8},{65,9},{0,72},{9,73},{80,16},{8... | collective-permute-start | bytes 6291464 | tf_op jit(solution)/shard_map/ppermute | solution.py:47
  112.8 17.2 %copy-start.4 = (s32[1,8,16]{2,1,0:T(8,128)S(1)}, s32[1,8,16]{2,1,0:T(8,128)}, u32[]{:S(2)}) copy-start(s32[1,8,16]{2,1,0:T(8,128)} %param.7) | copy-start | bytes 1540
  112.9 11.3 %collective-permute-start.19 = (bf16[2048,128]{1,0:T(8,128)(2,1)S(1)}, bf16[2048,128]{1,0:T(8,128)(2,1)S(1)}, u32[]{:S(2)}, u32[]{:S(2)}) collective-permute-start(bf16[2048,128]{1,0:T(8,128)(2,1)S(1)} %collective-permute-done.17), channel_id=1, source_target_pairs={{2,0},{7,1},{66,64},{71,65},{10,8},{15,9},{74,72},{79,73},{18,16},... | collective-permute-start | bytes 1572872 | tf_op jit(solution)/shard_map/ppermute | solution.py:47
  114.5 15.3 %collective-permute-start.20 = (bf16[2048,128]{1,0:T(8,128)(2,1)S(1)}, bf16[2048,128]{1,0:T(8,128)(2,1)S(1)}, u32[]{:S(2)}, u32[]{:S(2)}) collective-permute-start(bf16[2048,128]{1,0:T(8,128)(2,1)S(1)} %pad_maximum_fusion), channel_id=1, source_target_pairs={{1,0},{0,1},{65,64},{64,65},{9,8},{8,9},{73,72},{72,73},{17,16},{1... | collective-permute-start | bytes 1572872 | tf_op jit(solution)/shard_map/ppermute | solution.py:47
  121.1 8.9 %collective-permute-start.21 = (bf16[2048,128]{1,0:T(8,128)(2,1)S(1)}, bf16[2048,128]{1,0:T(8,128)(2,1)S(1)}, u32[]{:S(2)}, u32[]{:S(2)}) collective-permute-start(bf16[2048,128]{1,0:T(8,128)(2,1)S(1)} %collective-permute-done.17), channel_id=1, source_target_pairs={{1,0},{0,1},{65,64},{64,65},{9,8},{8,9},{73,72},{72,73},{17,16},{1... | collective-permute-start | bytes 1572872 | tf_op jit(solution)/shard_map/ppermute | solution.py:47
  124.3 6.9 %collective-permute-start.22 = (bf16[2048,128]{1,0:T(8,128)(2,1)S(1)}, bf16[2048,128]{1,0:T(8,128)(2,1)S(1)}, u32[]{:S(2)}, u32[]{:S(2)}) collective-permute-start(bf16[2048,128]{1,0:T(8,128)(2,1)S(1)} %collective-permute-done.19), channel_id=1, source_target_pairs={{1,0},{0,1},{65,64},{64,65},{9,8},{8,9},{73,72},{72,73},{17,16},{1... | collective-permute-start | bytes 1572872 | tf_op jit(solution)/shard_map/ppermute | solution.py:47
  129.8 2.1 %collective-permute-start.23 = (bf16[2048,128]{1,0:T(8,128)(2,1)S(1)}, bf16[2048,128]{1,0:T(8,128)(2,1)S(1)}, u32[]{:S(2)}, u32[]{:S(2)}) collective-permute-start(bf16[2048,128]{1,0:T(8,128)(2,1)S(1)} %collective-permute-done.18), channel_id=1, source_target_pairs={{1,0},{0,1},{65,64},{64,65},{9,8},{8,9},{73,72},{72,73},{17,16},{1... | collective-permute-start | bytes 1572872 | tf_op jit(solution)/shard_map/ppermute | solution.py:47
  130.0 10.7 %collective-permute-start = (s32[8,16]{1,0:T(8,128)S(1)}, s32[8,16]{1,0:T(8,128)S(1)}, u32[]{:S(2)}, u32[]{:S(2)}) collective-permute-start(s32[8,16]{1,0:T(8,128)S(1)} %bitcast.18), channel_id=1, source_target_pairs={{1,0},{0,1},{65,64},{64,65},{9,8},{8,9},{73,72},{72,73},{17,16},{1... | collective-permute-start | bytes 1544 | tf_op jit(solution)/shard_map/ppermute | solution.py:47
  132.0 8.8 %copy-start.2 = (bf16[16384,128]{1,0:T(8,128)(2,1)}, bf16[16384,128]{1,0:T(8,128)(2,1)S(1)}, u32[]{:S(2)}) copy-start(bf16[16384,128]{1,0:T(8,128)(2,1)S(1)} %constant_dynamic-update-slice_fusion.kv) | copy-start | bytes 12582916
  150.1 11.3 %collective-permute-start.24 = (bf16[512,512]{1,0:T(8,128)(2,1)}, bf16[512,512]{1,0:T(8,128)(2,1)}, u32[]{:S(2)}, u32[]{:S(2)}) collective-permute-start(bf16[512,512]{1,0:T(8,128)(2,1)} %shard_map.50), channel_id=1, source_target_pairs={{1,0},{0,1},{65,64},{64,65},{9,8},{8,9},{73,72},{72,73},{17,16},{1... | collective-permute-start | bytes 1572872 | tf_op jit(solution)/shard_map/ppermute | solution.py:47
  150.6 13.4 %copy-start.1 = (bf16[2048,256]{1,0:T(8,128)(2,1)S(1)}, bf16[2048,256]{1,0:T(8,128)(2,1)}, u32[]{:S(2)}) copy-start(bf16[2048,256]{1,0:T(8,128)(2,1)} %param.6) | copy-start | bytes 3145732
  150.6 2.3 %copy-start.3 = (bf16[16384,128]{1,0:T(8,128)(2,1)S(1)}, bf16[16384,128]{1,0:T(8,128)(2,1)}, u32[]{:S(2)}) copy-start(bf16[16384,128]{1,0:T(8,128)(2,1)} %copy-done.2) | copy-start | bytes 12582916

commit v4 on v3

--- a/solution.py
+++ b/solution.py
@@ -286,14 +286,6 @@
     sib_picks = get(picks[0], FROM_CORE)
     a0 = lax.dynamic_slice(query_weight, (0, c * width), (shard, width))
     kv_a1, kv_b0 = get(kv_a0, FROM_Y), get(kv_a0, FROM_Z)
-    kv_a1, kv_b0 = fence((kv_a1, kv_b0))
-    kv_a2, kv_b1, kv_a3 = get(kv_a1, FROM_Y), get(kv_a1, FROM_Z), get(kv_a1, FROM_PAIR)
-    kv_a2, kv_b1, kv_a3, a0 = fence((kv_a2, kv_b1, kv_a3, a0))
-    a1 = get(a0, FROM_Y)
-    kv_b2, kv_b3 = get(kv_a2, FROM_Z), get(kv_b1, FROM_PAIR)
-    kv_b2, kv_b3, sib, a0 = fence((kv_b2, kv_b3, sib, a0))
-    b0 = get(a0, FROM_Z)
-
     cos_own, sin_own = tables_of(seq * rows, rows)
     cos_sib, sin_sib = tables_of((seq + step) * rows, rows)
     plain = c == 1
@@ -301,26 +293,40 @@
         jnp.where(plain, 1.0, cos_own), jnp.where(plain, 0.0, sin_own),
         jnp.where(plain, 1.0, cos_sib), jnp.where(plain, 0.0, sin_sib),
     ]
+    kv_a1, kv_b0, cos_own, sin_own, cos_sib, sin_sib, kv_tables = fence(
+        (kv_a1, kv_b0, cos_own, sin_own, cos_sib, sin_sib, kv_tables)
+    )
+    kv_a2, kv_b1, kv_a3 = get(kv_a1, FROM_Y), get(kv_a1, FROM_Z), get(kv_a1, FROM_PAIR)
+    kv_a2, kv_b1, kv_a3, a0 = fence((kv_a2, kv_b1, kv_a3, a0))
+    a1 = get(a0, FROM_Y)
+    kv_b2, kv_b3 = get(kv_a2, FROM_Z), get(kv_b1, FROM_PAIR)
+    kv_b2, kv_b3, sib, a0 = fence((kv_b2, kv_b3, sib, a0))
+    b0 = get(a0, FROM_Z)
+
+    acc = project(
+        blocks((0, 0), (1, 0), (2, 0), (3, 0)), own, sib, [kv_a0, kv_a1, kv_a2, kv_a3]
+    )
+    kv_b0, a1, *acc = fence((kv_b0, a1, *acc))
+    a2 = get(a1, FROM_Y)
+    b1 = get(a1, FROM_Z)
+    a3 = get(a1, FROM_PAIR)
     kv_own, kv_sib = project(
-        blocks(*[(k, flip) for flip in (0, 1) for k in range(SIDE)]),
-        own, sib, [kv_a0, kv_a1, kv_a2, kv_a3, kv_b0, kv_b1, kv_b2, kv_b3],
-        tables=kv_tables,
+        blocks((0, 1), (1, 1), (2, 1), (3, 1)),
+        own, sib, [kv_b0, kv_b1, kv_b2, kv_b3], acc, tables=kv_tables,
     )
     here = jnp.where(
         plain,
         jnp.concatenate([kv_sib, kv_own], 0),
         jnp.concatenate([kv_own, kv_sib], 0),
     )
-    here, a1, b0 = fence((here, a1, b0))
-    a2 = get(a1, FROM_Y)
-    b1 = get(a1, FROM_Z)
-    a3 = get(a1, FROM_PAIR)
+    here, b0 = fence((here, b0))
     near = jnp.concatenate([here, get(here, FROM_Z2)], 0)
     acc = project_query(blocks((0, 0), (1, 0), (0, 1)), own, sib, [a0, a1, b0])
-    near, a2, b1, a3, acc = fence((near, a2, b1, a3, acc))
-    ahead, back = get(near, FROM_X), get(near, FROM_X_BACK)
+    a2, b1, a3, acc = fence((a2, b1, a3, acc))
     b2 = get(b1, FROM_Y)
     b3 = get(a3, FROM_Z)
+    near, a2, acc = fence((near, a2, acc))
+    ahead, back = get(near, FROM_X), get(near, FROM_X_BACK)
     acc = project_query(blocks((2, 0), (3, 0), (1, 1)), own, sib, [a2, a3, b1], acc)
     ahead, back, *acc = fence((ahead, back, *acc))
     chunks = [near, ahead, get(ahead, FROM_X), back]

time: 164 us -> 161 us (0.982)
  waiting for transfers between devices: 47.3 us -> 35.5 us
  starting transfers between devices: 32.2 us -> 38.7 us
  Pallas kernels: 68.4 us -> 71.1 us
    ppermute x25, waiting for transfers between devices: 47.3 us -> 35.5 us  [get(): return lax.ppermute(value, AXES, perm)]
    ppermute x25, starting transfers between devices: 32.2 us -> 38.7 us  [get(): return lax.ppermute(value, AXES, perm)]
    pallas_call x1 -> x2, Pallas kernels: 18.8 us -> 21.5 us  [project(): pl.pallas_call(functools.partial(project_kernel, n, first, last), grid_sp...]
    concatenate x2 -> x0, other arithmetic: 1.73 us -> none  [tables_of(): jnp.concatenate([cosine, cosine], 1)]
    unnamed x29 -> x25, local copies, waits for them, and re-layouts: 3.77 us -> 3.55 us
  transfers between devices with their start and end apart: 25 -> 25, of which waited for: 12 -> 13; matrix products, arithmetic and copies ran while one was open for 6% -> 6% of each run, Pallas kernels for 36% -> 39%
where the time goes in v4:
time: 161 us; the launch traced here: 160 us
  Pallas kernels  71.1 us (44%)
  starting transfers between devices  38.7 us (24%)
  waiting for transfers between devices  35.5 us (22%)
  other arithmetic  9.29 us (6%)
  local copies, waits for them, and re-layouts  5.38 us (3%)
    ppermute x25, starting transfers between devices, get(): return lax.ppermute(value, AXES, perm)  38.7 us
    ppermute x25, waiting for transfers between devices, get(): return lax.ppermute(value, AXES, perm)  35.5 us
    pallas_call x3, Pallas kernels, project_query(): pl.pallas_call(functools.partial(query_kernel, n, not acc), grid_spec=plt...  31.7 us
    pallas_call x2, Pallas kernels, project(): pl.pallas_call(functools.partial(project_kernel, n, first, last), grid_sp...  21.5 us
    pallas_call x2, Pallas kernels, attend(): pl.pallas_call(functools.partial(attend_kernel, nblk, heads), in_specs=[s...  17.9 us
    unnamed x25, local copies, waits for them, and re-layouts  3.55 us
  transfers between devices with their start and end apart: 25, of which 13 were waited for; matrix products, arithmetic and copies ran while one was open for 6% of the time, Pallas kernels for 39%

profile of v4, /device:TPU:1, one launch (start us, length us, event | category | flops | bytes accessed | tf_op | source)
XLA Modules:
  0.0 160.3 jit_solution(8131817067029166293)
XLA Ops:
  0.0 1.4 collective-permute-start.8
  1.5 2.3 %collective-permute-start.2 = (bf16[2048,128]{1,0:T(8,128)(2,1)S(1)}, bf16[2048,128]{1,0:T(8,128)(2,1)S(1)}, u32[]{:S(2)}, u32[]{:S(2)}) collective-permute-start(bf16[2048,128]{1,0:T(8,128)(2,1)S(1)} %constant_dynamic-slice_fusion.1.refs_3_), channel_id=1, source_target_pairs={{64,0},{73,1},{8,64},{1,65},{72,8},{65,9},{0,72},{9,73},{80,16},{8... | collective-permute-start | bytes 1572872 | tf_op jit(solution)/shard_map/ppermute | solution.py:47
  3.8 1.3 collective-permute-start.1
  5.1 1.9 %fusion.1 = (f32[512,64]{1,0:T(8,128)S(1)}, f32[512,64]{1,0:T(8,128)S(1)}, f32[512,64]{1,0:T(8,128)S(1)}, f32[512,64]{1,0:T(8,128)S(1)}, f32[512,64]{1,0:T(8,128)S(1)}, /*index=5*/f32[512,64]{1,0:T(8,128)S(1)}) fusion(f32[64]{0:T(128)S(1)} %negate_power_fusion, f32[512]{0:T(512)S(1)} %add_convert_fusion, f32[512]{0:T(512)S(1)} %add_convert_fusion.1), kind=kLoop, calls=%fused_computation.16 | loop fusion | flops 131072 | bytes 790784 | tf_op jit(solution)/shard_map/neg | solution.py:265
  7.0 1.0 broadcast_select_fusion.2
  8.1 1.0 broadcast_select_fusion
  9.1 3.4 %collective-permute-done.2.refs_3_ = bf16[2048,128]{1,0:T(8,128)(2,1)S(1)} collective-permute-done((bf16[2048,128]{1,0:T(8,128)(2,1)S(1)}, bf16[2048,128]{1,0:T(8,128)(2,1)S(1)}, u32[]{:S(2)}, u32[]{:S(2)}) %collective-permute-start.2) | collective-permute-done | bytes 524320 | tf_op jit(solution)/shard_map/ppermute | solution.py:47
  12.5 0.7 collective-permute-done.1.refs_4_
  13.2 2.2 %collective-permute-start.5 = (bf16[2048,128]{1,0:T(8,128)(2,1)}, bf16[2048,128]{1,0:T(8,128)(2,1)}, u32[]{:S(2)}, u32[]{:S(2)}) collective-permute-start(bf16[2048,128]{1,0:T(8,128)(2,1)} %collective-permute-done.1.refs_4_), channel_id=1, source_target_pairs={{2,0},{7,1},{66,64},{71,65},{10,8},{15,9},{74,72},{79,73},{18,16},... | collective-permute-start | bytes 1572872 | tf_op jit(solution)/shard_map/ppermute | solution.py:47
  15.4 1.4 collective-permute-start.4
  16.8 0.6 collective-permute-start.3
  17.4 1.7 %constant_dynamic-slice_fusion.refs_0_ = bf16[2048,512]{1,0:T(8,128)(2,1)S(1)} fusion(bf16[2048,1024]{1,0:T(8,128)(2,1)} %param.5, s32[]{:T(128)S(6)} %select_n.134), kind=kLoop, calls=%fused_computation.35 | loop fusion | bytes 4194308 | tf_op jit(solution)/shard_map/dynamic_slice | solution.py:287
  19.1 3.7 %collective-permute-done.5.refs_6_ = bf16[2048,128]{1,0:T(8,128)(2,1)} collective-permute-done((bf16[2048,128]{1,0:T(8,128)(2,1)}, bf16[2048,128]{1,0:T(8,128)(2,1)}, u32[]{:S(2)}, u32[]{:S(2)}) %collective-permute-start.5) | collective-permute-done | bytes 524320 | tf_op jit(solution)/shard_map/ppermute | solution.py:47
  22.8 2.2 %collective-permute-done.4.refs_4_ = bf16[2048,128]{1,0:T(8,128)(2,1)} collective-permute-done((bf16[2048,128]{1,0:T(8,128)(2,1)}, bf16[2048,128]{1,0:T(8,128)(2,1)}, u32[]{:S(2)}, u32[]{:S(2)}) %collective-permute-start.4) | collective-permute-done | bytes 524320 | tf_op jit(solution)/shard_map/ppermute | solution.py:47
  24.9 2.0 %collective-permute-done.3.refs_5_ = bf16[2048,128]{1,0:T(8,128)(2,1)} collective-permute-done((bf16[2048,128]{1,0:T(8,128)(2,1)}, bf16[2048,128]{1,0:T(8,128)(2,1)}, u32[]{:S(2)}, u32[]{:S(2)}) %collective-permute-start.3) | collective-permute-done | bytes 524320 | tf_op jit(solution)/shard_map/ppermute | solution.py:47
  26.9 1.3 collective-permute-start.6
  28.3 2.6 %collective-permute-start.7 = (bf16[2048,128]{1,0:T(8,128)(2,1)}, bf16[2048,128]{1,0:T(8,128)(2,1)S(1)}, u32[]{:S(2)}, u32[]{:S(2)}) collective-permute-start(bf16[2048,128]{1,0:T(8,128)(2,1)} %collective-permute-done.4.refs_4_), channel_id=1, source_target_pairs={{2,0},{7,1},{66,64},{71,65},{10,8},{15,9},{74,72},{79,73},{18,16},... | collective-permute-start | bytes 1572872 | tf_op jit(solution)/shard_map/ppermute | solution.py:47
  30.9 5.5 %collective-permute-done.6.refs_5_ = bf16[2048,128]{1,0:T(8,128)(2,1)S(1)} collective-permute-done((bf16[2048,128]{1,0:T(8,128)(2,1)}, bf16[2048,128]{1,0:T(8,128)(2,1)S(1)}, u32[]{:S(2)}, u32[]{:S(2)}) %collective-permute-start.6) | collective-permute-done | bytes 524320 | tf_op jit(solution)/shard_map/ppermute | solution.py:47
  36.4 1.3 collective-permute-done.7.refs_6_
  37.7 0.8 copy-done.8
  38.5 0.3 collective-permute-start.13
  38.8 0.6 pad_add_fusion.1.refs_0_
  39.4 10.6 %shard_map.46 = (f32[512,128]{1,0:T(8,128)}, f32[512,128]{1,0:T(8,128)}) custom-call(s32[4]{0:T(128)} %pad_add_fusion.1.refs_0_, bf16[512,16384]{1,0:T(8,128)(2,1)} %bitcast.21, bf16[512,16384]{1,0:T(8,128)(2,1)} %collective-permute-done.8.refs_2_.sib, bf16[2048,128]{1,0:T(8,128)(2,1)} %copy-done.5, bf16[2048,128]{1,0:T(8,128)(2,1)} %collective-permute-done.1.refs_4_, ...), custom_call_target="tpu_custom_call" | custom-call | flops 2147483648 | bytes 19922944 | tf_op jit(solution)/shard_map/pallas_call | solution.py:113
  50.0 3.2 %collective-permute-done.9.refs_1_ = bf16[2048,512]{1,0:T(8,128)(2,1)} collective-permute-done((bf16[2048,512]{1,0:T(8,128)(2,1)S(1)}, bf16[2048,512]{1,0:T(8,128)(2,1)}, u32[]{:S(2)}, u32[]{:S(2)}) %collective-permute-start.9) | collective-permute-done | bytes 2097184 | tf_op jit(solution)/shard_map/ppermute | solution.py:47
  53.1 1.3 collective-permute-start.11
  54.5 0.0 collective-permute-start.10
  54.5 0.1 pad_add_fusion.2.blocks
  54.6 0.1 pad_add_fusion.blocks
  54.6 0.6 pad_add_fusion.3.refs_0_
  55.2 0.1 pad_add_fusion.4.blocks
  55.3 11.0 %shard_map.47 = (bf16[512,128]{1,0:T(8,128)(2,1)}, bf16[512,128]{1,0:T(8,128)(2,1)}) custom-call(s32[4]{0:T(128)} %pad_add_fusion.3.refs_0_, bf16[512,16384]{1,0:T(8,128)(2,1)} %bitcast.22, bf16[512,16384]{1,0:T(8,128)(2,1)} %collective-permute-done.8.refs_2_.sib, bf16[2048,128]{1,0:T(8,128)(2,1)} %copy-done.6, ...), custom_call_target="tpu_custom_call" | custom-call | flops 2147483648 | bytes 19922944 | tf_op jit(solution)/shard_map/pallas_call | solution.py:113
  66.3 1.2 maximum_select_fusion.1
  67.5 2.2 %collective-permute-start.16 = (bf16[1024,128]{1,0:T(8,128)(2,1)S(1)}, bf16[1024,128]{1,0:T(8,128)(2,1)S(1)}, u32[]{:S(2)}, u32[]{:S(2)}) collective-permute-start(bf16[1024,128]{1,0:T(8,128)(2,1)S(1)} %maximum_select_fusion.1), channel_id=1, source_target_pairs={{8,0},{9,1},{72,64},{73,65},{0,8},{1,9},{64,72},{65,73},{24,16},{2... | collective-permute-start | bytes 786440 | tf_op jit(solution)/shard_map/ppermute | solution.py:47
  69.7 10.5 %shard_map.48 = (f32[512,512]{1,0:T(8,128)S(1)}, f32[512,512]{1,0:T(8,128)S(1)}) custom-call(s32[3]{0:T(128)S(1)} %pad_add_fusion.2.blocks, bf16[512,16384]{1,0:T(8,128)(2,1)} %bitcast.23, bf16[512,16384]{1,0:T(8,128)(2,1)} %collective-permute-done.8.refs_2_.sib, bf16[2048,512]{1,0:T(8,128)(2,1)S(1)} %constant_dynamic-slice_fusion.refs_0_, ...), custom_call_target="tpu_custom_call" | custom-call | flops 6442450944 | bytes 23068672 | tf_op jit(solution)/shard_map/pallas_call | solution.py:165
  80.3 9.8 %collective-permute-done.11.refs_2_ = bf16[2048,512]{1,0:T(8,128)(2,1)} collective-permute-done((bf16[2048,512]{1,0:T(8,128)(2,1)}, bf16[2048,512]{1,0:T(8,128)(2,1)}, u32[]{:S(2)}, u32[]{:S(2)}) %collective-permute-start.11) | collective-permute-done | bytes 2097184 | tf_op jit(solution)/shard_map/ppermute | solution.py:47
  90.0 0.6 collective-permute-start.14
  90.6 2.3 %collective-permute-done.16 = bf16[1024,128]{1,0:T(8,128)(2,1)S(1)} collective-permute-done((bf16[1024,128]{1,0:T(8,128)(2,1)S(1)}, bf16[1024,128]{1,0:T(8,128)(2,1)S(1)}, u32[]{:S(2)}, u32[]{:S(2)}) %collective-permute-start.16) | collective-permute-done | bytes 262176 | tf_op jit(solution)/shard_map/ppermute | solution.py:47
  92.9 3.1 %collective-permute-start.18 = (bf16[2048,128]{1,0:T(8,128)(2,1)S(1)}, bf16[2048,128]{1,0:T(8,128)(2,1)S(1)}, u32[]{:S(2)}, u32[]{:S(2)}) collective-permute-start(bf16[2048,128]{1,0:T(8,128)(2,1)S(1)} %pad_maximum_fusion), channel_id=1, source_target_pairs={{6,0},{3,1},{70,64},{67,65},{14,8},{11,9},{78,72},{75,73},{22,16},... | collective-permute-start | bytes 1572872 | tf_op jit(solution)/shard_map/ppermute | solution.py:47
  96.0 12.5 %shard_map.49 = (f32[512,512]{1,0:T(8,128)S(1)}, f32[512,512]{1,0:T(8,128)S(1)}) custom-call(s32[3]{0:T(128)S(1)} %pad_add_fusion.4.blocks, bf16[512,16384]{1,0:T(8,128)(2,1)} %bitcast.24, bf16[512,16384]{1,0:T(8,128)(2,1)} %collective-permute-done.8.refs_2_.sib, bf16[2048,512]{1,0:T(8,128)(2,1)} %collective-permute-done.10.refs_0_, ...), custom_call_target="tpu_custom_call" | custom-call | flops 6442450944 | bytes 23068672 | tf_op jit(solution)/shard_map/pallas_call | solution.py:165
  108.5 0.0 copy-start.4
  108.5 0.1 collective-permute-start.19
  108.6 0.1 add_add_fusion.where
  108.7 8.6 %collective-permute-start.20 = (bf16[2048,128]{1,0:T(8,128)(2,1)S(1)}, bf16[2048,128]{1,0:T(8,128)(2,1)S(1)}, u32[]{:S(2)}, u32[]{:S(2)}) collective-permute-start(bf16[2048,128]{1,0:T(8,128)(2,1)S(1)} %pad_maximum_fusion), channel_id=1, source_target_pairs={{1,0},{0,1},{65,64},{64,65},{9,8},{8,9},{73,72},{72,73},{17,16},{1... | collective-permute-start | bytes 1572872 | tf_op jit(solution)/shard_map/ppermute | solution.py:47
  117.3 0.1 collective-permute-start.21
  117.4 0.1 constant_dynamic-update-slice_fusion.6
  117.5 0.4 collective-permute-done.19
  117.8 8.2 %collective-permute-start.22 = (bf16[2048,128]{1,0:T(8,128)(2,1)S(1)}, bf16[2048,128]{1,0:T(8,128)(2,1)S(1)}, u32[]{:S(2)}, u32[]{:S(2)}) collective-permute-start(bf16[2048,128]{1,0:T(8,128)(2,1)S(1)} %collective-permute-done.19), channel_id=1, source_target_pairs={{1,0},{0,1},{65,64},{64,65},{9,8},{8,9},{73,72},{72,73},{17,16},{1... | collective-permute-start | bytes 1572872 | tf_op jit(solution)/shard_map/ppermute | solution.py:47
  126.0 0.1 constant_dynamic-update-slice_fusion.5
  126.1 0.1 constant_dynamic-update-slice_fusion.4
  126.1 0.1 collective-permute-start.23
  126.2 0.1 constant_dynamic-update-slice_fusion.3
  126.3 0.6 collective-permute-start
  126.9 0.1 constant_dynamic-update-slice_fusion.2
  127.0 0.5 collective-permute-done.22
  127.5 0.1 constant_dynamic-update-slice_fusion.1
  127.6 0.7 collective-permute-done.23
  128.3 0.1 constant_dynamic-update-slice_fusion.kv
  128.4 8.7 %shard_map.50 = (f32[512,512]{1,0:T(8,128)S(1)}, f32[512,512]{1,0:T(8,128)S(1)}) custom-call(s32[2]{0:T(128)S(1)} %pad_add_fusion.blocks, bf16[512,16384]{1,0:T(8,128)(2,1)} %bitcast.25, bf16[512,16384]{1,0:T(8,128)(2,1)} %collective-permute-done.8.refs_2_.sib, bf16[2048,512]{1,0:T(8,128)(2,1)S(1)} %collective-permute-done.14.refs_0_, ...), custom_call_target="tpu_custom_call" | custom-call | flops 4294967296 | bytes 16777216 | tf_op jit(solution)/shard_map/pallas_call | solution.py:165
  137.1 9.4 %shard_map.51 = bf16[512,512]{1,0:T(8,128)(2,1)} custom-call(s32[8,16]{1,0:T(8,128)S(1)} %collective-permute-done.picks, s32[4]{0:T(128)S(1)} %add_add_fusion.where, f32[512,512]{1,0:T(8,128)S(1)} %get-tuple-element.91.raw, f32[512,128]{1,0:T(8,128)S(1)} %get-tuple-element.92.cosine, f32[512,128]{1,0:T(8,128)S(1)} %get-tuple-element.93.sine, ...), custom_call_target="tpu_custom_call" | custom-call | flops 1073741824 | bytes 6291456 | tf_op jit(solution)/shard_map/pallas_call | solution.py:242
  146.5 0.4 collective-permute-start.24
  146.8 0.1 add_add_fusion.1.where
  146.9 2.3 %copy-done.3 = bf16[16384,128]{1,0:T(8,128)(2,1)S(1)} copy-done((bf16[16384,128]{1,0:T(8,128)(2,1)S(1)}, bf16[16384,128]{1,0:T(8,128)(2,1)}, u32[]{:S(2)}) %copy-start.3) | copy-done | bytes 4194328
  149.2 8.5 %shard_map.52 = bf16[512,512]{1,0:T(8,128)(2,1)S(1)} custom-call(s32[8,16]{1,0:T(8,128)S(1)} %bitcast.19, s32[4]{0:T(128)S(1)} %add_add_fusion.1.where, f32[512,512]{1,0:T(8,128)S(1)} %get-tuple-element.96.raw, f32[512,128]{1,0:T(8,128)S(1)} %get-tuple-element.97.cosine, f32[512,128]{1,0:T(8,128)S(1)} %get-tuple-element.98.sine, bf16[16384,128]{1,0:T(8,128)(2,1)S(1)} %copy-done.3), custom_call_target="tpu_custom_call" | custom-call | flops 1073741824 | bytes 6291456 | tf_op jit(solution)/shard_map/pallas_call | solution.py:242
  157.7 2.5 %maximum_select_fusion = bf16[1,512,1024]{2,1,0:T(8,128)(2,1)} fusion(bf16[1,512,512]{2,1,0:T(8,128)(2,1)S(1)} %bitcast.17, bf16[1,512,512]{2,1,0:T(8,128)(2,1)} %bitcast.14, pred[]{:T(512)S(6)} %eq.24), kind=kLoop, calls=%fused_computation | loop fusion | flops 4718592 | bytes 2097153 | tf_op jit(solution)/shard_map/jit(_where)/select_n | solution.py:344
  (37 shorter events, 0.2 us)
Async XLA Ops:
  0.0 1.4 copy-start
  0.0 37.7 %collective-permute-start.8 = (bf16[512,16384]{1,0:T(8,128)(2,1)}, bf16[512,16384]{1,0:T(8,128)(2,1)}, u32[]{:S(2)}, u32[]{:S(2)}) collective-permute-start(bf16[512,16384]{1,0:T(8,128)(2,1)} %bitcast.20), channel_id=1, source_target_pairs={{1,0},{0,1},{65,64},{64,65},{9,8},{8,9},{73,72},{72,73},{17,16},{1... | collective-permute-start | bytes 50331656 | tf_op jit(solution)/shard_map/ppermute | solution.py:47
  1.5 15.9 %copy-start.5 = (bf16[2048,128]{1,0:T(8,128)(2,1)}, bf16[2048,128]{1,0:T(8,128)(2,1)S(1)}, u32[]{:S(2)}) copy-start(bf16[2048,128]{1,0:T(8,128)(2,1)S(1)} %constant_dynamic-slice_fusion.1.refs_3_) | copy-start | bytes 1572868
  1.5 11.0 %collective-permute-start.2 = (bf16[2048,128]{1,0:T(8,128)(2,1)S(1)}, bf16[2048,128]{1,0:T(8,128)(2,1)S(1)}, u32[]{:S(2)}, u32[]{:S(2)}) collective-permute-start(bf16[2048,128]{1,0:T(8,128)(2,1)S(1)} %constant_dynamic-slice_fusion.1.refs_3_), channel_id=1, source_target_pairs={{64,0},{73,1},{8,64},{1,65},{72,8},{65,9},{0,72},{9,73},{80,16},{8... | collective-permute-start | bytes 1572872 | tf_op jit(solution)/shard_map/ppermute | solution.py:47
  3.8 9.4 %collective-permute-start.1 = (bf16[2048,128]{1,0:T(8,128)(2,1)S(1)}, bf16[2048,128]{1,0:T(8,128)(2,1)}, u32[]{:S(2)}, u32[]{:S(2)}) collective-permute-start(bf16[2048,128]{1,0:T(8,128)(2,1)S(1)} %constant_dynamic-slice_fusion.1.refs_3_), channel_id=1, source_target_pairs={{16,0},{49,1},{80,64},{113,65},{24,8},{57,9},{88,72},{121,73},{32,... | collective-permute-start | bytes 1572872 | tf_op jit(solution)/shard_map/ppermute | solution.py:47
  12.5 4.9 %copy-start.6 = (bf16[2048,128]{1,0:T(8,128)(2,1)}, bf16[2048,128]{1,0:T(8,128)(2,1)S(1)}, u32[]{:S(2)}) copy-start(bf16[2048,128]{1,0:T(8,128)(2,1)S(1)} %collective-permute-done.2.refs_3_) | copy-start | bytes 1572868
  13.2 9.6 %collective-permute-start.5 = (bf16[2048,128]{1,0:T(8,128)(2,1)}, bf16[2048,128]{1,0:T(8,128)(2,1)}, u32[]{:S(2)}, u32[]{:S(2)}) collective-permute-start(bf16[2048,128]{1,0:T(8,128)(2,1)} %collective-permute-done.1.refs_4_), channel_id=1, source_target_pairs={{2,0},{7,1},{66,64},{71,65},{10,8},{15,9},{74,72},{79,73},{18,16},... | collective-permute-start | bytes 1572872 | tf_op jit(solution)/shard_map/ppermute | solution.py:47
  15.4 9.6 %collective-permute-start.4 = (bf16[2048,128]{1,0:T(8,128)(2,1)}, bf16[2048,128]{1,0:T(8,128)(2,1)}, u32[]{:S(2)}, u32[]{:S(2)}) collective-permute-start(bf16[2048,128]{1,0:T(8,128)(2,1)} %collective-permute-done.1.refs_4_), channel_id=1, source_target_pairs={{64,0},{73,1},{8,64},{1,65},{72,8},{65,9},{0,72},{9,73},{80,16},{8... | collective-permute-start | bytes 1572872 | tf_op jit(solution)/shard_map/ppermute | solution.py:47
  16.8 10.1 %collective-permute-start.3 = (bf16[2048,128]{1,0:T(8,128)(2,1)}, bf16[2048,128]{1,0:T(8,128)(2,1)}, u32[]{:S(2)}, u32[]{:S(2)}) collective-permute-start(bf16[2048,128]{1,0:T(8,128)(2,1)} %collective-permute-done.1.refs_4_), channel_id=1, source_target_pairs={{16,0},{49,1},{80,64},{113,65},{24,8},{57,9},{88,72},{121,73},{32,... | collective-permute-start | bytes 1572872 | tf_op jit(solution)/shard_map/ppermute | solution.py:47
  26.9 26.2 %collective-permute-start.9 = (bf16[2048,512]{1,0:T(8,128)(2,1)S(1)}, bf16[2048,512]{1,0:T(8,128)(2,1)}, u32[]{:S(2)}, u32[]{:S(2)}) collective-permute-start(bf16[2048,512]{1,0:T(8,128)(2,1)S(1)} %constant_dynamic-slice_fusion.refs_0_), channel_id=1, source_target_pairs={{16,0},{49,1},{80,64},{113,65},{24,8},{57,9},{88,72},{121,73},{32,... | collective-permute-start | bytes 6291464 | tf_op jit(solution)/shard_map/ppermute | solution.py:47
  26.9 9.5 %collective-permute-start.6 = (bf16[2048,128]{1,0:T(8,128)(2,1)}, bf16[2048,128]{1,0:T(8,128)(2,1)S(1)}, u32[]{:S(2)}, u32[]{:S(2)}) collective-permute-start(bf16[2048,128]{1,0:T(8,128)(2,1)} %collective-permute-done.3.refs_5_), channel_id=1, source_target_pairs={{64,0},{73,1},{8,64},{1,65},{72,8},{65,9},{0,72},{9,73},{80,16},{8... | collective-permute-start | bytes 1572872 | tf_op jit(solution)/shard_map/ppermute | solution.py:47
  28.3 9.5 %collective-permute-start.7 = (bf16[2048,128]{1,0:T(8,128)(2,1)}, bf16[2048,128]{1,0:T(8,128)(2,1)S(1)}, u32[]{:S(2)}, u32[]{:S(2)}) collective-permute-start(bf16[2048,128]{1,0:T(8,128)(2,1)} %collective-permute-done.4.refs_4_), channel_id=1, source_target_pairs={{2,0},{7,1},{66,64},{71,65},{10,8},{15,9},{74,72},{79,73},{18,16},... | collective-permute-start | bytes 1572872 | tf_op jit(solution)/shard_map/ppermute | solution.py:47
  36.4 1.3 copy-start.7
  37.7 0.8 copy-start.8
  38.5 28.9 %collective-permute-start.13 = (bf16[2048,512]{1,0:T(8,128)(2,1)S(1)}, bf16[2048,512]{1,0:T(8,128)(2,1)}, u32[]{:S(2)}, u32[]{:S(2)}) collective-permute-start(bf16[2048,512]{1,0:T(8,128)(2,1)S(1)} %constant_dynamic-slice_fusion.refs_0_), channel_id=1, source_target_pairs={{64,0},{73,1},{8,64},{1,65},{72,8},{65,9},{0,72},{9,73},{80,16},{8... | collective-permute-start | bytes 6291464 | tf_op jit(solution)/shard_map/ppermute | solution.py:47
  53.1 27.1 %collective-permute-start.12 = (bf16[2048,512]{1,0:T(8,128)(2,1)}, bf16[2048,512]{1,0:T(8,128)(2,1)}, u32[]{:S(2)}, u32[]{:S(2)}) collective-permute-start(bf16[2048,512]{1,0:T(8,128)(2,1)} %collective-permute-done.9.refs_1_), channel_id=1, source_target_pairs={{2,0},{7,1},{66,64},{71,65},{10,8},{15,9},{74,72},{79,73},{18,16},... | collective-permute-start | bytes 6291464 | tf_op jit(solution)/shard_map/ppermute | solution.py:47
  53.1 36.9 %collective-permute-start.11 = (bf16[2048,512]{1,0:T(8,128)(2,1)}, bf16[2048,512]{1,0:T(8,128)(2,1)}, u32[]{:S(2)}, u32[]{:S(2)}) collective-permute-start(bf16[2048,512]{1,0:T(8,128)(2,1)} %collective-permute-done.9.refs_1_), channel_id=1, source_target_pairs={{64,0},{73,1},{8,64},{1,65},{72,8},{65,9},{0,72},{9,73},{80,16},{8... | collective-permute-start | bytes 6291464 | tf_op jit(solution)/shard_map/ppermute | solution.py:47
  54.5 35.5 %collective-permute-start.10 = (bf16[2048,512]{1,0:T(8,128)(2,1)}, bf16[2048,512]{1,0:T(8,128)(2,1)}, u32[]{:S(2)}, u32[]{:S(2)}) collective-permute-start(bf16[2048,512]{1,0:T(8,128)(2,1)} %collective-permute-done.9.refs_1_), channel_id=1, source_target_pairs={{16,0},{49,1},{80,64},{113,65},{24,8},{57,9},{88,72},{121,73},{32,... | collective-permute-start | bytes 6291464 | tf_op jit(solution)/shard_map/ppermute | solution.py:47
  67.5 25.4 %collective-permute-start.16 = (bf16[1024,128]{1,0:T(8,128)(2,1)S(1)}, bf16[1024,128]{1,0:T(8,128)(2,1)S(1)}, u32[]{:S(2)}, u32[]{:S(2)}) collective-permute-start(bf16[1024,128]{1,0:T(8,128)(2,1)S(1)} %maximum_select_fusion.1), channel_id=1, source_target_pairs={{8,0},{9,1},{72,64},{73,65},{0,8},{1,9},{64,72},{65,73},{24,16},{2... | collective-permute-start | bytes 786440 | tf_op jit(solution)/shard_map/ppermute | solution.py:47
  90.0 38.3 %collective-permute-start.14 = (bf16[2048,512]{1,0:T(8,128)(2,1)}, bf16[2048,512]{1,0:T(8,128)(2,1)S(1)}, u32[]{:S(2)}, u32[]{:S(2)}) collective-permute-start(bf16[2048,512]{1,0:T(8,128)(2,1)} %collective-permute-done.11.refs_2_), channel_id=1, source_target_pairs={{16,0},{49,1},{80,64},{113,65},{24,8},{57,9},{88,72},{121,73},{32,... | collective-permute-start | bytes 6291464 | tf_op jit(solution)/shard_map/ppermute | solution.py:47
  90.6 37.8 %collective-permute-start.15 = (bf16[2048,512]{1,0:T(8,128)(2,1)}, bf16[2048,512]{1,0:T(8,128)(2,1)S(1)}, u32[]{:S(2)}, u32[]{:S(2)}) collective-permute-start(bf16[2048,512]{1,0:T(8,128)(2,1)} %collective-permute-done.12.refs_1_), channel_id=1, source_target_pairs={{64,0},{73,1},{8,64},{1,65},{72,8},{65,9},{0,72},{9,73},{80,16},{8... | collective-permute-start | bytes 6291464 | tf_op jit(solution)/shard_map/ppermute | solution.py:47
  92.9 15.6 %collective-permute-start.18 = (bf16[2048,128]{1,0:T(8,128)(2,1)S(1)}, bf16[2048,128]{1,0:T(8,128)(2,1)S(1)}, u32[]{:S(2)}, u32[]{:S(2)}) collective-permute-start(bf16[2048,128]{1,0:T(8,128)(2,1)S(1)} %pad_maximum_fusion), channel_id=1, source_target_pairs={{6,0},{3,1},{70,64},{67,65},{14,8},{11,9},{78,72},{75,73},{22,16},... | collective-permute-start | bytes 1572872 | tf_op jit(solution)/shard_map/ppermute | solution.py:47
  96.0 12.5 %collective-permute-start.17 = (bf16[2048,128]{1,0:T(8,128)(2,1)S(1)}, bf16[2048,128]{1,0:T(8,128)(2,1)S(1)}, u32[]{:S(2)}, u32[]{:S(2)}) collective-permute-start(bf16[2048,128]{1,0:T(8,128)(2,1)S(1)} %pad_maximum_fusion), channel_id=1, source_target_pairs={{2,0},{7,1},{66,64},{71,65},{10,8},{15,9},{74,72},{79,73},{18,16},... | collective-permute-start | bytes 1572872 | tf_op jit(solution)/shard_map/ppermute | solution.py:47
  108.5 17.9 %copy-start.4 = (s32[1,8,16]{2,1,0:T(8,128)S(1)}, s32[1,8,16]{2,1,0:T(8,128)}, u32[]{:S(2)}) copy-start(s32[1,8,16]{2,1,0:T(8,128)} %param.7) | copy-start | bytes 1540
  108.5 9.3 %collective-permute-start.19 = (bf16[2048,128]{1,0:T(8,128)(2,1)S(1)}, bf16[2048,128]{1,0:T(8,128)(2,1)S(1)}, u32[]{:S(2)}, u32[]{:S(2)}) collective-permute-start(bf16[2048,128]{1,0:T(8,128)(2,1)S(1)} %collective-permute-done.17), channel_id=1, source_target_pairs={{2,0},{7,1},{66,64},{71,65},{10,8},{15,9},{74,72},{79,73},{18,16},... | collective-permute-start | bytes 1572872 | tf_op jit(solution)/shard_map/ppermute | solution.py:47
  108.7 17.5 %collective-permute-start.20 = (bf16[2048,128]{1,0:T(8,128)(2,1)S(1)}, bf16[2048,128]{1,0:T(8,128)(2,1)S(1)}, u32[]{:S(2)}, u32[]{:S(2)}) collective-permute-start(bf16[2048,128]{1,0:T(8,128)(2,1)S(1)} %pad_maximum_fusion), channel_id=1, source_target_pairs={{1,0},{0,1},{65,64},{64,65},{9,8},{8,9},{73,72},{72,73},{17,16},{1... | collective-permute-start | bytes 1572872 | tf_op jit(solution)/shard_map/ppermute | solution.py:47
  117.3 9.0 %collective-permute-start.21 = (bf16[2048,128]{1,0:T(8,128)(2,1)S(1)}, bf16[2048,128]{1,0:T(8,128)(2,1)S(1)}, u32[]{:S(2)}, u32[]{:S(2)}) collective-permute-start(bf16[2048,128]{1,0:T(8,128)(2,1)S(1)} %collective-permute-done.17), channel_id=1, source_target_pairs={{1,0},{0,1},{65,64},{64,65},{9,8},{8,9},{73,72},{72,73},{17,16},{1... | collective-permute-start | bytes 1572872 | tf_op jit(solution)/shard_map/ppermute | solution.py:47
  117.8 9.7 %collective-permute-start.22 = (bf16[2048,128]{1,0:T(8,128)(2,1)S(1)}, bf16[2048,128]{1,0:T(8,128)(2,1)S(1)}, u32[]{:S(2)}, u32[]{:S(2)}) collective-permute-start(bf16[2048,128]{1,0:T(8,128)(2,1)S(1)} %collective-permute-done.19), channel_id=1, source_target_pairs={{1,0},{0,1},{65,64},{64,65},{9,8},{8,9},{73,72},{72,73},{17,16},{1... | collective-permute-start | bytes 1572872 | tf_op jit(solution)/shard_map/ppermute | solution.py:47
  126.1 2.1 %collective-permute-start.23 = (bf16[2048,128]{1,0:T(8,128)(2,1)S(1)}, bf16[2048,128]{1,0:T(8,128)(2,1)S(1)}, u32[]{:S(2)}, u32[]{:S(2)}) collective-permute-start(bf16[2048,128]{1,0:T(8,128)(2,1)S(1)} %collective-permute-done.18), channel_id=1, source_target_pairs={{1,0},{0,1},{65,64},{64,65},{9,8},{8,9},{73,72},{72,73},{17,16},{1... | collective-permute-start | bytes 1572872 | tf_op jit(solution)/shard_map/ppermute | solution.py:47
  126.3 10.7 %collective-permute-start = (s32[8,16]{1,0:T(8,128)S(1)}, s32[8,16]{1,0:T(8,128)S(1)}, u32[]{:S(2)}, u32[]{:S(2)}) collective-permute-start(s32[8,16]{1,0:T(8,128)S(1)} %bitcast.18), channel_id=1, source_target_pairs={{1,0},{0,1},{65,64},{64,65},{9,8},{8,9},{73,72},{72,73},{17,16},{1... | collective-permute-start | bytes 1544 | tf_op jit(solution)/shard_map/ppermute | solution.py:47
  128.3 8.8 %copy-start.2 = (bf16[16384,128]{1,0:T(8,128)(2,1)}, bf16[16384,128]{1,0:T(8,128)(2,1)S(1)}, u32[]{:S(2)}) copy-start(bf16[16384,128]{1,0:T(8,128)(2,1)S(1)} %constant_dynamic-update-slice_fusion.kv) | copy-start | bytes 12582916
  146.5 11.3 %collective-permute-start.24 = (bf16[512,512]{1,0:T(8,128)(2,1)}, bf16[512,512]{1,0:T(8,128)(2,1)}, u32[]{:S(2)}, u32[]{:S(2)}) collective-permute-start(bf16[512,512]{1,0:T(8,128)(2,1)} %shard_map.51), channel_id=1, source_target_pairs={{1,0},{0,1},{65,64},{64,65},{9,8},{8,9},{73,72},{72,73},{17,16},{1... | collective-permute-start | bytes 1572872 | tf_op jit(solution)/shard_map/ppermute | solution.py:47
  146.9 13.4 %copy-start.1 = (bf16[2048,256]{1,0:T(8,128)(2,1)S(1)}, bf16[2048,256]{1,0:T(8,128)(2,1)}, u32[]{:S(2)}) copy-start(bf16[2048,256]{1,0:T(8,128)(2,1)} %param.6) | copy-start | bytes 3145732
  146.9 2.3 %copy-start.3 = (bf16[16384,128]{1,0:T(8,128)(2,1)S(1)}, bf16[16384,128]{1,0:T(8,128)(2,1)}, u32[]{:S(2)}) copy-start(bf16[16384,128]{1,0:T(8,128)(2,1)} %copy-done.2) | copy-start | bytes 12582916

commit v5 on v4

--- a/solution.py
+++ b/solution.py
@@ -232,7 +232,7 @@
     lax.fori_loop(0, nblk, body, 0)
 
 
-def attend(picks, where, raw, cosine, sine, kv):
+def attend(picks, where, raw, cosine, sine, kv, limit):
     rows, width = raw.shape
     heads = width // HD
     nblk = rows // BLK
@@ -249,7 +249,7 @@
             pltpu.VMEM((PICKS * BLK, HD), BF16),
             pltpu.VMEM((heads * BLK, HD), BF16),
         ],
-        compiler_params=pltpu.CompilerParams(vmem_limit_bytes=40 << 20),
+        compiler_params=pltpu.CompilerParams(vmem_limit_bytes=limit << 20),
         cost_estimate=pl.CostEstimate(
             flops=4 * pairs * HD, bytes_accessed=kv.size * 2 + raw.size * 8, transcendentals=pairs
         ),
@@ -338,9 +338,9 @@
     def where(s):
         return jnp.stack([s * blocks_here, x, z_hi, c]).astype(jnp.int32)
 
-    out_sib = attend(sib_picks, where(seq + step), acc[1], cos_sib, sin_sib, kv)
+    out_sib = attend(sib_picks, where(seq + step), acc[1], cos_sib, sin_sib, kv, 40)
     received = get(out_sib, FROM_CORE)
-    out_own = attend(picks[0], where(seq), acc[0], cos_own, sin_own, kv)
+    out_own = attend(picks[0], where(seq), acc[0], cos_own, sin_own, kv, 58)
     out = jnp.where(
         plain,
         jnp.concatenate([received, out_own], 1),

time: 161 us -> 157 us (0.975)
  starting transfers between devices: 38.7 us -> 30.4 us
  waiting for transfers between devices: 35.5 us -> 40.2 us
  local copies, waits for them, and re-layouts: 5.38 us -> 3.12 us
  Pallas kernels: 71.1 us -> 73.2 us
    ppermute x25, starting transfers between devices: 38.7 us -> 30.4 us  [get(): return lax.ppermute(value, AXES, perm)]
    ppermute x25, waiting for transfers between devices: 35.5 us -> 40.2 us  [get(): return lax.ppermute(value, AXES, perm)]
    unnamed x25, local copies, waits for them, and re-layouts: 3.55 us -> 1.29 us
    pallas_call x2, Pallas kernels: 17.9 us -> 20 us  [attend(): pl.pallas_call(functools.partial(attend_kernel, nblk, heads), in_specs=[s...]
  transfers between devices with their start and end apart: 25 -> 25, of which waited for: 13 -> 14; matrix products, arithmetic and copies ran while one was open for 6% -> 6% of each run, Pallas kernels for 39% -> 41%
where the time goes in v5:
time: 157 us
  Pallas kernels  73.2 us (47%)
  waiting for transfers between devices  40.2 us (26%)
  starting transfers between devices  30.4 us (19%)
  other arithmetic  10 us (6%)
  local copies, waits for them, and re-layouts  3.12 us (2%)
    ppermute x25, waiting for transfers between devices, get(): return lax.ppermute(value, AXES, perm)  40.2 us
    pallas_call x3, Pallas kernels, project_query(): pl.pallas_call(functools.partial(query_kernel, n, not acc), grid_spec=plt...  31.7 us
    ppermute x25, starting transfers between devices, get(): return lax.ppermute(value, AXES, perm)  30.4 us
    pallas_call x2, Pallas kernels, project(): pl.pallas_call(functools.partial(project_kernel, n, first, last), grid_sp...  21.5 us
    pallas_call x2, Pallas kernels, attend(): pl.pallas_call(functools.partial(attend_kernel, nblk, heads), in_specs=[s...  20 us
  transfers between devices with their start and end apart: 25, of which 14 were waited for; matrix products, arithmetic and copies ran while one was open for 6% of the time, Pallas kernels for 41%

profile of v5, /device:TPU:1, one launch (start us, length us, event | category | flops | bytes accessed | tf_op | source)
XLA Modules:
  0.0 157.1 jit_solution(675456196808958537)
XLA Ops:
  0.0 1.4 collective-permute-start.8
  1.5 2.3 %collective-permute-start.2 = (bf16[2048,128]{1,0:T(8,128)(2,1)S(1)}, bf16[2048,128]{1,0:T(8,128)(2,1)S(1)}, u32[]{:S(2)}, u32[]{:S(2)}) collective-permute-start(bf16[2048,128]{1,0:T(8,128)(2,1)S(1)} %constant_dynamic-slice_fusion.1.refs_3_), channel_id=1, source_target_pairs={{64,0},{73,1},{8,64},{1,65},{72,8},{65,9},{0,72},{9,73},{80,16},{8... | collective-permute-start | bytes 1572872 | tf_op jit(solution)/shard_map/ppermute | solution.py:47
  3.8 1.3 collective-permute-start.1
  5.1 1.9 %fusion.1 = (f32[512,64]{1,0:T(8,128)S(1)}, f32[512,64]{1,0:T(8,128)S(1)}, f32[512,64]{1,0:T(8,128)S(1)}, f32[512,64]{1,0:T(8,128)S(1)}, f32[512,64]{1,0:T(8,128)S(1)}, /*index=5*/f32[512,64]{1,0:T(8,128)S(1)}) fusion(f32[64]{0:T(128)S(1)} %negate_power_fusion, f32[512]{0:T(512)S(1)} %add_convert_fusion, f32[512]{0:T(512)S(1)} %add_convert_fusion.1), kind=kLoop, calls=%fused_computation.16 | loop fusion | flops 131072 | bytes 790784 | tf_op jit(solution)/shard_map/neg | solution.py:265
  7.0 1.1 broadcast_select_fusion.2
  8.2 1.1 broadcast_select_fusion
  9.3 3.2 %collective-permute-done.2.refs_3_ = bf16[2048,128]{1,0:T(8,128)(2,1)S(1)} collective-permute-done((bf16[2048,128]{1,0:T(8,128)(2,1)S(1)}, bf16[2048,128]{1,0:T(8,128)(2,1)S(1)}, u32[]{:S(2)}, u32[]{:S(2)}) %collective-permute-start.2) | collective-permute-done | bytes 524320 | tf_op jit(solution)/shard_map/ppermute | solution.py:47
  12.5 0.7 collective-permute-done.1.refs_4_
  13.2 2.2 %collective-permute-start.5 = (bf16[2048,128]{1,0:T(8,128)(2,1)}, bf16[2048,128]{1,0:T(8,128)(2,1)}, u32[]{:S(2)}, u32[]{:S(2)}) collective-permute-start(bf16[2048,128]{1,0:T(8,128)(2,1)} %collective-permute-done.1.refs_4_), channel_id=1, source_target_pairs={{2,0},{7,1},{66,64},{71,65},{10,8},{15,9},{74,72},{79,73},{18,16},... | collective-permute-start | bytes 1572872 | tf_op jit(solution)/shard_map/ppermute | solution.py:47
  15.4 1.4 collective-permute-start.4
  16.8 0.6 collective-permute-start.3
  17.4 1.7 %constant_dynamic-slice_fusion.refs_0_ = bf16[2048,512]{1,0:T(8,128)(2,1)S(1)} fusion(bf16[2048,1024]{1,0:T(8,128)(2,1)} %param.5, s32[]{:T(128)S(6)} %select_n.134), kind=kLoop, calls=%fused_computation.35 | loop fusion | bytes 4194308 | tf_op jit(solution)/shard_map/dynamic_slice | solution.py:287
  19.1 3.7 %collective-permute-done.5.refs_6_ = bf16[2048,128]{1,0:T(8,128)(2,1)} collective-permute-done((bf16[2048,128]{1,0:T(8,128)(2,1)}, bf16[2048,128]{1,0:T(8,128)(2,1)}, u32[]{:S(2)}, u32[]{:S(2)}) %collective-permute-start.5) | collective-permute-done | bytes 524320 | tf_op jit(solution)/shard_map/ppermute | solution.py:47
  22.8 2.2 %collective-permute-done.4.refs_4_ = bf16[2048,128]{1,0:T(8,128)(2,1)} collective-permute-done((bf16[2048,128]{1,0:T(8,128)(2,1)}, bf16[2048,128]{1,0:T(8,128)(2,1)}, u32[]{:S(2)}, u32[]{:S(2)}) %collective-permute-start.4) | collective-permute-done | bytes 524320 | tf_op jit(solution)/shard_map/ppermute | solution.py:47
  24.9 2.0 %collective-permute-done.3.refs_5_ = bf16[2048,128]{1,0:T(8,128)(2,1)} collective-permute-done((bf16[2048,128]{1,0:T(8,128)(2,1)}, bf16[2048,128]{1,0:T(8,128)(2,1)}, u32[]{:S(2)}, u32[]{:S(2)}) %collective-permute-start.3) | collective-permute-done | bytes 524320 | tf_op jit(solution)/shard_map/ppermute | solution.py:47
  26.9 1.3 collective-permute-start.6
  28.3 2.6 %collective-permute-start.7 = (bf16[2048,128]{1,0:T(8,128)(2,1)}, bf16[2048,128]{1,0:T(8,128)(2,1)S(1)}, u32[]{:S(2)}, u32[]{:S(2)}) collective-permute-start(bf16[2048,128]{1,0:T(8,128)(2,1)} %collective-permute-done.4.refs_4_), channel_id=1, source_target_pairs={{2,0},{7,1},{66,64},{71,65},{10,8},{15,9},{74,72},{79,73},{18,16},... | collective-permute-start | bytes 1572872 | tf_op jit(solution)/shard_map/ppermute | solution.py:47
  30.9 5.5 %collective-permute-done.6.refs_5_ = bf16[2048,128]{1,0:T(8,128)(2,1)S(1)} collective-permute-done((bf16[2048,128]{1,0:T(8,128)(2,1)}, bf16[2048,128]{1,0:T(8,128)(2,1)S(1)}, u32[]{:S(2)}, u32[]{:S(2)}) %collective-permute-start.6) | collective-permute-done | bytes 524320 | tf_op jit(solution)/shard_map/ppermute | solution.py:47
  36.4 1.3 collective-permute-done.7.refs_6_
  37.7 0.8 copy-done.7
  38.5 0.3 collective-permute-start.13
  38.8 0.7 pad_add_fusion.1.refs_0_
  39.5 10.5 %shard_map.46 = (f32[512,128]{1,0:T(8,128)}, f32[512,128]{1,0:T(8,128)}) custom-call(s32[4]{0:T(128)} %pad_add_fusion.1.refs_0_, bf16[512,16384]{1,0:T(8,128)(2,1)} %bitcast.18, bf16[512,16384]{1,0:T(8,128)(2,1)} %collective-permute-done.8.refs_2_.sib, bf16[2048,128]{1,0:T(8,128)(2,1)} %copy-done.4, bf16[2048,128]{1,0:T(8,128)(2,1)} %collective-permute-done.1.refs_4_, ...), custom_call_target="tpu_custom_call" | custom-call | flops 2147483648 | bytes 19922944 | tf_op jit(solution)/shard_map/pallas_call | solution.py:113
  50.0 3.1 %collective-permute-done.9.refs_1_ = bf16[2048,512]{1,0:T(8,128)(2,1)} collective-permute-done((bf16[2048,512]{1,0:T(8,128)(2,1)S(1)}, bf16[2048,512]{1,0:T(8,128)(2,1)}, u32[]{:S(2)}, u32[]{:S(2)}) %collective-permute-start.9) | collective-permute-done | bytes 2097184 | tf_op jit(solution)/shard_map/ppermute | solution.py:47
  53.1 1.3 collective-permute-start.11
  54.5 0.0 collective-permute-start.10
  54.5 0.1 pad_add_fusion.2.blocks
  54.6 0.1 pad_add_fusion.blocks
  54.6 0.6 pad_add_fusion.3.refs_0_
  55.3 0.1 pad_add_fusion.4.blocks
  55.3 11.0 %shard_map.47 = (bf16[512,128]{1,0:T(8,128)(2,1)}, bf16[512,128]{1,0:T(8,128)(2,1)}) custom-call(s32[4]{0:T(128)} %pad_add_fusion.3.refs_0_, bf16[512,16384]{1,0:T(8,128)(2,1)} %bitcast.19, bf16[512,16384]{1,0:T(8,128)(2,1)} %collective-permute-done.8.refs_2_.sib, bf16[2048,128]{1,0:T(8,128)(2,1)} %copy-done.5, ...), custom_call_target="tpu_custom_call" | custom-call | flops 2147483648 | bytes 19922944 | tf_op jit(solution)/shard_map/pallas_call | solution.py:113
  66.3 1.2 maximum_select_fusion.1
  67.5 2.3 %collective-permute-start.16 = (bf16[1024,128]{1,0:T(8,128)(2,1)S(1)}, bf16[1024,128]{1,0:T(8,128)(2,1)S(1)}, u32[]{:S(2)}, u32[]{:S(2)}) collective-permute-start(bf16[1024,128]{1,0:T(8,128)(2,1)S(1)} %maximum_select_fusion.1), channel_id=1, source_target_pairs={{8,0},{9,1},{72,64},{73,65},{0,8},{1,9},{64,72},{65,73},{24,16},{2... | collective-permute-start | bytes 786440 | tf_op jit(solution)/shard_map/ppermute | solution.py:47
  69.8 10.5 %shard_map.48 = (f32[512,512]{1,0:T(8,128)S(1)}, f32[512,512]{1,0:T(8,128)S(1)}) custom-call(s32[3]{0:T(128)S(1)} %pad_add_fusion.2.blocks, bf16[512,16384]{1,0:T(8,128)(2,1)} %bitcast.20, bf16[512,16384]{1,0:T(8,128)(2,1)} %collective-permute-done.8.refs_2_.sib, bf16[2048,512]{1,0:T(8,128)(2,1)S(1)} %constant_dynamic-slice_fusion.refs_0_, ...), custom_call_target="tpu_custom_call" | custom-call | flops 6442450944 | bytes 23068672 | tf_op jit(solution)/shard_map/pallas_call | solution.py:165
  80.4 9.7 %collective-permute-done.11.refs_2_ = bf16[2048,512]{1,0:T(8,128)(2,1)} collective-permute-done((bf16[2048,512]{1,0:T(8,128)(2,1)}, bf16[2048,512]{1,0:T(8,128)(2,1)}, u32[]{:S(2)}, u32[]{:S(2)}) %collective-permute-start.11) | collective-permute-done | bytes 2097184 | tf_op jit(solution)/shard_map/ppermute | solution.py:47
  90.0 0.6 collective-permute-start.14
  90.6 2.3 %collective-permute-done.16 = bf16[1024,128]{1,0:T(8,128)(2,1)S(1)} collective-permute-done((bf16[1024,128]{1,0:T(8,128)(2,1)S(1)}, bf16[1024,128]{1,0:T(8,128)(2,1)S(1)}, u32[]{:S(2)}, u32[]{:S(2)}) %collective-permute-start.16) | collective-permute-done | bytes 262176 | tf_op jit(solution)/shard_map/ppermute | solution.py:47
  92.9 3.1 %collective-permute-start.18 = (bf16[2048,128]{1,0:T(8,128)(2,1)S(1)}, bf16[2048,128]{1,0:T(8,128)(2,1)S(1)}, u32[]{:S(2)}, u32[]{:S(2)}) collective-permute-start(bf16[2048,128]{1,0:T(8,128)(2,1)S(1)} %pad_maximum_fusion), channel_id=1, source_target_pairs={{6,0},{3,1},{70,64},{67,65},{14,8},{11,9},{78,72},{75,73},{22,16},... | collective-permute-start | bytes 1572872 | tf_op jit(solution)/shard_map/ppermute | solution.py:47
  96.0 12.5 %shard_map.49 = (f32[512,512]{1,0:T(8,128)S(1)}, f32[512,512]{1,0:T(8,128)S(1)}) custom-call(s32[3]{0:T(128)S(1)} %pad_add_fusion.4.blocks, bf16[512,16384]{1,0:T(8,128)(2,1)} %bitcast.21, bf16[512,16384]{1,0:T(8,128)(2,1)} %collective-permute-done.8.refs_2_.sib, bf16[2048,512]{1,0:T(8,128)(2,1)} %collective-permute-done.10.refs_0_, ...), custom_call_target="tpu_custom_call" | custom-call | flops 6442450944 | bytes 23068672 | tf_op jit(solution)/shard_map/pallas_call | solution.py:165
  108.5 0.0 copy-start.8
  108.5 0.7 collective-permute-done.17
  109.2 0.1 add_add_fusion.where
  109.3 4.4 %collective-permute-start.20 = (bf16[2048,128]{1,0:T(8,128)(2,1)S(1)}, bf16[2048,128]{1,0:T(8,128)(2,1)S(1)}, u32[]{:S(2)}, u32[]{:S(2)}) collective-permute-start(bf16[2048,128]{1,0:T(8,128)(2,1)S(1)} %pad_maximum_fusion), channel_id=1, source_target_pairs={{1,0},{0,1},{65,64},{64,65},{9,8},{8,9},{73,72},{72,73},{17,16},{1... | collective-permute-start | bytes 1572872 | tf_op jit(solution)/shard_map/ppermute | solution.py:47
  113.7 0.1 collective-permute-start.21
  113.8 0.1 constant_dynamic-update-slice_fusion.6
  113.9 4.6 %collective-permute-done.19 = bf16[2048,128]{1,0:T(8,128)(2,1)S(1)} collective-permute-done((bf16[2048,128]{1,0:T(8,128)(2,1)S(1)}, bf16[2048,128]{1,0:T(8,128)(2,1)S(1)}, u32[]{:S(2)}, u32[]{:S(2)}) %collective-permute-start.19) | collective-permute-done | bytes 524320 | tf_op jit(solution)/shard_map/ppermute | solution.py:47
  118.4 4.0 %collective-permute-start.22 = (bf16[2048,128]{1,0:T(8,128)(2,1)S(1)}, bf16[2048,128]{1,0:T(8,128)(2,1)S(1)}, u32[]{:S(2)}, u32[]{:S(2)}) collective-permute-start(bf16[2048,128]{1,0:T(8,128)(2,1)S(1)} %collective-permute-done.19), channel_id=1, source_target_pairs={{1,0},{0,1},{65,64},{64,65},{9,8},{8,9},{73,72},{72,73},{17,16},{1... | collective-permute-start | bytes 1572872 | tf_op jit(solution)/shard_map/ppermute | solution.py:47
  122.4 0.1 constant_dynamic-update-slice_fusion.5
  122.5 0.1 constant_dynamic-update-slice_fusion.4
  122.6 0.1 collective-permute-start.23
  122.7 0.1 constant_dynamic-update-slice_fusion.3
  122.8 0.6 collective-permute-start
  123.3 0.1 constant_dynamic-update-slice_fusion.2
  123.4 0.5 collective-permute-done.22
  123.9 0.1 constant_dynamic-update-slice_fusion.1
  124.0 0.7 collective-permute-done.23
  124.7 0.1 constant_dynamic-update-slice_fusion.kv
  124.8 8.7 %shard_map.50 = (f32[512,512]{1,0:T(8,128)S(1)}, f32[512,512]{1,0:T(8,128)S(1)}) custom-call(s32[2]{0:T(128)S(1)} %pad_add_fusion.blocks, bf16[512,16384]{1,0:T(8,128)(2,1)} %bitcast.22, bf16[512,16384]{1,0:T(8,128)(2,1)} %collective-permute-done.8.refs_2_.sib, bf16[2048,512]{1,0:T(8,128)(2,1)S(1)} %collective-permute-done.14.refs_0_, ...), custom_call_target="tpu_custom_call" | custom-call | flops 4294967296 | bytes 16777216 | tf_op jit(solution)/shard_map/pallas_call | solution.py:165
  133.5 0.0 copy-start.3
  133.5 8.6 %shard_map.51 = bf16[512,512]{1,0:T(8,128)(2,1)S(1)} custom-call(s32[8,16]{1,0:T(8,128)S(1)} %collective-permute-done.picks, s32[4]{0:T(128)S(1)} %add_add_fusion.where, f32[512,512]{1,0:T(8,128)S(1)} %get-tuple-element.91.raw, f32[512,128]{1,0:T(8,128)S(1)} %get-tuple-element.92.cosine, f32[512,128]{1,0:T(8,128)S(1)} %get-tuple-element.93.sine, ...), custom_call_target="tpu_custom_call" | custom-call | flops 1073741824 | bytes 6291456 | tf_op jit(solution)/shard_map/pallas_call | solution.py:242
  142.1 0.5 collective-permute-start.24
  142.6 0.6 add_add_fusion.1.where
  143.2 11.4 %shard_map.52 = bf16[512,512]{1,0:T(8,128)(2,1)} custom-call(s32[8,16]{1,0:T(8,128)} %bitcast.25, s32[4]{0:T(128)} %add_add_fusion.1.where, f32[512,512]{1,0:T(8,128)} %copy-done.3, f32[512,128]{1,0:T(8,128)} %get-tuple-element.97.cosine, f32[512,128]{1,0:T(8,128)} %get-tuple-element.98.sine, bf16[16384,128]{1,0:T(8,128)(2,1)} %copy-done.2), custom_call_target="tpu_custom_call" | custom-call | flops 1073741824 | bytes 6291456 | tf_op jit(solution)/shard_map/pallas_call | solution.py:242
  154.6 2.5 %maximum_select_fusion = bf16[1,512,1024]{2,1,0:T(8,128)(2,1)} fusion(bf16[1,512,512]{2,1,0:T(8,128)(2,1)} %bitcast.23, bf16[1,512,512]{2,1,0:T(8,128)(2,1)S(1)} %bitcast.24, pred[]{:T(512)S(6)} %eq.24), kind=kLoop, calls=%fused_computation | loop fusion | flops 4718592 | bytes 2097153 | tf_op jit(solution)/shard_map/jit(_where)/select_n | solution.py:344
  (37 shorter events, 0.2 us)
Async XLA Ops:
  0.0 1.4 copy-start
  0.0 38.5 %collective-permute-start.8 = (bf16[512,16384]{1,0:T(8,128)(2,1)}, bf16[512,16384]{1,0:T(8,128)(2,1)}, u32[]{:S(2)}, u32[]{:S(2)}) collective-permute-start(bf16[512,16384]{1,0:T(8,128)(2,1)} %bitcast.17), channel_id=1, source_target_pairs={{1,0},{0,1},{65,64},{64,65},{9,8},{8,9},{73,72},{72,73},{17,16},{1... | collective-permute-start | bytes 50331656 | tf_op jit(solution)/shard_map/ppermute | solution.py:47
  1.5 17.6 %copy-start.4 = (bf16[2048,128]{1,0:T(8,128)(2,1)}, bf16[2048,128]{1,0:T(8,128)(2,1)S(1)}, u32[]{:S(2)}) copy-start(bf16[2048,128]{1,0:T(8,128)(2,1)S(1)} %constant_dynamic-slice_fusion.1.refs_3_) | copy-start | bytes 1572868
  1.5 11.0 %collective-permute-start.2 = (bf16[2048,128]{1,0:T(8,128)(2,1)S(1)}, bf16[2048,128]{1,0:T(8,128)(2,1)S(1)}, u32[]{:S(2)}, u32[]{:S(2)}) collective-permute-start(bf16[2048,128]{1,0:T(8,128)(2,1)S(1)} %constant_dynamic-slice_fusion.1.refs_3_), channel_id=1, source_target_pairs={{64,0},{73,1},{8,64},{1,65},{72,8},{65,9},{0,72},{9,73},{80,16},{8... | collective-permute-start | bytes 1572872 | tf_op jit(solution)/shard_map/ppermute | solution.py:47
  3.8 9.4 %collective-permute-start.1 = (bf16[2048,128]{1,0:T(8,128)(2,1)S(1)}, bf16[2048,128]{1,0:T(8,128)(2,1)}, u32[]{:S(2)}, u32[]{:S(2)}) collective-permute-start(bf16[2048,128]{1,0:T(8,128)(2,1)S(1)} %constant_dynamic-slice_fusion.1.refs_3_), channel_id=1, source_target_pairs={{16,0},{49,1},{80,64},{113,65},{24,8},{57,9},{88,72},{121,73},{32,... | collective-permute-start | bytes 1572872 | tf_op jit(solution)/shard_map/ppermute | solution.py:47
  12.5 4.9 %copy-start.5 = (bf16[2048,128]{1,0:T(8,128)(2,1)}, bf16[2048,128]{1,0:T(8,128)(2,1)S(1)}, u32[]{:S(2)}) copy-start(bf16[2048,128]{1,0:T(8,128)(2,1)S(1)} %collective-permute-done.2.refs_3_) | copy-start | bytes 1572868
  13.2 9.6 %collective-permute-start.5 = (bf16[2048,128]{1,0:T(8,128)(2,1)}, bf16[2048,128]{1,0:T(8,128)(2,1)}, u32[]{:S(2)}, u32[]{:S(2)}) collective-permute-start(bf16[2048,128]{1,0:T(8,128)(2,1)} %collective-permute-done.1.refs_4_), channel_id=1, source_target_pairs={{2,0},{7,1},{66,64},{71,65},{10,8},{15,9},{74,72},{79,73},{18,16},... | collective-permute-start | bytes 1572872 | tf_op jit(solution)/shard_map/ppermute | solution.py:47
  15.4 9.6 %collective-permute-start.4 = (bf16[2048,128]{1,0:T(8,128)(2,1)}, bf16[2048,128]{1,0:T(8,128)(2,1)}, u32[]{:S(2)}, u32[]{:S(2)}) collective-permute-start(bf16[2048,128]{1,0:T(8,128)(2,1)} %collective-permute-done.1.refs_4_), channel_id=1, source_target_pairs={{64,0},{73,1},{8,64},{1,65},{72,8},{65,9},{0,72},{9,73},{80,16},{8... | collective-permute-start | bytes 1572872 | tf_op jit(solution)/shard_map/ppermute | solution.py:47
  16.8 10.1 %collective-permute-start.3 = (bf16[2048,128]{1,0:T(8,128)(2,1)}, bf16[2048,128]{1,0:T(8,128)(2,1)}, u32[]{:S(2)}, u32[]{:S(2)}) collective-permute-start(bf16[2048,128]{1,0:T(8,128)(2,1)} %collective-permute-done.1.refs_4_), channel_id=1, source_target_pairs={{16,0},{49,1},{80,64},{113,65},{24,8},{57,9},{88,72},{121,73},{32,... | collective-permute-start | bytes 1572872 | tf_op jit(solution)/shard_map/ppermute | solution.py:47
  26.9 26.2 %collective-permute-start.9 = (bf16[2048,512]{1,0:T(8,128)(2,1)S(1)}, bf16[2048,512]{1,0:T(8,128)(2,1)}, u32[]{:S(2)}, u32[]{:S(2)}) collective-permute-start(bf16[2048,512]{1,0:T(8,128)(2,1)S(1)} %constant_dynamic-slice_fusion.refs_0_), channel_id=1, source_target_pairs={{16,0},{49,1},{80,64},{113,65},{24,8},{57,9},{88,72},{121,73},{32,... | collective-permute-start | bytes 6291464 | tf_op jit(solution)/shard_map/ppermute | solution.py:47
  26.9 9.5 %collective-permute-start.6 = (bf16[2048,128]{1,0:T(8,128)(2,1)}, bf16[2048,128]{1,0:T(8,128)(2,1)S(1)}, u32[]{:S(2)}, u32[]{:S(2)}) collective-permute-start(bf16[2048,128]{1,0:T(8,128)(2,1)} %collective-permute-done.3.refs_5_), channel_id=1, source_target_pairs={{64,0},{73,1},{8,64},{1,65},{72,8},{65,9},{0,72},{9,73},{80,16},{8... | collective-permute-start | bytes 1572872 | tf_op jit(solution)/shard_map/ppermute | solution.py:47
  28.3 9.5 %collective-permute-start.7 = (bf16[2048,128]{1,0:T(8,128)(2,1)}, bf16[2048,128]{1,0:T(8,128)(2,1)S(1)}, u32[]{:S(2)}, u32[]{:S(2)}) collective-permute-start(bf16[2048,128]{1,0:T(8,128)(2,1)} %collective-permute-done.4.refs_4_), channel_id=1, source_target_pairs={{2,0},{7,1},{66,64},{71,65},{10,8},{15,9},{74,72},{79,73},{18,16},... | collective-permute-start | bytes 1572872 | tf_op jit(solution)/shard_map/ppermute | solution.py:47
  36.4 13.6 %copy-start.6 = (bf16[2048,128]{1,0:T(8,128)(2,1)}, bf16[2048,128]{1,0:T(8,128)(2,1)S(1)}, u32[]{:S(2)}) copy-start(bf16[2048,128]{1,0:T(8,128)(2,1)S(1)} %collective-permute-done.6.refs_5_) | copy-start | bytes 1572868
  37.7 0.8 copy-start.7
  38.5 29.0 %collective-permute-start.13 = (bf16[2048,512]{1,0:T(8,128)(2,1)S(1)}, bf16[2048,512]{1,0:T(8,128)(2,1)}, u32[]{:S(2)}, u32[]{:S(2)}) collective-permute-start(bf16[2048,512]{1,0:T(8,128)(2,1)S(1)} %constant_dynamic-slice_fusion.refs_0_), channel_id=1, source_target_pairs={{64,0},{73,1},{8,64},{1,65},{72,8},{65,9},{0,72},{9,73},{80,16},{8... | collective-permute-start | bytes 6291464 | tf_op jit(solution)/shard_map/ppermute | solution.py:47
  53.1 27.2 %collective-permute-start.12 = (bf16[2048,512]{1,0:T(8,128)(2,1)}, bf16[2048,512]{1,0:T(8,128)(2,1)}, u32[]{:S(2)}, u32[]{:S(2)}) collective-permute-start(bf16[2048,512]{1,0:T(8,128)(2,1)} %collective-permute-done.9.refs_1_), channel_id=1, source_target_pairs={{2,0},{7,1},{66,64},{71,65},{10,8},{15,9},{74,72},{79,73},{18,16},... | collective-permute-start | bytes 6291464 | tf_op jit(solution)/shard_map/ppermute | solution.py:47
  53.1 36.9 %collective-permute-start.11 = (bf16[2048,512]{1,0:T(8,128)(2,1)}, bf16[2048,512]{1,0:T(8,128)(2,1)}, u32[]{:S(2)}, u32[]{:S(2)}) collective-permute-start(bf16[2048,512]{1,0:T(8,128)(2,1)} %collective-permute-done.9.refs_1_), channel_id=1, source_target_pairs={{64,0},{73,1},{8,64},{1,65},{72,8},{65,9},{0,72},{9,73},{80,16},{8... | collective-permute-start | bytes 6291464 | tf_op jit(solution)/shard_map/ppermute | solution.py:47
  54.5 35.5 %collective-permute-start.10 = (bf16[2048,512]{1,0:T(8,128)(2,1)}, bf16[2048,512]{1,0:T(8,128)(2,1)}, u32[]{:S(2)}, u32[]{:S(2)}) collective-permute-start(bf16[2048,512]{1,0:T(8,128)(2,1)} %collective-permute-done.9.refs_1_), channel_id=1, source_target_pairs={{16,0},{49,1},{80,64},{113,65},{24,8},{57,9},{88,72},{121,73},{32,... | collective-permute-start | bytes 6291464 | tf_op jit(solution)/shard_map/ppermute | solution.py:47
  67.5 25.3 %collective-permute-start.16 = (bf16[1024,128]{1,0:T(8,128)(2,1)S(1)}, bf16[1024,128]{1,0:T(8,128)(2,1)S(1)}, u32[]{:S(2)}, u32[]{:S(2)}) collective-permute-start(bf16[1024,128]{1,0:T(8,128)(2,1)S(1)} %maximum_select_fusion.1), channel_id=1, source_target_pairs={{8,0},{9,1},{72,64},{73,65},{0,8},{1,9},{64,72},{65,73},{24,16},{2... | collective-permute-start | bytes 786440 | tf_op jit(solution)/shard_map/ppermute | solution.py:47
  90.0 34.8 %collective-permute-start.14 = (bf16[2048,512]{1,0:T(8,128)(2,1)}, bf16[2048,512]{1,0:T(8,128)(2,1)S(1)}, u32[]{:S(2)}, u32[]{:S(2)}) collective-permute-start(bf16[2048,512]{1,0:T(8,128)(2,1)} %collective-permute-done.11.refs_2_), channel_id=1, source_target_pairs={{16,0},{49,1},{80,64},{113,65},{24,8},{57,9},{88,72},{121,73},{32,... | collective-permute-start | bytes 6291464 | tf_op jit(solution)/shard_map/ppermute | solution.py:47
  90.6 34.2 %collective-permute-start.15 = (bf16[2048,512]{1,0:T(8,128)(2,1)}, bf16[2048,512]{1,0:T(8,128)(2,1)S(1)}, u32[]{:S(2)}, u32[]{:S(2)}) collective-permute-start(bf16[2048,512]{1,0:T(8,128)(2,1)} %collective-permute-done.12.refs_1_), channel_id=1, source_target_pairs={{64,0},{73,1},{8,64},{1,65},{72,8},{65,9},{0,72},{9,73},{80,16},{8... | collective-permute-start | bytes 6291464 | tf_op jit(solution)/shard_map/ppermute | solution.py:47
  92.9 15.6 %collective-permute-start.18 = (bf16[2048,128]{1,0:T(8,128)(2,1)S(1)}, bf16[2048,128]{1,0:T(8,128)(2,1)S(1)}, u32[]{:S(2)}, u32[]{:S(2)}) collective-permute-start(bf16[2048,128]{1,0:T(8,128)(2,1)S(1)} %pad_maximum_fusion), channel_id=1, source_target_pairs={{6,0},{3,1},{70,64},{67,65},{14,8},{11,9},{78,72},{75,73},{22,16},... | collective-permute-start | bytes 1572872 | tf_op jit(solution)/shard_map/ppermute | solution.py:47
  96.0 13.2 %collective-permute-start.17 = (bf16[2048,128]{1,0:T(8,128)(2,1)S(1)}, bf16[2048,128]{1,0:T(8,128)(2,1)S(1)}, u32[]{:S(2)}, u32[]{:S(2)}) collective-permute-start(bf16[2048,128]{1,0:T(8,128)(2,1)S(1)} %pad_maximum_fusion), channel_id=1, source_target_pairs={{2,0},{7,1},{66,64},{71,65},{10,8},{15,9},{74,72},{79,73},{18,16},... | collective-permute-start | bytes 1572872 | tf_op jit(solution)/shard_map/ppermute | solution.py:47
  108.5 14.3 %copy-start.8 = (s32[1,8,16]{2,1,0:T(8,128)S(1)}, s32[1,8,16]{2,1,0:T(8,128)}, u32[]{:S(2)}) copy-start(s32[1,8,16]{2,1,0:T(8,128)} %param.7) | copy-start | bytes 1540
  109.2 9.2 %collective-permute-start.19 = (bf16[2048,128]{1,0:T(8,128)(2,1)S(1)}, bf16[2048,128]{1,0:T(8,128)(2,1)S(1)}, u32[]{:S(2)}, u32[]{:S(2)}) collective-permute-start(bf16[2048,128]{1,0:T(8,128)(2,1)S(1)} %collective-permute-done.17), channel_id=1, source_target_pairs={{2,0},{7,1},{66,64},{71,65},{10,8},{15,9},{74,72},{79,73},{18,16},... | collective-permute-start | bytes 1572872 | tf_op jit(solution)/shard_map/ppermute | solution.py:47
  109.3 13.3 %collective-permute-start.20 = (bf16[2048,128]{1,0:T(8,128)(2,1)S(1)}, bf16[2048,128]{1,0:T(8,128)(2,1)S(1)}, u32[]{:S(2)}, u32[]{:S(2)}) collective-permute-start(bf16[2048,128]{1,0:T(8,128)(2,1)S(1)} %pad_maximum_fusion), channel_id=1, source_target_pairs={{1,0},{0,1},{65,64},{64,65},{9,8},{8,9},{73,72},{72,73},{17,16},{1... | collective-permute-start | bytes 1572872 | tf_op jit(solution)/shard_map/ppermute | solution.py:47
  113.7 9.0 %collective-permute-start.21 = (bf16[2048,128]{1,0:T(8,128)(2,1)S(1)}, bf16[2048,128]{1,0:T(8,128)(2,1)S(1)}, u32[]{:S(2)}, u32[]{:S(2)}) collective-permute-start(bf16[2048,128]{1,0:T(8,128)(2,1)S(1)} %collective-permute-done.17), channel_id=1, source_target_pairs={{1,0},{0,1},{65,64},{64,65},{9,8},{8,9},{73,72},{72,73},{17,16},{1... | collective-permute-start | bytes 1572872 | tf_op jit(solution)/shard_map/ppermute | solution.py:47
  118.4 5.5 %collective-permute-start.22 = (bf16[2048,128]{1,0:T(8,128)(2,1)S(1)}, bf16[2048,128]{1,0:T(8,128)(2,1)S(1)}, u32[]{:S(2)}, u32[]{:S(2)}) collective-permute-start(bf16[2048,128]{1,0:T(8,128)(2,1)S(1)} %collective-permute-done.19), channel_id=1, source_target_pairs={{1,0},{0,1},{65,64},{64,65},{9,8},{8,9},{73,72},{72,73},{17,16},{1... | collective-permute-start | bytes 1572872 | tf_op jit(solution)/shard_map/ppermute | solution.py:47
  122.6 2.1 %collective-permute-start.23 = (bf16[2048,128]{1,0:T(8,128)(2,1)S(1)}, bf16[2048,128]{1,0:T(8,128)(2,1)S(1)}, u32[]{:S(2)}, u32[]{:S(2)}) collective-permute-start(bf16[2048,128]{1,0:T(8,128)(2,1)S(1)} %collective-permute-done.18), channel_id=1, source_target_pairs={{1,0},{0,1},{65,64},{64,65},{9,8},{8,9},{73,72},{72,73},{17,16},{1... | collective-permute-start | bytes 1572872 | tf_op jit(solution)/shard_map/ppermute | solution.py:47
  122.8 10.8 %collective-permute-start = (s32[8,16]{1,0:T(8,128)S(1)}, s32[8,16]{1,0:T(8,128)S(1)}, u32[]{:S(2)}, u32[]{:S(2)}) collective-permute-start(s32[8,16]{1,0:T(8,128)S(1)} %bitcast.26), channel_id=1, source_target_pairs={{1,0},{0,1},{65,64},{64,65},{9,8},{8,9},{73,72},{72,73},{17,16},{1... | collective-permute-start | bytes 1544 | tf_op jit(solution)/shard_map/ppermute | solution.py:47
  124.8 8.8 %copy-start.2 = (bf16[16384,128]{1,0:T(8,128)(2,1)}, bf16[16384,128]{1,0:T(8,128)(2,1)S(1)}, u32[]{:S(2)}) copy-start(bf16[16384,128]{1,0:T(8,128)(2,1)S(1)} %constant_dynamic-update-slice_fusion.kv) | copy-start | bytes 12582916
  133.5 8.6 %copy-start.3 = (f32[512,512]{1,0:T(8,128)}, f32[512,512]{1,0:T(8,128)S(1)}, u32[]{:S(2)}) copy-start(f32[512,512]{1,0:T(8,128)S(1)} %get-tuple-element.96.raw) | copy-start | bytes 3145732
  142.1 12.5 %collective-permute-start.24 = (bf16[512,512]{1,0:T(8,128)(2,1)S(1)}, bf16[512,512]{1,0:T(8,128)(2,1)S(1)}, u32[]{:S(2)}, u32[]{:S(2)}) collective-permute-start(bf16[512,512]{1,0:T(8,128)(2,1)S(1)} %shard_map.51), channel_id=1, source_target_pairs={{1,0},{0,1},{65,64},{64,65},{9,8},{8,9},{73,72},{72,73},{17,16},{1... | collective-permute-start | bytes 1572872 | tf_op jit(solution)/shard_map/ppermute | solution.py:47
  143.2 14.0 %copy-start.1 = (bf16[2048,256]{1,0:T(8,128)(2,1)S(1)}, bf16[2048,256]{1,0:T(8,128)(2,1)}, u32[]{:S(2)}) copy-start(bf16[2048,256]{1,0:T(8,128)(2,1)} %param.6) | copy-start | bytes 3145732

commit v6 on v5

--- a/solution.py
+++ b/solution.py
@@ -229,7 +229,7 @@
             out[rows, h * HD : (h + 1) * HD] = mixed[h * BLK : (h + 1) * BLK, :]
         return carry
 
-    lax.fori_loop(0, nblk, body, 0)
+    lax.fori_loop(0, nblk, body, 0, unroll=2)
 
 
 def attend(picks, where, raw, cosine, sine, kv, limit):

time: 157 us -> 157 us (level)
  no operation moved by 1% of the time
where the time goes in v6:
time: 157 us
  Pallas kernels  73 us (46%)
  waiting for transfers between devices  40.2 us (26%)
  starting transfers between devices  30.4 us (19%)
  other arithmetic  10 us (6%)
  local copies, waits for them, and re-layouts  3.12 us (2%)
    ppermute x25, waiting for transfers between devices, get(): return lax.ppermute(value, AXES, perm)  40.2 us
    pallas_call x3, Pallas kernels, project_query(): pl.pallas_call(functools.partial(query_kernel, n, not acc), grid_spec=plt...  31.7 us
    ppermute x25, starting transfers between devices, get(): return lax.ppermute(value, AXES, perm)  30.4 us
    pallas_call x2, Pallas kernels, project(): pl.pallas_call(functools.partial(project_kernel, n, first, last), grid_sp...  21.5 us
    pallas_call x2, Pallas kernels, attend(): pl.pallas_call(functools.partial(attend_kernel, nblk, heads), in_specs=[s...  19.8 us
  transfers between devices with their start and end apart: 25, of which 14 were waited for; matrix products, arithmetic and copies ran while one was open for 6% of the time, Pallas kernels for 41%

profile of v6, /device:TPU:1, one launch (start us, length us, event | category | flops | bytes accessed | tf_op | source)
XLA Modules:
  0.0 157.0 jit_solution(4196184833343089798)
XLA Ops:
  0.0 1.4 collective-permute-start.8
  1.5 2.3 %collective-permute-start.2 = (bf16[2048,128]{1,0:T(8,128)(2,1)S(1)}, bf16[2048,128]{1,0:T(8,128)(2,1)S(1)}, u32[]{:S(2)}, u32[]{:S(2)}) collective-permute-start(bf16[2048,128]{1,0:T(8,128)(2,1)S(1)} %constant_dynamic-slice_fusion.1.refs_3_), channel_id=1, source_target_pairs={{64,0},{73,1},{8,64},{1,65},{72,8},{65,9},{0,72},{9,73},{80,16},{8... | collective-permute-start | bytes 1572872 | tf_op jit(solution)/shard_map/ppermute | solution.py:47
  3.8 1.3 collective-permute-start.1
  5.1 1.9 %fusion.1 = (f32[512,64]{1,0:T(8,128)S(1)}, f32[512,64]{1,0:T(8,128)S(1)}, f32[512,64]{1,0:T(8,128)S(1)}, f32[512,64]{1,0:T(8,128)S(1)}, f32[512,64]{1,0:T(8,128)S(1)}, /*index=5*/f32[512,64]{1,0:T(8,128)S(1)}) fusion(f32[64]{0:T(128)S(1)} %negate_power_fusion, f32[512]{0:T(512)S(1)} %add_convert_fusion, f32[512]{0:T(512)S(1)} %add_convert_fusion.1), kind=kLoop, calls=%fused_computation.16 | loop fusion | flops 131072 | bytes 790784 | tf_op jit(solution)/shard_map/neg | solution.py:265
  7.0 1.1 broadcast_select_fusion.2
  8.2 1.1 broadcast_select_fusion
  9.3 3.2 %collective-permute-done.2.refs_3_ = bf16[2048,128]{1,0:T(8,128)(2,1)S(1)} collective-permute-done((bf16[2048,128]{1,0:T(8,128)(2,1)S(1)}, bf16[2048,128]{1,0:T(8,128)(2,1)S(1)}, u32[]{:S(2)}, u32[]{:S(2)}) %collective-permute-start.2) | collective-permute-done | bytes 524320 | tf_op jit(solution)/shard_map/ppermute | solution.py:47
  12.5 0.7 collective-permute-done.1.refs_4_
  13.2 2.2 %collective-permute-start.5 = (bf16[2048,128]{1,0:T(8,128)(2,1)}, bf16[2048,128]{1,0:T(8,128)(2,1)}, u32[]{:S(2)}, u32[]{:S(2)}) collective-permute-start(bf16[2048,128]{1,0:T(8,128)(2,1)} %collective-permute-done.1.refs_4_), channel_id=1, source_target_pairs={{2,0},{7,1},{66,64},{71,65},{10,8},{15,9},{74,72},{79,73},{18,16},... | collective-permute-start | bytes 1572872 | tf_op jit(solution)/shard_map/ppermute | solution.py:47
  15.4 1.4 collective-permute-start.4
  16.8 0.6 collective-permute-start.3
  17.4 1.7 %constant_dynamic-slice_fusion.refs_0_ = bf16[2048,512]{1,0:T(8,128)(2,1)S(1)} fusion(bf16[2048,1024]{1,0:T(8,128)(2,1)} %param.5, s32[]{:T(128)S(6)} %select_n.134), kind=kLoop, calls=%fused_computation.35 | loop fusion | bytes 4194308 | tf_op jit(solution)/shard_map/dynamic_slice | solution.py:287
  19.1 3.7 %collective-permute-done.5.refs_6_ = bf16[2048,128]{1,0:T(8,128)(2,1)} collective-permute-done((bf16[2048,128]{1,0:T(8,128)(2,1)}, bf16[2048,128]{1,0:T(8,128)(2,1)}, u32[]{:S(2)}, u32[]{:S(2)}) %collective-permute-start.5) | collective-permute-done | bytes 524320 | tf_op jit(solution)/shard_map/ppermute | solution.py:47
  22.8 2.2 %collective-permute-done.4.refs_4_ = bf16[2048,128]{1,0:T(8,128)(2,1)} collective-permute-done((bf16[2048,128]{1,0:T(8,128)(2,1)}, bf16[2048,128]{1,0:T(8,128)(2,1)}, u32[]{:S(2)}, u32[]{:S(2)}) %collective-permute-start.4) | collective-permute-done | bytes 524320 | tf_op jit(solution)/shard_map/ppermute | solution.py:47
  24.9 2.0 %collective-permute-done.3.refs_5_ = bf16[2048,128]{1,0:T(8,128)(2,1)} collective-permute-done((bf16[2048,128]{1,0:T(8,128)(2,1)}, bf16[2048,128]{1,0:T(8,128)(2,1)}, u32[]{:S(2)}, u32[]{:S(2)}) %collective-permute-start.3) | collective-permute-done | bytes 524320 | tf_op jit(solution)/shard_map/ppermute | solution.py:47
  26.9 1.3 collective-permute-start.6
  28.3 2.6 %collective-permute-start.7 = (bf16[2048,128]{1,0:T(8,128)(2,1)}, bf16[2048,128]{1,0:T(8,128)(2,1)S(1)}, u32[]{:S(2)}, u32[]{:S(2)}) collective-permute-start(bf16[2048,128]{1,0:T(8,128)(2,1)} %collective-permute-done.4.refs_4_), channel_id=1, source_target_pairs={{2,0},{7,1},{66,64},{71,65},{10,8},{15,9},{74,72},{79,73},{18,16},... | collective-permute-start | bytes 1572872 | tf_op jit(solution)/shard_map/ppermute | solution.py:47
  30.9 5.5 %collective-permute-done.6.refs_5_ = bf16[2048,128]{1,0:T(8,128)(2,1)S(1)} collective-permute-done((bf16[2048,128]{1,0:T(8,128)(2,1)}, bf16[2048,128]{1,0:T(8,128)(2,1)S(1)}, u32[]{:S(2)}, u32[]{:S(2)}) %collective-permute-start.6) | collective-permute-done | bytes 524320 | tf_op jit(solution)/shard_map/ppermute | solution.py:47
  36.4 1.3 collective-permute-done.7.refs_6_
  37.7 0.8 copy-done.7
  38.5 0.3 collective-permute-start.13
  38.8 0.7 pad_add_fusion.1.refs_0_
  39.5 10.5 %shard_map.46 = (f32[512,128]{1,0:T(8,128)}, f32[512,128]{1,0:T(8,128)}) custom-call(s32[4]{0:T(128)} %pad_add_fusion.1.refs_0_, bf16[512,16384]{1,0:T(8,128)(2,1)} %bitcast.18, bf16[512,16384]{1,0:T(8,128)(2,1)} %collective-permute-done.8.refs_2_.sib, bf16[2048,128]{1,0:T(8,128)(2,1)} %copy-done.4, bf16[2048,128]{1,0:T(8,128)(2,1)} %collective-permute-done.1.refs_4_, ...), custom_call_target="tpu_custom_call" | custom-call | flops 2147483648 | bytes 19922944 | tf_op jit(solution)/shard_map/pallas_call | solution.py:113
  50.0 3.1 %collective-permute-done.9.refs_1_ = bf16[2048,512]{1,0:T(8,128)(2,1)} collective-permute-done((bf16[2048,512]{1,0:T(8,128)(2,1)S(1)}, bf16[2048,512]{1,0:T(8,128)(2,1)}, u32[]{:S(2)}, u32[]{:S(2)}) %collective-permute-start.9) | collective-permute-done | bytes 2097184 | tf_op jit(solution)/shard_map/ppermute | solution.py:47
  53.1 1.3 collective-permute-start.11
  54.5 0.0 collective-permute-start.10
  54.5 0.1 pad_add_fusion.2.blocks
  54.6 0.1 pad_add_fusion.blocks
  54.6 0.6 pad_add_fusion.3.refs_0_
  55.3 0.1 pad_add_fusion.4.blocks
  55.3 11.0 %shard_map.47 = (bf16[512,128]{1,0:T(8,128)(2,1)}, bf16[512,128]{1,0:T(8,128)(2,1)}) custom-call(s32[4]{0:T(128)} %pad_add_fusion.3.refs_0_, bf16[512,16384]{1,0:T(8,128)(2,1)} %bitcast.19, bf16[512,16384]{1,0:T(8,128)(2,1)} %collective-permute-done.8.refs_2_.sib, bf16[2048,128]{1,0:T(8,128)(2,1)} %copy-done.5, ...), custom_call_target="tpu_custom_call" | custom-call | flops 2147483648 | bytes 19922944 | tf_op jit(solution)/shard_map/pallas_call | solution.py:113
  66.3 1.2 maximum_select_fusion.1
  67.5 2.3 %collective-permute-start.16 = (bf16[1024,128]{1,0:T(8,128)(2,1)S(1)}, bf16[1024,128]{1,0:T(8,128)(2,1)S(1)}, u32[]{:S(2)}, u32[]{:S(2)}) collective-permute-start(bf16[1024,128]{1,0:T(8,128)(2,1)S(1)} %maximum_select_fusion.1), channel_id=1, source_target_pairs={{8,0},{9,1},{72,64},{73,65},{0,8},{1,9},{64,72},{65,73},{24,16},{2... | collective-permute-start | bytes 786440 | tf_op jit(solution)/shard_map/ppermute | solution.py:47
  69.8 10.5 %shard_map.48 = (f32[512,512]{1,0:T(8,128)S(1)}, f32[512,512]{1,0:T(8,128)S(1)}) custom-call(s32[3]{0:T(128)S(1)} %pad_add_fusion.2.blocks, bf16[512,16384]{1,0:T(8,128)(2,1)} %bitcast.20, bf16[512,16384]{1,0:T(8,128)(2,1)} %collective-permute-done.8.refs_2_.sib, bf16[2048,512]{1,0:T(8,128)(2,1)S(1)} %constant_dynamic-slice_fusion.refs_0_, ...), custom_call_target="tpu_custom_call" | custom-call | flops 6442450944 | bytes 23068672 | tf_op jit(solution)/shard_map/pallas_call | solution.py:165
  80.4 9.7 %collective-permute-done.11.refs_2_ = bf16[2048,512]{1,0:T(8,128)(2,1)} collective-permute-done((bf16[2048,512]{1,0:T(8,128)(2,1)}, bf16[2048,512]{1,0:T(8,128)(2,1)}, u32[]{:S(2)}, u32[]{:S(2)}) %collective-permute-start.11) | collective-permute-done | bytes 2097184 | tf_op jit(solution)/shard_map/ppermute | solution.py:47
  90.0 0.6 collective-permute-start.14
  90.6 2.3 %collective-permute-done.16 = bf16[1024,128]{1,0:T(8,128)(2,1)S(1)} collective-permute-done((bf16[1024,128]{1,0:T(8,128)(2,1)S(1)}, bf16[1024,128]{1,0:T(8,128)(2,1)S(1)}, u32[]{:S(2)}, u32[]{:S(2)}) %collective-permute-start.16) | collective-permute-done | bytes 262176 | tf_op jit(solution)/shard_map/ppermute | solution.py:47
  92.9 3.1 %collective-permute-start.18 = (bf16[2048,128]{1,0:T(8,128)(2,1)S(1)}, bf16[2048,128]{1,0:T(8,128)(2,1)S(1)}, u32[]{:S(2)}, u32[]{:S(2)}) collective-permute-start(bf16[2048,128]{1,0:T(8,128)(2,1)S(1)} %pad_maximum_fusion), channel_id=1, source_target_pairs={{6,0},{3,1},{70,64},{67,65},{14,8},{11,9},{78,72},{75,73},{22,16},... | collective-permute-start | bytes 1572872 | tf_op jit(solution)/shard_map/ppermute | solution.py:47
  96.0 12.5 %shard_map.49 = (f32[512,512]{1,0:T(8,128)S(1)}, f32[512,512]{1,0:T(8,128)S(1)}) custom-call(s32[3]{0:T(128)S(1)} %pad_add_fusion.4.blocks, bf16[512,16384]{1,0:T(8,128)(2,1)} %bitcast.21, bf16[512,16384]{1,0:T(8,128)(2,1)} %collective-permute-done.8.refs_2_.sib, bf16[2048,512]{1,0:T(8,128)(2,1)} %collective-permute-done.10.refs_0_, ...), custom_call_target="tpu_custom_call" | custom-call | flops 6442450944 | bytes 23068672 | tf_op jit(solution)/shard_map/pallas_call | solution.py:165
  108.5 0.0 copy-start.8
  108.5 0.7 collective-permute-done.17
  109.2 0.1 add_add_fusion.where
  109.3 4.4 %collective-permute-start.20 = (bf16[2048,128]{1,0:T(8,128)(2,1)S(1)}, bf16[2048,128]{1,0:T(8,128)(2,1)S(1)}, u32[]{:S(2)}, u32[]{:S(2)}) collective-permute-start(bf16[2048,128]{1,0:T(8,128)(2,1)S(1)} %pad_maximum_fusion), channel_id=1, source_target_pairs={{1,0},{0,1},{65,64},{64,65},{9,8},{8,9},{73,72},{72,73},{17,16},{1... | collective-permute-start | bytes 1572872 | tf_op jit(solution)/shard_map/ppermute | solution.py:47
  113.7 0.1 collective-permute-start.21
  113.8 0.1 constant_dynamic-update-slice_fusion.6
  113.9 4.6 %collective-permute-done.19 = bf16[2048,128]{1,0:T(8,128)(2,1)S(1)} collective-permute-done((bf16[2048,128]{1,0:T(8,128)(2,1)S(1)}, bf16[2048,128]{1,0:T(8,128)(2,1)S(1)}, u32[]{:S(2)}, u32[]{:S(2)}) %collective-permute-start.19) | collective-permute-done | bytes 524320 | tf_op jit(solution)/shard_map/ppermute | solution.py:47
  118.4 4.0 %collective-permute-start.22 = (bf16[2048,128]{1,0:T(8,128)(2,1)S(1)}, bf16[2048,128]{1,0:T(8,128)(2,1)S(1)}, u32[]{:S(2)}, u32[]{:S(2)}) collective-permute-start(bf16[2048,128]{1,0:T(8,128)(2,1)S(1)} %collective-permute-done.19), channel_id=1, source_target_pairs={{1,0},{0,1},{65,64},{64,65},{9,8},{8,9},{73,72},{72,73},{17,16},{1... | collective-permute-start | bytes 1572872 | tf_op jit(solution)/shard_map/ppermute | solution.py:47
  122.4 0.1 constant_dynamic-update-slice_fusion.5
  122.5 0.1 constant_dynamic-update-slice_fusion.4
  122.6 0.1 collective-permute-start.23
  122.7 0.1 constant_dynamic-update-slice_fusion.3
  122.8 0.6 collective-permute-start
  123.3 0.1 constant_dynamic-update-slice_fusion.2
  123.4 0.5 collective-permute-done.22
  123.9 0.1 constant_dynamic-update-slice_fusion.1
  124.0 0.7 collective-permute-done.23
  124.7 0.1 constant_dynamic-update-slice_fusion.kv
  124.8 8.7 %shard_map.50 = (f32[512,512]{1,0:T(8,128)S(1)}, f32[512,512]{1,0:T(8,128)S(1)}) custom-call(s32[2]{0:T(128)S(1)} %pad_add_fusion.blocks, bf16[512,16384]{1,0:T(8,128)(2,1)} %bitcast.22, bf16[512,16384]{1,0:T(8,128)(2,1)} %collective-permute-done.8.refs_2_.sib, bf16[2048,512]{1,0:T(8,128)(2,1)S(1)} %collective-permute-done.14.refs_0_, ...), custom_call_target="tpu_custom_call" | custom-call | flops 4294967296 | bytes 16777216 | tf_op jit(solution)/shard_map/pallas_call | solution.py:165
  133.5 0.0 copy-start.3
  133.5 8.5 %shard_map.51 = bf16[512,512]{1,0:T(8,128)(2,1)S(1)} custom-call(s32[8,16]{1,0:T(8,128)S(1)} %collective-permute-done.picks, s32[4]{0:T(128)S(1)} %add_add_fusion.where, f32[512,512]{1,0:T(8,128)S(1)} %get-tuple-element.91.raw, f32[512,128]{1,0:T(8,128)S(1)} %get-tuple-element.92.cosine, f32[512,128]{1,0:T(8,128)S(1)} %get-tuple-element.93.sine, ...), custom_call_target="tpu_custom_call" | custom-call | flops 1073741824 | bytes 6291456 | tf_op jit(solution)/shard_map/pallas_call | solution.py:242
  142.1 0.5 collective-permute-start.24
  142.5 0.6 add_add_fusion.1.where
  143.1 11.3 %shard_map.52 = bf16[512,512]{1,0:T(8,128)(2,1)} custom-call(s32[8,16]{1,0:T(8,128)} %bitcast.25, s32[4]{0:T(128)} %add_add_fusion.1.where, f32[512,512]{1,0:T(8,128)} %copy-done.3, f32[512,128]{1,0:T(8,128)} %get-tuple-element.97.cosine, f32[512,128]{1,0:T(8,128)} %get-tuple-element.98.sine, bf16[16384,128]{1,0:T(8,128)(2,1)} %copy-done.2), custom_call_target="tpu_custom_call" | custom-call | flops 1073741824 | bytes 6291456 | tf_op jit(solution)/shard_map/pallas_call | solution.py:242
  154.5 2.5 %maximum_select_fusion = bf16[1,512,1024]{2,1,0:T(8,128)(2,1)} fusion(bf16[1,512,512]{2,1,0:T(8,128)(2,1)} %bitcast.23, bf16[1,512,512]{2,1,0:T(8,128)(2,1)S(1)} %bitcast.24, pred[]{:T(512)S(6)} %eq.24), kind=kLoop, calls=%fused_computation | loop fusion | flops 4718592 | bytes 2097153 | tf_op jit(solution)/shard_map/jit(_where)/select_n | solution.py:344
  (37 shorter events, 0.2 us)
Async XLA Ops:
  0.0 1.4 copy-start
  0.0 38.5 %collective-permute-start.8 = (bf16[512,16384]{1,0:T(8,128)(2,1)}, bf16[512,16384]{1,0:T(8,128)(2,1)}, u32[]{:S(2)}, u32[]{:S(2)}) collective-permute-start(bf16[512,16384]{1,0:T(8,128)(2,1)} %bitcast.17), channel_id=1, source_target_pairs={{1,0},{0,1},{65,64},{64,65},{9,8},{8,9},{73,72},{72,73},{17,16},{1... | collective-permute-start | bytes 50331656 | tf_op jit(solution)/shard_map/ppermute | solution.py:47
  1.5 17.6 %copy-start.4 = (bf16[2048,128]{1,0:T(8,128)(2,1)}, bf16[2048,128]{1,0:T(8,128)(2,1)S(1)}, u32[]{:S(2)}) copy-start(bf16[2048,128]{1,0:T(8,128)(2,1)S(1)} %constant_dynamic-slice_fusion.1.refs_3_) | copy-start | bytes 1572868
  1.5 11.0 %collective-permute-start.2 = (bf16[2048,128]{1,0:T(8,128)(2,1)S(1)}, bf16[2048,128]{1,0:T(8,128)(2,1)S(1)}, u32[]{:S(2)}, u32[]{:S(2)}) collective-permute-start(bf16[2048,128]{1,0:T(8,128)(2,1)S(1)} %constant_dynamic-slice_fusion.1.refs_3_), channel_id=1, source_target_pairs={{64,0},{73,1},{8,64},{1,65},{72,8},{65,9},{0,72},{9,73},{80,16},{8... | collective-permute-start | bytes 1572872 | tf_op jit(solution)/shard_map/ppermute | solution.py:47
  3.8 9.4 %collective-permute-start.1 = (bf16[2048,128]{1,0:T(8,128)(2,1)S(1)}, bf16[2048,128]{1,0:T(8,128)(2,1)}, u32[]{:S(2)}, u32[]{:S(2)}) collective-permute-start(bf16[2048,128]{1,0:T(8,128)(2,1)S(1)} %constant_dynamic-slice_fusion.1.refs_3_), channel_id=1, source_target_pairs={{16,0},{49,1},{80,64},{113,65},{24,8},{57,9},{88,72},{121,73},{32,... | collective-permute-start | bytes 1572872 | tf_op jit(solution)/shard_map/ppermute | solution.py:47
  12.5 4.9 %copy-start.5 = (bf16[2048,128]{1,0:T(8,128)(2,1)}, bf16[2048,128]{1,0:T(8,128)(2,1)S(1)}, u32[]{:S(2)}) copy-start(bf16[2048,128]{1,0:T(8,128)(2,1)S(1)} %collective-permute-done.2.refs_3_) | copy-start | bytes 1572868
  13.2 9.6 %collective-permute-start.5 = (bf16[2048,128]{1,0:T(8,128)(2,1)}, bf16[2048,128]{1,0:T(8,128)(2,1)}, u32[]{:S(2)}, u32[]{:S(2)}) collective-permute-start(bf16[2048,128]{1,0:T(8,128)(2,1)} %collective-permute-done.1.refs_4_), channel_id=1, source_target_pairs={{2,0},{7,1},{66,64},{71,65},{10,8},{15,9},{74,72},{79,73},{18,16},... | collective-permute-start | bytes 1572872 | tf_op jit(solution)/shard_map/ppermute | solution.py:47
  15.4 9.6 %collective-permute-start.4 = (bf16[2048,128]{1,0:T(8,128)(2,1)}, bf16[2048,128]{1,0:T(8,128)(2,1)}, u32[]{:S(2)}, u32[]{:S(2)}) collective-permute-start(bf16[2048,128]{1,0:T(8,128)(2,1)} %collective-permute-done.1.refs_4_), channel_id=1, source_target_pairs={{64,0},{73,1},{8,64},{1,65},{72,8},{65,9},{0,72},{9,73},{80,16},{8... | collective-permute-start | bytes 1572872 | tf_op jit(solution)/shard_map/ppermute | solution.py:47
  16.8 10.1 %collective-permute-start.3 = (bf16[2048,128]{1,0:T(8,128)(2,1)}, bf16[2048,128]{1,0:T(8,128)(2,1)}, u32[]{:S(2)}, u32[]{:S(2)}) collective-permute-start(bf16[2048,128]{1,0:T(8,128)(2,1)} %collective-permute-done.1.refs_4_), channel_id=1, source_target_pairs={{16,0},{49,1},{80,64},{113,65},{24,8},{57,9},{88,72},{121,73},{32,... | collective-permute-start | bytes 1572872 | tf_op jit(solution)/shard_map/ppermute | solution.py:47
  26.9 26.2 %collective-permute-start.9 = (bf16[2048,512]{1,0:T(8,128)(2,1)S(1)}, bf16[2048,512]{1,0:T(8,128)(2,1)}, u32[]{:S(2)}, u32[]{:S(2)}) collective-permute-start(bf16[2048,512]{1,0:T(8,128)(2,1)S(1)} %constant_dynamic-slice_fusion.refs_0_), channel_id=1, source_target_pairs={{16,0},{49,1},{80,64},{113,65},{24,8},{57,9},{88,72},{121,73},{32,... | collective-permute-start | bytes 6291464 | tf_op jit(solution)/shard_map/ppermute | solution.py:47
  26.9 9.5 %collective-permute-start.6 = (bf16[2048,128]{1,0:T(8,128)(2,1)}, bf16[2048,128]{1,0:T(8,128)(2,1)S(1)}, u32[]{:S(2)}, u32[]{:S(2)}) collective-permute-start(bf16[2048,128]{1,0:T(8,128)(2,1)} %collective-permute-done.3.refs_5_), channel_id=1, source_target_pairs={{64,0},{73,1},{8,64},{1,65},{72,8},{65,9},{0,72},{9,73},{80,16},{8... | collective-permute-start | bytes 1572872 | tf_op jit(solution)/shard_map/ppermute | solution.py:47
  28.3 9.5 %collective-permute-start.7 = (bf16[2048,128]{1,0:T(8,128)(2,1)}, bf16[2048,128]{1,0:T(8,128)(2,1)S(1)}, u32[]{:S(2)}, u32[]{:S(2)}) collective-permute-start(bf16[2048,128]{1,0:T(8,128)(2,1)} %collective-permute-done.4.refs_4_), channel_id=1, source_target_pairs={{2,0},{7,1},{66,64},{71,65},{10,8},{15,9},{74,72},{79,73},{18,16},... | collective-permute-start | bytes 1572872 | tf_op jit(solution)/shard_map/ppermute | solution.py:47
  36.4 13.6 %copy-start.6 = (bf16[2048,128]{1,0:T(8,128)(2,1)}, bf16[2048,128]{1,0:T(8,128)(2,1)S(1)}, u32[]{:S(2)}) copy-start(bf16[2048,128]{1,0:T(8,128)(2,1)S(1)} %collective-permute-done.6.refs_5_) | copy-start | bytes 1572868
  37.7 0.8 copy-start.7
  38.5 29.0 %collective-permute-start.13 = (bf16[2048,512]{1,0:T(8,128)(2,1)S(1)}, bf16[2048,512]{1,0:T(8,128)(2,1)}, u32[]{:S(2)}, u32[]{:S(2)}) collective-permute-start(bf16[2048,512]{1,0:T(8,128)(2,1)S(1)} %constant_dynamic-slice_fusion.refs_0_), channel_id=1, source_target_pairs={{64,0},{73,1},{8,64},{1,65},{72,8},{65,9},{0,72},{9,73},{80,16},{8... | collective-permute-start | bytes 6291464 | tf_op jit(solution)/shard_map/ppermute | solution.py:47
  53.1 27.2 %collective-permute-start.12 = (bf16[2048,512]{1,0:T(8,128)(2,1)}, bf16[2048,512]{1,0:T(8,128)(2,1)}, u32[]{:S(2)}, u32[]{:S(2)}) collective-permute-start(bf16[2048,512]{1,0:T(8,128)(2,1)} %collective-permute-done.9.refs_1_), channel_id=1, source_target_pairs={{2,0},{7,1},{66,64},{71,65},{10,8},{15,9},{74,72},{79,73},{18,16},... | collective-permute-start | bytes 6291464 | tf_op jit(solution)/shard_map/ppermute | solution.py:47
  53.1 36.9 %collective-permute-start.11 = (bf16[2048,512]{1,0:T(8,128)(2,1)}, bf16[2048,512]{1,0:T(8,128)(2,1)}, u32[]{:S(2)}, u32[]{:S(2)}) collective-permute-start(bf16[2048,512]{1,0:T(8,128)(2,1)} %collective-permute-done.9.refs_1_), channel_id=1, source_target_pairs={{64,0},{73,1},{8,64},{1,65},{72,8},{65,9},{0,72},{9,73},{80,16},{8... | collective-permute-start | bytes 6291464 | tf_op jit(solution)/shard_map/ppermute | solution.py:47
  54.5 35.5 %collective-permute-start.10 = (bf16[2048,512]{1,0:T(8,128)(2,1)}, bf16[2048,512]{1,0:T(8,128)(2,1)}, u32[]{:S(2)}, u32[]{:S(2)}) collective-permute-start(bf16[2048,512]{1,0:T(8,128)(2,1)} %collective-permute-done.9.refs_1_), channel_id=1, source_target_pairs={{16,0},{49,1},{80,64},{113,65},{24,8},{57,9},{88,72},{121,73},{32,... | collective-permute-start | bytes 6291464 | tf_op jit(solution)/shard_map/ppermute | solution.py:47
  67.5 25.3 %collective-permute-start.16 = (bf16[1024,128]{1,0:T(8,128)(2,1)S(1)}, bf16[1024,128]{1,0:T(8,128)(2,1)S(1)}, u32[]{:S(2)}, u32[]{:S(2)}) collective-permute-start(bf16[1024,128]{1,0:T(8,128)(2,1)S(1)} %maximum_select_fusion.1), channel_id=1, source_target_pairs={{8,0},{9,1},{72,64},{73,65},{0,8},{1,9},{64,72},{65,73},{24,16},{2... | collective-permute-start | bytes 786440 | tf_op jit(solution)/shard_map/ppermute | solution.py:47
  90.0 34.8 %collective-permute-start.14 = (bf16[2048,512]{1,0:T(8,128)(2,1)}, bf16[2048,512]{1,0:T(8,128)(2,1)S(1)}, u32[]{:S(2)}, u32[]{:S(2)}) collective-permute-start(bf16[2048,512]{1,0:T(8,128)(2,1)} %collective-permute-done.11.refs_2_), channel_id=1, source_target_pairs={{16,0},{49,1},{80,64},{113,65},{24,8},{57,9},{88,72},{121,73},{32,... | collective-permute-start | bytes 6291464 | tf_op jit(solution)/shard_map/ppermute | solution.py:47
  90.6 34.2 %collective-permute-start.15 = (bf16[2048,512]{1,0:T(8,128)(2,1)}, bf16[2048,512]{1,0:T(8,128)(2,1)S(1)}, u32[]{:S(2)}, u32[]{:S(2)}) collective-permute-start(bf16[2048,512]{1,0:T(8,128)(2,1)} %collective-permute-done.12.refs_1_), channel_id=1, source_target_pairs={{64,0},{73,1},{8,64},{1,65},{72,8},{65,9},{0,72},{9,73},{80,16},{8... | collective-permute-start | bytes 6291464 | tf_op jit(solution)/shard_map/ppermute | solution.py:47
  92.9 15.6 %collective-permute-start.18 = (bf16[2048,128]{1,0:T(8,128)(2,1)S(1)}, bf16[2048,128]{1,0:T(8,128)(2,1)S(1)}, u32[]{:S(2)}, u32[]{:S(2)}) collective-permute-start(bf16[2048,128]{1,0:T(8,128)(2,1)S(1)} %pad_maximum_fusion), channel_id=1, source_target_pairs={{6,0},{3,1},{70,64},{67,65},{14,8},{11,9},{78,72},{75,73},{22,16},... | collective-permute-start | bytes 1572872 | tf_op jit(solution)/shard_map/ppermute | solution.py:47
  96.0 13.2 %collective-permute-start.17 = (bf16[2048,128]{1,0:T(8,128)(2,1)S(1)}, bf16[2048,128]{1,0:T(8,128)(2,1)S(1)}, u32[]{:S(2)}, u32[]{:S(2)}) collective-permute-start(bf16[2048,128]{1,0:T(8,128)(2,1)S(1)} %pad_maximum_fusion), channel_id=1, source_target_pairs={{2,0},{7,1},{66,64},{71,65},{10,8},{15,9},{74,72},{79,73},{18,16},... | collective-permute-start | bytes 1572872 | tf_op jit(solution)/shard_map/ppermute | solution.py:47
  108.5 14.3 %copy-start.8 = (s32[1,8,16]{2,1,0:T(8,128)S(1)}, s32[1,8,16]{2,1,0:T(8,128)}, u32[]{:S(2)}) copy-start(s32[1,8,16]{2,1,0:T(8,128)} %param.7) | copy-start | bytes 1540
  109.2 9.2 %collective-permute-start.19 = (bf16[2048,128]{1,0:T(8,128)(2,1)S(1)}, bf16[2048,128]{1,0:T(8,128)(2,1)S(1)}, u32[]{:S(2)}, u32[]{:S(2)}) collective-permute-start(bf16[2048,128]{1,0:T(8,128)(2,1)S(1)} %collective-permute-done.17), channel_id=1, source_target_pairs={{2,0},{7,1},{66,64},{71,65},{10,8},{15,9},{74,72},{79,73},{18,16},... | collective-permute-start | bytes 1572872 | tf_op jit(solution)/shard_map/ppermute | solution.py:47
  109.3 13.3 %collective-permute-start.20 = (bf16[2048,128]{1,0:T(8,128)(2,1)S(1)}, bf16[2048,128]{1,0:T(8,128)(2,1)S(1)}, u32[]{:S(2)}, u32[]{:S(2)}) collective-permute-start(bf16[2048,128]{1,0:T(8,128)(2,1)S(1)} %pad_maximum_fusion), channel_id=1, source_target_pairs={{1,0},{0,1},{65,64},{64,65},{9,8},{8,9},{73,72},{72,73},{17,16},{1... | collective-permute-start | bytes 1572872 | tf_op jit(solution)/shard_map/ppermute | solution.py:47
  113.7 9.0 %collective-permute-start.21 = (bf16[2048,128]{1,0:T(8,128)(2,1)S(1)}, bf16[2048,128]{1,0:T(8,128)(2,1)S(1)}, u32[]{:S(2)}, u32[]{:S(2)}) collective-permute-start(bf16[2048,128]{1,0:T(8,128)(2,1)S(1)} %collective-permute-done.17), channel_id=1, source_target_pairs={{1,0},{0,1},{65,64},{64,65},{9,8},{8,9},{73,72},{72,73},{17,16},{1... | collective-permute-start | bytes 1572872 | tf_op jit(solution)/shard_map/ppermute | solution.py:47
  118.4 5.5 %collective-permute-start.22 = (bf16[2048,128]{1,0:T(8,128)(2,1)S(1)}, bf16[2048,128]{1,0:T(8,128)(2,1)S(1)}, u32[]{:S(2)}, u32[]{:S(2)}) collective-permute-start(bf16[2048,128]{1,0:T(8,128)(2,1)S(1)} %collective-permute-done.19), channel_id=1, source_target_pairs={{1,0},{0,1},{65,64},{64,65},{9,8},{8,9},{73,72},{72,73},{17,16},{1... | collective-permute-start | bytes 1572872 | tf_op jit(solution)/shard_map/ppermute | solution.py:47
  122.6 2.1 %collective-permute-start.23 = (bf16[2048,128]{1,0:T(8,128)(2,1)S(1)}, bf16[2048,128]{1,0:T(8,128)(2,1)S(1)}, u32[]{:S(2)}, u32[]{:S(2)}) collective-permute-start(bf16[2048,128]{1,0:T(8,128)(2,1)S(1)} %collective-permute-done.18), channel_id=1, source_target_pairs={{1,0},{0,1},{65,64},{64,65},{9,8},{8,9},{73,72},{72,73},{17,16},{1... | collective-permute-start | bytes 1572872 | tf_op jit(solution)/shard_map/ppermute | solution.py:47
  122.8 10.8 %collective-permute-start = (s32[8,16]{1,0:T(8,128)S(1)}, s32[8,16]{1,0:T(8,128)S(1)}, u32[]{:S(2)}, u32[]{:S(2)}) collective-permute-start(s32[8,16]{1,0:T(8,128)S(1)} %bitcast.26), channel_id=1, source_target_pairs={{1,0},{0,1},{65,64},{64,65},{9,8},{8,9},{73,72},{72,73},{17,16},{1... | collective-permute-start | bytes 1544 | tf_op jit(solution)/shard_map/ppermute | solution.py:47
  124.8 8.8 %copy-start.2 = (bf16[16384,128]{1,0:T(8,128)(2,1)}, bf16[16384,128]{1,0:T(8,128)(2,1)S(1)}, u32[]{:S(2)}) copy-start(bf16[16384,128]{1,0:T(8,128)(2,1)S(1)} %constant_dynamic-update-slice_fusion.kv) | copy-start | bytes 12582916
  133.5 8.5 %copy-start.3 = (f32[512,512]{1,0:T(8,128)}, f32[512,512]{1,0:T(8,128)S(1)}, u32[]{:S(2)}) copy-start(f32[512,512]{1,0:T(8,128)S(1)} %get-tuple-element.96.raw) | copy-start | bytes 3145732
  142.1 12.4 %collective-permute-start.24 = (bf16[512,512]{1,0:T(8,128)(2,1)S(1)}, bf16[512,512]{1,0:T(8,128)(2,1)S(1)}, u32[]{:S(2)}, u32[]{:S(2)}) collective-permute-start(bf16[512,512]{1,0:T(8,128)(2,1)S(1)} %shard_map.51), channel_id=1, source_target_pairs={{1,0},{0,1},{65,64},{64,65},{9,8},{8,9},{73,72},{72,73},{17,16},{1... | collective-permute-start | bytes 1572872 | tf_op jit(solution)/shard_map/ppermute | solution.py:47
  143.1 13.9 %copy-start.1 = (bf16[2048,256]{1,0:T(8,128)(2,1)S(1)}, bf16[2048,256]{1,0:T(8,128)(2,1)}, u32[]{:S(2)}) copy-start(bf16[2048,256]{1,0:T(8,128)(2,1)} %param.6) | copy-start | bytes 3145732
